TPU v7x, 32 devices: a whole 2x2x4 slice. The times are simulated.
32 devices in a mesh: section: 2 (over x), tensor: 4 (over y, core), dp: 4 (over z).
Axes of the slice: x: 2, y: 2, z: 4, core: 2. Of those that a mesh axis runs over, the one named last changes fastest.
Arguments:
- endpoints: bfloat16 [2, 2, 4, 1024, 1024], P('section', None, 'dp', 'tensor'), may hold values from -6 to 6
- lengths: int32 [2, 4, 6], P(None, 'dp'), may hold values from 0 to 1024, as said below
- timesteps: int32 [2, 4, 6], P(None, 'dp'), may hold values from 0 to 999
- w_qkv: bfloat16 [2, 3, 1024, 1024], P('section', None, 'dp', 'tensor'), may hold values from -0.1875 to 0.1875
- b_qkv: bfloat16 [2, 3, 1024], P('section', None, ('tensor', 'dp')), may hold values from -3 to 3
- w_out: bfloat16 [2, 1024, 1024], P('section', 'tensor', 'dp'), may hold values from -1.5 to 1.5
- b_out: bfloat16 [2, 1024], P('section', 'dp'), may hold values from -3 to 3
- w_up: bfloat16 [2, 1024, 2048], P('section', 'dp', 'tensor'), may hold values from -0.1875 to 0.1875
- b_up: bfloat16 [2, 2048], P('section', ('tensor', 'dp')), may hold values from -3 to 3
- w_down: bfloat16 [2, 2048, 1024], P('section', 'tensor', 'dp'), may hold values from -0.125 to 0.125
- b_down: bfloat16 [2, 1024], P('section', 'dp'), may hold values from -3 to 3
- w_mod: bfloat16 [2, 1024, 6144], P('section', 'dp'), may hold values from -0.375 to 0.375
- b_mod: bfloat16 [2, 6144], P('section', 'dp'), may hold values from -3 to 3
Outputs:
- activations: bfloat16 [2, 2, 4, 1024, 1024], P('section', None, 'dp', 'tensor')
- input_grads: bfloat16 [2, 2, 4, 1024, 1024], P('section', None, 'dp', 'tensor')
- grad_w_qkv: float32 [2, 3, 1024, 1024], P('section', None, 'dp', 'tensor')
- grad_b_qkv: float32 [2, 3, 1024], P('section', None, ('tensor', 'dp'))
- grad_w_out: float32 [2, 1024, 1024], P('section', 'tensor', 'dp')
- grad_b_out: float32 [2, 1024], P('section', 'dp')
- grad_w_up: float32 [2, 1024, 2048], P('section', 'dp', 'tensor')
- grad_b_up: float32 [2, 2048], P('section', ('tensor', 'dp'))
- grad_w_down: float32 [2, 2048, 1024], P('section', 'tensor', 'dp')
- grad_b_down: float32 [2, 1024], P('section', 'dp')
- grad_w_mod: float32 [2, 1024, 6144], P('section', 'dp')
- grad_b_mod: float32 [2, 6144], P('section', 'dp')
Inputs may be any that keep to these rules, and one draw needn't show every extreme that they name: lengths[m, g] lists the frame counts of the 6 utterance slots of buffer (m, g), laid one after another from frame 0 in slot order (a slot may be empty); they sum to at most 1024, the frames after them are padding; in one buffer of each group one utterance begins before frame 256 and ends after frame 1024 - 256, and in some group it fills its whole buffer.
All inputs are finite; a program needn't handle non-finite values.
Results may differ from a plain program's by a relative error of at most 0.035.
Values may be sent and summed in bfloat16 or wider, within the bound.
No kernel may reach another device: no remote copies, remote signals or barrier semaphores. Data moves between devices by JAX's collectives and lax.ppermute only.
A program may use at most 256 MiB of HBM per device.

v0:
```python
import math

import jax
import jax.numpy as jnp
from jax import lax
from jax.sharding import PartitionSpec as P

HEAD_DIM = 64


norm_eps = 1e-06
big_negative = -1e30
highest = lax.Precision.HIGHEST
block_target = 512


def shifted(block, axis, distance):
    devices = range(lax.axis_size(axis))
    route = [(i - distance, i) for i in devices if i - distance in devices]
    return lax.ppermute(block, axis, route)


def layer_norm_mod(residual_stream, scale_part, shift_part):
    centre = residual_stream - jnp.mean(residual_stream, axis=-1, keepdims=True)
    spread = jnp.mean(centre * centre, axis=-1, keepdims=True)
    return centre * lax.rsqrt(spread + norm_eps) * (1.0 + scale_part) + shift_part


def rotary_tables(token_position, table_width, head_width):
    column = jnp.arange(table_width, dtype=jnp.int32) % head_width
    inverse = jnp.exp((column // 2).astype(jnp.float32) * (-2.0 * math.log(10000.0) / head_width))
    angles = token_position.astype(jnp.float32)[:, None] * inverse[None, :]
    return (jnp.cos(angles), jnp.sin(angles))


def rotate(values, cos_table, sin_table):
    row_total, table_width = values.shape
    paired = values.reshape(row_total, table_width // 2, 2)
    turned = jnp.stack([-paired[:, :, 1], paired[:, :, 0]], axis=-1).reshape(row_total, table_width)
    return values * cos_table + turned * sin_table


def segment_layout(lengths_here, total_rows):
    seg_end = jnp.cumsum(lengths_here)
    seg_start = seg_end - lengths_here
    frames = jnp.arange(total_rows, dtype=jnp.int32)
    utterance_segment = jnp.sum((frames[:, None] >= seg_end[None, :]).astype(jnp.int32), axis=1)
    member = (
        utterance_segment[:, None] == jnp.arange(lengths_here.shape[0], dtype=jnp.int32)[None, :]
    )
    seg_begin = jnp.sum(jnp.where(member, seg_start[None, :], 0), axis=1)
    return (utterance_segment, frames - seg_begin)


def time_silu(step_values, code_width):
    half_width = code_width // 2
    frequency = jnp.exp(
        jnp.arange(half_width, dtype=jnp.float32) * (-math.log(10000.0) / (half_width - 1))
    )
    angles = step_values.astype(jnp.float32)[:, None] * frequency[None, :]
    return jax.nn.silu(jnp.concatenate([jnp.sin(angles), jnp.cos(angles)], axis=1))


def gelu_tanh(pre_values):
    return jax.nn.gelu(pre_values, approximate=True)


def place(buffer, update, buffer_index, is_valid):
    return buffer.at[buffer_index].set(jnp.where(is_valid, update, buffer[buffer_index]))


def cross_rows(left_rows, right_rows):
    return lax.dot_general(
        left_rows, right_rows, (((0,), (0,)), ((), ())), preferred_element_type=jnp.float32
    )


def column_sum(rows_low):
    return jnp.sum(rows_low.astype(jnp.float32), axis=0)


def weight_terms(pieces):
    (
        gathered,
        d_queries,
        d_keys,
        d_values,
        mixed_heads,
        wide_dattn,
        gathered2,
        d_pre,
        activated,
        wide_dffn,
        d_attn,
        d_ffn,
    ) = pieces
    return (
        jnp.stack(
            [
                cross_rows(gathered, d_queries),
                cross_rows(gathered, d_keys),
                cross_rows(gathered, d_values),
            ]
        ),
        jnp.stack([column_sum(d_queries), column_sum(d_keys), column_sum(d_values)]),
        cross_rows(mixed_heads, wide_dattn),
        column_sum(d_attn),
        cross_rows(gathered2, d_pre),
        column_sum(d_pre),
        cross_rows(activated, wide_dffn),
        column_sum(d_ffn),
    )


def per_device(
    endpoints,
    lengths,
    timesteps,
    w_qkv,
    b_qkv,
    w_out,
    b_out,
    w_up,
    b_up,
    w_down,
    b_down,
    w_mod,
    b_mod,
):
    section_count = lax.axis_size("section")
    section_index = lax.axis_index("section")
    tensor_count = lax.axis_size("tensor")
    tensor_index = lax.axis_index("tensor")
    micro_count = endpoints.shape[1]
    row_count = endpoints.shape[3]
    model_width = endpoints.shape[4]
    total_rows = row_count * tensor_count
    block_rows = min(block_target, total_rows)
    block_count = total_rows // block_rows
    score_scale = 1.0 / math.sqrt(HEAD_DIM)
    contract_last = (((1,), (1,)), ((), ()))
    codes_local = (
        time_silu(timesteps[:, 0].reshape(-1), model_width)
        .reshape(micro_count, -1, model_width)
        .astype(jnp.bfloat16)
    )
    full_set = (
        lax.all_gather(w_qkv, "dp", axis=2, tiled=True),
        lax.all_gather(b_qkv, "dp", axis=2, tiled=True),
        lax.all_gather(w_out, "dp", axis=2, tiled=True),
        lax.all_gather(b_out, "dp", axis=1, tiled=True),
        lax.all_gather(w_up, "dp", axis=1, tiled=True),
        lax.all_gather(b_up, "dp", axis=1, tiled=True),
        lax.all_gather(w_down, "dp", axis=2, tiled=True),
        lax.all_gather(b_down, "dp", axis=1, tiled=True),
        lax.all_gather(w_mod, "dp", axis=1, tiled=True),
        lax.all_gather(b_mod, "dp", axis=1, tiled=True),
    )
    (
        wqkv_full,
        bqkv_full,
        wout_full,
        bout_full,
        wup_full,
        bup_full,
        wdown_full,
        bdown_full,
        wmod_full,
        bmod_full,
    ) = [shard_full[0] for shard_full in full_set]
    mod_all = jnp.einsum(
        "mud,de->mue", codes_local, wmod_full, preferred_element_type=jnp.float32
    ) + bmod_full.astype(jnp.float32)
    local_width = wqkv_full.shape[2]
    heads_here = local_width // HEAD_DIM
    slot_count = mod_all.shape[1]

    def collect(normed):
        return lax.all_gather(normed, "tensor", axis=0, tiled=True)

    def collect_grad(rows_low):
        return lax.all_gather(rows_low, "tensor", axis=0, tiled=True)

    def spread_sum(left_rows, right_mat):

        def partial_rows(first_row, count_rows):
            return jnp.dot(left_rows, right_mat, preferred_element_type=jnp.float32)

        return lax.psum_scatter(
            partial_rows(jnp.int32(0), row_count * lax.axis_size("tensor")).astype(jnp.bfloat16),
            "tensor",
            scatter_dimension=0,
            tiled=True,
        ).astype(jnp.float32)

    def spread_back(pair_list):

        def partial_rows(first_row, count_rows):
            total_term = jnp.zeros((count_rows, model_width), jnp.float32)
            for left_rows, right_mat in pair_list:
                total_term = total_term + lax.dot_general(
                    left_rows, right_mat, contract_last, preferred_element_type=jnp.float32
                )
            return total_term

        return lax.psum_scatter(
            partial_rows(jnp.int32(0), row_count * lax.axis_size("tensor")).astype(jnp.bfloat16),
            "tensor",
            scatter_dimension=0,
            tiled=True,
        ).astype(jnp.float32)

    def split_blocks(matrix):
        return matrix.reshape(block_count, block_rows, heads_here, HEAD_DIM)

    def attend_back(queries, key_rows, values, utterance_segment, lse_blocks, d_mixed):
        k_heads = key_rows.reshape(total_rows, heads_here, HEAD_DIM)
        v_heads = values.reshape(total_rows, heads_here, HEAD_DIM)

        def one_step(carry_pair, operands):
            dk_acc, dv_acc = carry_pair
            q_block, seg_block, lse_block, g_block = operands
            scores = (
                jnp.einsum("qhd,khd->hqk", q_block, k_heads, preferred_element_type=jnp.float32)
                * score_scale
            )
            allowed = (seg_block[:, None] == utterance_segment[None, :])[None]
            scores = jnp.where(allowed, scores, big_negative)
            attn_prob = jnp.exp(scores - lse_block[:, :, None])
            dv_acc = dv_acc + jnp.einsum(
                "hqk,qhd->khd",
                attn_prob.astype(jnp.bfloat16),
                g_block,
                preferred_element_type=jnp.float32,
            )
            d_prob = jnp.einsum(
                "qhd,khd->hqk", g_block, v_heads, preferred_element_type=jnp.float32
            )
            d_scores = (
                attn_prob * (d_prob - jnp.sum(attn_prob * d_prob, axis=-1, keepdims=True))
            ).astype(jnp.bfloat16)
            dq_block = (
                jnp.einsum("hqk,khd->qhd", d_scores, k_heads, preferred_element_type=jnp.float32)
                * score_scale
            )
            dk_acc = (
                dk_acc
                + jnp.einsum("hqk,qhd->khd", d_scores, q_block, preferred_element_type=jnp.float32)
                * score_scale
            )
            return ((dk_acc, dv_acc), dq_block)

        zero_heads = jnp.zeros((total_rows, heads_here, HEAD_DIM), jnp.float32)
        operands = (
            split_blocks(queries),
            utterance_segment.reshape(block_count, block_rows),
            lse_blocks,
            split_blocks(d_mixed),
        )
        (dk_all, dv_all), dq_blocks = lax.scan(one_step, (zero_heads, zero_heads), operands)
        return (
            dq_blocks.reshape(total_rows, local_width),
            dk_all.reshape(total_rows, local_width),
            dv_all.reshape(total_rows, local_width),
        )

    def backward_micro(saved_state, grad_rows):
        (
            residual_stream,
            residual1,
            gathered,
            queries,
            key_rows,
            values,
            lse_blocks,
            mixed_heads,
            attn_sum,
            gathered2,
            pre_act,
            activated,
            ffn_sum,
            micro_info,
        ) = saved_state
        utterance_segment, cos_table, sin_table, picker, frame_parts, live_rows = micro_info
        shift_a, scale_a, gate_a, shift_b, scale_b, gate_b = frame_parts
        d_gate_b = grad_rows * ffn_sum
        d_ffn = (grad_rows * gate_b).astype(jnp.bfloat16)
        wide_dffn = collect_grad(d_ffn)
        d_activated = lax.dot_general(
            wide_dffn, wdown_full, contract_last, preferred_element_type=jnp.float32
        )
        _, gelu_back = jax.vjp(gelu_tanh, pre_act)
        d_pre = gelu_back(d_activated)[0].astype(jnp.bfloat16)
        d_normed2 = spread_back(((d_pre, wup_full),))
        _, norm_back2 = jax.vjp(layer_norm_mod, residual1, scale_b, shift_b)
        d_res1, d_scale_b, d_shift_b = norm_back2(d_normed2)
        d_res1 = d_res1 + grad_rows
        d_gate_a = d_res1 * attn_sum
        d_attn = (d_res1 * gate_a).astype(jnp.bfloat16)
        wide_dattn = collect_grad(d_attn)
        d_mixed = lax.dot_general(
            wide_dattn, wout_full, contract_last, preferred_element_type=jnp.float32
        ).astype(jnp.bfloat16)
        dq_turned, dk_turned, dv_full = attend_back(
            queries, key_rows, values, utterance_segment, lse_blocks, d_mixed
        )
        _, unrotate = jax.vjp(lambda values_in: rotate(values_in, cos_table, sin_table), dq_turned)
        d_queries = unrotate(dq_turned)[0].astype(jnp.bfloat16)
        d_keys = unrotate(dk_turned)[0].astype(jnp.bfloat16)
        d_values = dv_full.astype(jnp.bfloat16)
        d_normed1 = spread_back(
            ((d_queries, wqkv_full[0]), (d_keys, wqkv_full[1]), (d_values, wqkv_full[2]))
        )
        _, norm_back1 = jax.vjp(layer_norm_mod, residual_stream, scale_a, shift_a)
        d_res, d_scale_a, d_shift_a = norm_back1(d_normed1)
        d_res = d_res + d_res1
        d_frame = jnp.concatenate(
            [d_shift_a, d_scale_a, d_gate_a, d_shift_b, d_scale_b, d_gate_b], axis=1
        )
        d_modulation = lax.dot_general(picker, d_frame, (((0,), (0,)), ((), ())), precision=highest)
        pieces = (
            gathered,
            d_queries,
            d_keys,
            d_values,
            mixed_heads,
            wide_dattn,
            gathered2,
            d_pre,
            activated,
            wide_dffn,
            d_attn,
            d_ffn,
        )
        return (d_res, pieces, d_modulation)

    tick_count = micro_count + section_count - 1
    layer_store = jnp.zeros((micro_count, row_count, model_width), jnp.bfloat16)
    incoming = jnp.zeros((row_count, model_width), jnp.bfloat16)
    saved_store = None
    for tick_index in range(tick_count):
        raw_index = tick_index - section_index
        is_valid = (raw_index >= 0) & (raw_index < micro_count)
        buffer_index = jnp.clip(raw_index, 0, micro_count - 1)
        source = jnp.where(section_index == 0, endpoints[0, buffer_index, 0], incoming)
        micro_utterance_segment, token_position = segment_layout(
            lengths[buffer_index, 0], total_rows
        )
        modulation = mod_all[buffer_index]
        local_seg = lax.dynamic_slice_in_dim(
            micro_utterance_segment, tensor_index * row_count, row_count
        )
        micro_picker = (
            local_seg[:, None] == jnp.arange(slot_count, dtype=jnp.int32)[None, :]
        ).astype(jnp.float32)
        frame_mod = jnp.dot(micro_picker, modulation, precision=highest)
        micro_cos_table, micro_sin_table = rotary_tables(token_position, local_width, HEAD_DIM)
        micro_live_rows = (local_seg < slot_count).astype(jnp.float32)
        forward_micro_info = (
            micro_utterance_segment,
            micro_cos_table,
            micro_sin_table,
            micro_picker,
            tuple(jnp.split(frame_mod, 6, axis=1)),
            micro_live_rows,
        )
        (
            forward_utterance_segment,
            forward_cos_table,
            forward_sin_table,
            forward_picker,
            forward_frame_parts,
            forward_live_rows,
        ) = forward_micro_info
        (
            forward_shift_a,
            forward_scale_a,
            forward_gate_a,
            forward_shift_b,
            forward_scale_b,
            forward_gate_b,
        ) = forward_frame_parts
        forward_residual_stream = source.astype(jnp.float32)
        forward_gathered = collect(
            layer_norm_mod(forward_residual_stream, forward_scale_a, forward_shift_a).astype(
                jnp.bfloat16
            )
        )

        def project(part_index):
            return jnp.dot(
                forward_gathered, wqkv_full[part_index], preferred_element_type=jnp.float32
            ) + bqkv_full[part_index].astype(jnp.float32)

        forward_queries = rotate(project(0), forward_cos_table, forward_sin_table).astype(
            jnp.bfloat16
        )
        forward_key_rows = rotate(project(1), forward_cos_table, forward_sin_table).astype(
            jnp.bfloat16
        )
        forward_values = project(2).astype(jnp.bfloat16)
        attend_utterance_segment = forward_utterance_segment
        attend_k_heads = forward_key_rows.reshape(total_rows, heads_here, HEAD_DIM)
        attend_v_heads = forward_values.reshape(total_rows, heads_here, HEAD_DIM)

        def one_block(operands):
            q_block, seg_block = operands
            scores = (
                jnp.einsum(
                    "qhd,khd->hqk", q_block, attend_k_heads, preferred_element_type=jnp.float32
                )
                * score_scale
            )
            allowed = (seg_block[:, None] == attend_utterance_segment[None, :])[None]
            scores = jnp.where(allowed, scores, big_negative)
            row_max = jnp.max(scores, axis=-1, keepdims=True)
            weight = jnp.exp(scores - row_max)
            weight_sum = jnp.sum(weight, axis=-1, keepdims=True)
            attn_prob = (weight / weight_sum).astype(jnp.bfloat16)
            mixed_block = jnp.einsum(
                "hqk,khd->qhd", attn_prob, attend_v_heads, preferred_element_type=jnp.float32
            )
            return (
                mixed_block.astype(jnp.bfloat16).reshape(block_rows, local_width),
                (row_max + jnp.log(weight_sum))[:, :, 0],
            )

        mixed_blocks, attend_lse_blocks = lax.map(
            one_block,
            (
                split_blocks(forward_queries),
                attend_utterance_segment.reshape(block_count, block_rows),
            ),
        )
        forward_mixed_heads = mixed_blocks.reshape(total_rows, local_width)
        forward_attn_sum = spread_sum(forward_mixed_heads, wout_full) + bout_full.astype(
            jnp.float32
        )
        forward_residual1 = forward_residual_stream + forward_gate_a * forward_attn_sum
        forward_gathered2 = collect(
            layer_norm_mod(forward_residual1, forward_scale_b, forward_shift_b).astype(jnp.bfloat16)
        )
        forward_pre_act = jnp.dot(
            forward_gathered2, wup_full, preferred_element_type=jnp.float32
        ) + bup_full.astype(jnp.float32)
        forward_activated = gelu_tanh(forward_pre_act).astype(jnp.bfloat16)
        forward_ffn_sum = spread_sum(forward_activated, wdown_full) + bdown_full.astype(jnp.float32)
        layer_output = forward_residual1 + forward_gate_b * forward_ffn_sum
        forward_saved_state = (
            forward_residual_stream,
            forward_residual1,
            forward_gathered,
            forward_queries,
            forward_key_rows,
            forward_values,
            attend_lse_blocks,
            forward_mixed_heads,
            forward_attn_sum,
            forward_gathered2,
            forward_pre_act,
            forward_activated,
            forward_ffn_sum,
            forward_micro_info,
        )
        layer_output, saved_state = (layer_output, forward_saved_state)
        sent_rows = layer_output.astype(jnp.bfloat16)
        if saved_store is None:
            saved_store = jax.tree.map(
                lambda leaf_arr: jnp.zeros((micro_count,) + leaf_arr.shape, leaf_arr.dtype),
                saved_state,
            )
        saved_store = jax.tree.map(
            lambda buffer, update: place(buffer, update, buffer_index, is_valid),
            saved_store,
            saved_state,
        )
        layer_store = place(layer_store, sent_rows, buffer_index, is_valid)
        if tick_index < tick_count - 1:
            incoming = shifted(sent_rows, "section", 1)
    grad_store = jnp.zeros((micro_count, row_count, model_width), jnp.bfloat16)
    dmod_store = jnp.zeros(mod_all.shape, jnp.float32)
    incoming = jnp.zeros((row_count, model_width), jnp.bfloat16)
    sums_now = None
    for tick_index in range(tick_count):
        raw_index = tick_index - (section_count - 1 - section_index)
        is_valid = (raw_index >= 0) & (raw_index < micro_count)
        buffer_index = jnp.clip(raw_index, 0, micro_count - 1)
        saved_state = jax.tree.map(lambda stored: stored[buffer_index], saved_store)
        live_rows = saved_state[-1][-1]
        cotangent = endpoints[0, buffer_index, 0].astype(jnp.float32) * live_rows[:, None]
        grad_rows = jnp.where(
            section_index == section_count - 1, cotangent, incoming.astype(jnp.float32)
        )
        d_res, pieces, d_modulation = backward_micro(saved_state, grad_rows)
        sent_rows = d_res.astype(jnp.bfloat16)
        grad_store = place(grad_store, sent_rows, buffer_index, is_valid)
        dmod_store = place(dmod_store, d_modulation, buffer_index, is_valid)
        term_set = jax.tree.map(
            lambda term_arr: jnp.where(is_valid, term_arr, 0.0), weight_terms(pieces)
        )
        sums_now = term_set if sums_now is None else jax.tree.map(jnp.add, sums_now, term_set)
        if tick_index < tick_count - 1:
            incoming = shifted(sent_rows, "section", -1)
    grad_terms = tuple((term_arr[None] for term_arr in sums_now))
    codes_flat = codes_local.reshape(-1, model_width).astype(jnp.float32)
    dmod_flat = dmod_store.reshape(-1, dmod_store.shape[2])
    g_wmod = lax.dot_general(codes_flat, dmod_flat, (((0,), (0,)), ((), ())), precision=highest)
    g_bmod = jnp.sum(dmod_flat, axis=0)
    reduced_all = (
        lax.psum_scatter(
            grad_terms[0].astype(jnp.bfloat16), "dp", scatter_dimension=2, tiled=True
        ).astype(jnp.float32),
        lax.psum_scatter(
            grad_terms[1].astype(jnp.bfloat16), "dp", scatter_dimension=2, tiled=True
        ).astype(jnp.float32),
        lax.psum_scatter(
            grad_terms[2].astype(jnp.bfloat16), "dp", scatter_dimension=2, tiled=True
        ).astype(jnp.float32),
        lax.psum_scatter(
            grad_terms[3].astype(jnp.bfloat16), "dp", scatter_dimension=1, tiled=True
        ).astype(jnp.float32),
        lax.psum_scatter(
            grad_terms[4].astype(jnp.bfloat16), "dp", scatter_dimension=1, tiled=True
        ).astype(jnp.float32),
        lax.psum_scatter(
            grad_terms[5].astype(jnp.bfloat16), "dp", scatter_dimension=1, tiled=True
        ).astype(jnp.float32),
        lax.psum_scatter(
            grad_terms[6].astype(jnp.bfloat16), "dp", scatter_dimension=2, tiled=True
        ).astype(jnp.float32),
        lax.psum_scatter(
            grad_terms[7].astype(jnp.bfloat16), "dp", scatter_dimension=1, tiled=True
        ).astype(jnp.float32),
        lax.psum_scatter(
            g_wmod[None].astype(jnp.bfloat16), "dp", scatter_dimension=1, tiled=True
        ).astype(jnp.float32),
        lax.psum_scatter(
            g_bmod[None].astype(jnp.bfloat16), "dp", scatter_dimension=1, tiled=True
        ).astype(jnp.float32),
    )
    reduced = reduced_all[:8]
    mod_grads = (reduced_all[8], reduced_all[9])
    shared = (
        lax.psum(reduced[3].astype(jnp.bfloat16), "tensor").astype(jnp.float32),
        lax.psum(reduced[7].astype(jnp.bfloat16), "tensor").astype(jnp.float32),
        lax.psum(mod_grads[0].astype(jnp.bfloat16), "tensor").astype(jnp.float32),
        lax.psum(mod_grads[1].astype(jnp.bfloat16), "tensor").astype(jnp.float32),
    )
    return (
        layer_store[None, :, None],
        grad_store[None, :, None],
        reduced[0],
        reduced[1],
        reduced[2],
        shared[0],
        reduced[4],
        reduced[5],
        reduced[6],
        shared[1],
        shared[2],
        shared[3],
    )


def solution(mesh):
    return jax.shard_map(
        per_device,
        mesh=mesh,
        in_specs=(
            P("section", None, "dp", "tensor", None),
            P(None, "dp", None),
            P(None, "dp", None),
            P("section", None, "dp", "tensor"),
            P("section", None, ("tensor", "dp")),
            P("section", "tensor", "dp"),
            P("section", "dp"),
            P("section", "dp", "tensor"),
            P("section", ("tensor", "dp")),
            P("section", "tensor", "dp"),
            P("section", "dp"),
            P("section", "dp", None),
            P("section", "dp"),
        ),
        out_specs=(
            P("section", None, "dp", "tensor", None),
            P("section", None, "dp", "tensor", None),
            P("section", None, "dp", "tensor"),
            P("section", None, ("tensor", "dp")),
            P("section", "tensor", "dp"),
            P("section", "dp"),
            P("section", "dp", "tensor"),
            P("section", ("tensor", "dp")),
            P("section", "tensor", "dp"),
            P("section", "dp"),
            P("section", "dp", None),
            P("section", "dp"),
        ),
        check_vma=False,
    )
```

profile of v0, /device:TPU:0, one launch (start us, length us, event | category | flops | bytes accessed | tf_op | source)
XLA Modules:
  0.0 2204.9 jit_solution(16620102079889722311)
XLA Ops:
  30.4 200.3 %all-gather.17.cloned.1.call-done = bf16[1,1024,6144]{2,1,0:T(8,128)(2,1)} async-done(((bf16[1,256,6144]{2,1,0:T(8,128)(2,1)}), bf16[1,1024,6144]{2,1,0:T(8,128)(2,1)}) %all-gather.17.cloned.1.call-update) | async-done | bytes 12582928 | tf_op jit(solution)/shard_map/all_gather | solution.py:156
  365.5 20.0 reduce-scatter.33.cloned.1.call-done
  415.0 24.2 %all-gather.23.cloned.1.call-done = bf16[1024,1024]{1,0:T(8,128)(2,1)} async-done(((bf16[256,1024]{1,0:T(8,128)(2,1)}), bf16[1024,1024]{1,0:T(8,128)(2,1)}) %all-gather.23.cloned.1.call-update) | async-done | bytes 2097168 | tf_op jit(solution)/shard_map/all_gather | solution.py:179
  445.9 25.2 %all-gather.27.cloned.1.call-done = bf16[1,512,1024]{2,1,0:T(8,128)(2,1)} async-done(((bf16[1,512,256]{2,1,0:T(8,128)(2,1)}), bf16[1,512,1024]{2,1,0:T(8,128)(2,1)}) %all-gather.27.cloned.1.call-update) | async-done | bytes 1048592 | tf_op jit(solution)/shard_map/all_gather | solution.py:154
  632.6 20.1 reduce-scatter.37.cloned.1.call-done
  700.3 29.7 %reduce-scatter.39.cloned.1.call-done = bf16[256,1024]{1,0:T(8,128)(2,1)} async-done(((bf16[1024,1024]{1,0:T(8,128)(2,1)}), bf16[256,1024]{1,0:T(8,128)(2,1)}) %reduce-scatter.39.cloned.1.call-update) | async-done | bytes 524304 | tf_op jit(solution)/shard_map/reduce_scatter | solution.py:189
  851.5 25.8 %reduce-scatter.41.cloned.1.call-done = bf16[256,1024]{1,0:T(8,128)(2,1)} async-done(((bf16[1024,1024]{1,0:T(8,128)(2,1)}), bf16[256,1024]{1,0:T(8,128)(2,1)}) %reduce-scatter.41.cloned.1.call-update) | async-done | bytes 524304 | tf_op jit(solution)/shard_map/reduce_scatter | solution.py:189
  951.1 28.1 %reduce-scatter.45.cloned.1.call-done = bf16[256,1024]{1,0:T(8,128)(2,1)} async-done(((bf16[1024,1024]{1,0:T(8,128)(2,1)}), bf16[256,1024]{1,0:T(8,128)(2,1)}) %reduce-scatter.45.cloned.1.call-update) | async-done | bytes 524304 | tf_op jit(solution)/shard_map/reduce_scatter | solution.py:206
  1043.5 55.5 %while.159 = (s32[]{:T(128)}, f32[1024,4,64]{0,2,1:T(8,128)S(1)}, f32[1024,4,64]{0,2,1:T(8,128)}, f32[2,512,4,64]{1,0,3,2:T(2,128)}, bf16[2,512,4,64]{1,3,2,0:T(...) while((s32[]{:T(128)}, f32[1024,4,64]{0,2,1:T(8,128)S(1)}, ...), condition=%wide.region_56.57_spmd.clone, body=%wide.region_54.56_spmd.clone.sunk | while | flops 1375598592 | bytes 82905312 | solution.py:260
  1125.5 28.6 %reduce-scatter.47.cloned.1.call-done = bf16[256,1024]{1,0:T(8,128)(2,1)} async-done(((bf16[1024,1024]{1,0:T(8,128)(2,1)}), bf16[256,1024]{1,0:T(8,128)(2,1)}) %reduce-scatter.47.cloned.1.call-update) | async-done | bytes 524304 | tf_op jit(solution)/shard_map/reduce_scatter | solution.py:206
  1179.6 21.6 all-gather.41.cloned.1.call-done
  1210.7 31.0 %reduce-scatter.49.cloned.1.call-done = bf16[256,1024]{1,0:T(8,128)(2,1)} async-done(((bf16[1024,1024]{1,0:T(8,128)(2,1)}), bf16[256,1024]{1,0:T(8,128)(2,1)}) %reduce-scatter.49.cloned.1.call-update) | async-done | bytes 524304 | tf_op jit(solution)/shard_map/reduce_scatter | solution.py:206
  1280.0 55.3 %while.160 = (s32[]{:T(128)}, f32[1024,4,64]{0,2,1:T(8,128)}, f32[1024,4,64]{0,2,1:T(8,128)}, f32[2,512,4,64]{1,0,3,2:T(2,128)}, bf16[2,512,4,64]{1,3,2,0:T(8,12...) while((s32[]{:T(128)}, f32[1024,4,64]{0,2,1:T(8,128)}, ...), condition=%wide.region_70.71_spmd.clone, body=%wide.region_68.70_spmd.clone.sunk | while | flops 1375598592 | bytes 91294032 | solution.py:260
  1364.4 29.6 %reduce-scatter.51.cloned.1.call-done = bf16[256,1024]{1,0:T(8,128)(2,1)} async-done(((bf16[1024,1024]{1,0:T(8,128)(2,1)}), bf16[256,1024]{1,0:T(8,128)(2,1)}) %reduce-scatter.51.cloned.1.call-update) | async-done | bytes 524304 | tf_op jit(solution)/shard_map/reduce_scatter | solution.py:206
  1417.4 21.6 all-gather.45.cloned.1.call-done
  1449.0 30.9 %reduce-scatter.53.cloned.1.call-done = bf16[256,1024]{1,0:T(8,128)(2,1)} async-done(((bf16[1024,1024]{1,0:T(8,128)(2,1)}), bf16[256,1024]{1,0:T(8,128)(2,1)}) %reduce-scatter.53.cloned.1.call-update) | async-done | bytes 524304 | tf_op jit(solution)/shard_map/reduce_scatter | solution.py:206
  1518.1 55.3 %while.161 = (s32[]{:T(128)}, f32[1024,4,64]{0,2,1:T(8,128)}, f32[1024,4,64]{0,2,1:T(8,128)}, f32[2,512,4,64]{1,0,3,2:T(2,128)}, bf16[2,512,4,64]{1,3,2,0:T(8,12...) while((s32[]{:T(128)}, f32[1024,4,64]{0,2,1:T(8,128)}, ...), condition=%wide.region_84.85_spmd.clone, body=%wide.region_82.84_spmd.clone.sunk | while | flops 1375598592 | bytes 91294032 | solution.py:260
  1788.3 99.4 %reduce-scatter.65.cloned.1.call-done = bf16[1,256,6144]{2,1,0:T(8,128)(2,1)} async-done(((bf16[1,1024,6144]{2,1,0:T(8,128)(2,1)}), bf16[1,256,6144]{2,1,0:T(8,128)(2,1)}) %reduce-scatter.65.cloned.1.call-update) | async-done | bytes 3145744 | tf_op jit(solution)/shard_map/reduce_scatter | solution.py:534
  1932.2 26.3 %reduce-scatter.63.cloned.1.call-done = bf16[1,512,256]{2,1,0:T(8,128)(2,1)} async-done(((bf16[1,512,1024]{2,1,0:T(8,128)(2,1)}), bf16[1,512,256]{2,1,0:T(8,128)(2,1)}) %reduce-scatter.63.cloned.1.call-update) | async-done | bytes 262160 | tf_op jit(solution)/shard_map/reduce_scatter | solution.py:528
  1960.3 26.3 %reduce-scatter.61.cloned.1.call-done = bf16[1,256,512]{2,1,0:T(8,128)(2,1)} async-done(((bf16[1,1024,512]{2,1,0:T(8,128)(2,1)}), bf16[1,256,512]{2,1,0:T(8,128)(2,1)}) %reduce-scatter.61.cloned.1.call-update) | async-done | bytes 262160 | tf_op jit(solution)/shard_map/reduce_scatter | solution.py:522
  2028.8 21.2 reduce-scatter.59.cloned.1.call-done
  2051.6 34.7 %reduce-scatter.57.cloned.1.call-done = bf16[1,3,256,256]{3,2,1,0:T(8,128)(2,1)} async-done(((bf16[1,3,1024,256]{3,2,1,0:T(8,128)(2,1)}), bf16[1,3,256,256]{3,2,1,0:T(8,128)(2,1)}) %reduce-scatter.57.cloned.1.call-update) | async-done | bytes 393232 | tf_op jit(solution)/shard_map/reduce_scatter | solution.py:510
  2090.0 32.9 %reduce-scatter.75.cloned.1.call-done = bf16[1536,1]{1,0:T(8,128)(2,1)} async-done(((bf16[6144,1]{1,0:T(8,128)(2,1)}), bf16[1536,1]{1,0:T(8,128)(2,1)}) %reduce-scatter.75.cloned.1.call-update) | async-done | bytes 3088
  2132.3 60.3 %all-reduce.15.cloned.1.call-done = bf16[1,256,6144]{2,1,0:T(8,128)(2,1)} async-done(((bf16[1,256,6144]{2,1,0:T(8,128)(2,1)}), bf16[1,256,6144]{2,1,0:T(8,128)(2,1)}) %all-reduce.15.cloned.1.call-update) | async-done | bytes 3145744 | tf_op jit(solution)/shard_map/psum | solution.py:546
  (1211 shorter events, 1402.4 us)
Async XLA Ops:
  7.2 223.4 %all-gather.17.cloned.1.call-start = ((), (), s32[]{:S(2)}) async-start(), calls=%async_computation.22 | async-start | bytes 15728640 | tf_op jit(solution)/shard_map/all_gather | solution.py:156
  8.0 277.5 %all-gather.21.cloned.1.call-start = ((), (), s32[]{:S(2)}) async-start(), calls=%async_computation.24 | async-start | bytes 1966080 | tf_op jit(solution)/shard_map/all_gather | solution.py:148
  8.7 284.5 %all-gather.19.cloned.1.call-start = ((), (), s32[]{:S(2)}) async-start(), calls=%async_computation.23 | async-start | bytes 2621440 | tf_op jit(solution)/shard_map/all_gather | solution.py:179
  252.5 133.1 %reduce-scatter.33.cloned.1.call-start = ((), (), s32[]{:S(2)}) async-start(), calls=%async_computation.25 | async-start | bytes 2621440 | tf_op jit(solution)/shard_map/reduce_scatter | solution.py:189
  396.4 109.4 %reduce-scatter.35.cloned.1.call-start = ((), (), s32[]{:S(2)}) async-start(), calls=%async_computation.29 | async-start | bytes 2621440 | tf_op jit(solution)/shard_map/reduce_scatter | solution.py:189
  528.4 124.3 %reduce-scatter.37.cloned.1.call-start = ((), (), s32[]{:S(2)}) async-start(), calls=%async_computation.31 | async-start | bytes 2621440 | tf_op jit(solution)/shard_map/reduce_scatter | solution.py:189
  753.5 123.8 %reduce-scatter.41.cloned.1.call-start = ((), (), s32[]{:S(2)}) async-start(), calls=%async_computation.35 | async-start | bytes 2621440 | tf_op jit(solution)/shard_map/reduce_scatter | solution.py:189
  891.4 87.7 %reduce-scatter.45.cloned.1.call-start = ((), (), s32[]{:S(2)}) async-start(), calls=%async_computation.39 | async-start | bytes 2621440 | tf_op jit(solution)/shard_map/reduce_scatter | solution.py:206
  947.6 86.5 %all-gather.39.cloned.1.call-start = ((), (), s32[]{:S(2)}) async-start(), calls=%async_computation.40 | async-start | bytes 2621440 | tf_op jit(solution)/shard_map/all_gather | solution.py:182
  984.5 169.6 %reduce-scatter.47.cloned.1.call-start = ((), (), s32[]{:S(2)}) async-start(), calls=%async_computation.41 | async-start | bytes 2621440 | tf_op jit(solution)/shard_map/reduce_scatter | solution.py:206
  1247.5 146.5 %reduce-scatter.51.cloned.1.call-start = ((), (), s32[]{:S(2)}) async-start(), calls=%async_computation.45 | async-start | bytes 2621440 | tf_op jit(solution)/shard_map/reduce_scatter | solution.py:206
  1485.8 134.4 %reduce-scatter.43.cloned.1.call-start = ((), (), s32[]{:S(2)}) async-start(), calls=%async_computation.37 | async-start | bytes 2621440 | tf_op jit(solution)/shard_map/reduce_scatter | solution.py:189
  1500.5 130.3 %reduce-scatter.55.cloned.1.call-start = ((), (), s32[]{:S(2)}) async-start(), calls=%async_computation.49 | async-start | bytes 2621440 | tf_op jit(solution)/shard_map/reduce_scatter | solution.py:206
  1599.2 288.5 %reduce-scatter.65.cloned.1.call-start = ((), (), s32[]{:S(2)}) async-start(), calls=%async_computation.54 | async-start | bytes 15728640 | tf_op jit(solution)/shard_map/reduce_scatter | solution.py:534
  1675.6 235.4 %reduce-scatter.73.cloned.1.call-start = ((), (), s32[]{:S(2)}) async-start(), calls=%async_computation.59 | async-start | bytes 327680
  1729.3 201.6 %reduce-scatter.71.cloned.1.call-start = ((), (), s32[]{:S(2)}) async-start(), calls=%async_computation.58 | async-start | bytes 163840
  1730.9 227.6 %reduce-scatter.63.cloned.1.call-start = ((), (), s32[]{:S(2)}) async-start(), calls=%async_computation.53 | async-start | bytes 1310720 | tf_op jit(solution)/shard_map/reduce_scatter | solution.py:528
  1735.5 251.1 %reduce-scatter.61.cloned.1.call-start = ((), (), s32[]{:S(2)}) async-start(), calls=%async_computation.52 | async-start | bytes 1310720 | tf_op jit(solution)/shard_map/reduce_scatter | solution.py:522
  1748.8 259.0 %reduce-scatter.69.cloned.1.call-start = ((), (), s32[]{:S(2)}) async-start(), calls=%async_computation.57 | async-start | bytes 327680
  1770.8 256.6 %reduce-scatter.67.cloned.1.call-start = ((), (), s32[]{:S(2)}) async-start(), calls=%async_computation.56 | async-start | bytes 81920
  1774.5 275.4 %reduce-scatter.59.cloned.1.call-start = ((), (), s32[]{:S(2)}) async-start(), calls=%async_computation.51 | async-start | bytes 655360 | tf_op jit(solution)/shard_map/reduce_scatter | solution.py:516
  1777.7 308.5 %reduce-scatter.57.cloned.1.call-start = ((), (), s32[]{:S(2)}) async-start(), calls=%async_computation.50 | async-start | bytes 1966080 | tf_op jit(solution)/shard_map/reduce_scatter | solution.py:510
  1786.2 336.6 %reduce-scatter.75.cloned.1.call-start = ((), (), s32[]{:S(2)}) async-start(), calls=%async_computation.60 | async-start | bytes 1966080
  1788.3 404.2 %all-reduce.15.cloned.1.call-start = ((), (), s32[]{:S(2)}) async-start(), calls=%async_computation.55 | async-start | bytes 6291456 | tf_op jit(solution)/shard_map/psum | solution.py:546
  (292 other events, 5979.7 us)
Sparse Core Ops, SparseCore 0:
  9.6 220.9 all-gather.16
  232.2 37.3 all-gather.20
  354.1 31.4 reduce-scatter.32
  387.0 27.9 all-gather.24
  440.9 30.1 all-gather.26
  476.0 29.7 reduce-scatter.34
  528.5 23.6 all-gather.28
  621.1 31.4 reduce-scatter.36
  698.5 31.4 reduce-scatter.38
  753.7 23.5 all-gather.32
  845.8 31.4 reduce-scatter.40
  947.7 31.4 reduce-scatter.44
  1122.7 31.3 reduce-scatter.46
  1210.2 31.3 reduce-scatter.48
  1362.5 31.4 reduce-scatter.50
  1448.4 31.3 reduce-scatter.52
  1510.9 31.4 reduce-scatter.42
  1599.3 31.4 reduce-scatter.54
  1675.7 211.9 reduce-scatter.64
  1933.2 25.3 reduce-scatter.62
  1960.8 25.8 reduce-scatter.60
  2052.7 33.5 reduce-scatter.56
  2088.6 34.2 reduce-scatter.74
  2125.1 67.3 all-reduce.14
  (15 shorter events, 315.2 us)
where the time goes:
time: 2230 us; the launch traced here: 2200 us
  waiting for transfers between devices  1120 us (50%)
  local copies, waits for them, and re-layouts  338 us (15%)
  other arithmetic  328 us (15%)
  matrix products  308 us (14%)
  blocking collectives  83.6 us (4%)
    all_gather x1, waiting for transfers between devices, per_device(): lax.all_gather(w_mod, 'dp', axis=1, tiled=True)  200 us
    reduce_scatter x6, waiting for transfers between devices, spread_back(): lax.psum_scatter(partial_rows(jnp.int32(0), row_count * lax.axis_size('te...  156 us
    scatter x49, other arithmetic, place(): buffer.at[buffer_index]  139 us
    reduce_scatter x6, waiting for transfers between devices, spread_sum(): lax.psum_scatter(partial_rows(jnp.int32(0), row_count * lax.axis_size('te...  115 us
    unnamed x44, waiting for transfers between devices  111 us
    all_gather x6, waiting for transfers between devices, collect(): return lax.all_gather(normed, 'tensor', axis=0, tiled=True)  106 us
    reduce_scatter x1, waiting for transfers between devices, per_device(): lax.psum_scatter(g_wmod[None].astype(jnp.bfloat16), 'dp', scatter_dimensi...  99.4 us
    all_gather x6, waiting for transfers between devices, collect_grad(): return lax.all_gather(rows_low, 'tensor', axis=0, tiled=True)  82.1 us
  transfers between devices with their start and end apart: 43, of which 40 were waited for; matrix products, arithmetic and copies ran while one was open for 18% of the time, Pallas kernels for 0%

commit v1 on v0

v1 whole, which is shorter than its diff:
```python
import functools
import math

import jax
import jax.numpy as jnp
from jax import lax
from jax.experimental import pallas as pl
from jax.experimental.pallas import tpu as pltpu
from jax.sharding import PartitionSpec as P

HEAD_DIM = 64
SLOT_ROWS = 8
norm_eps = 1e-06
big_negative = -1e30
f32 = jnp.float32
bf16 = jnp.bfloat16
vmem_limit = 52 * 1024 * 1024


def swap(block, axis, bit):
    return lax.ppermute(block, axis, [(i, i ^ bit) for i in range(lax.axis_size(axis))])


def bits_of(count):
    bit = 1
    while bit < count:
        yield bit
        bit *= 2


def gather_rows(block):
    blocks = {0: block}
    for bit in reversed(list(bits_of(lax.axis_size("tensor")))):
        blocks.update({j | bit: swap(part, "tensor", bit) for j, part in list(blocks.items())})
    return [blocks[j] for j in range(len(blocks))]


def scatter_rows(parts):
    kept = dict(enumerate(parts))
    addends = [parts[0]]
    for bit in bits_of(len(parts)):
        arrived = {j: swap(kept[j | bit], "tensor", bit) for j in kept if not j & bit}
        addends.append(arrived.pop(0))
        kept = {
            0: parts[0],
            **{
                j: (kept[j].astype(f32) + part.astype(f32)).astype(parts[0].dtype)
                for j, part in arrived.items()
            },
        }
    return addends


def gather_groups(block):
    return lax.all_gather(block, "dp", axis=0, tiled=False)


def call(body, outs, *args, scratch=(), flops=0):
    moved = sum(x.size * x.dtype.itemsize for x in args)
    moved += sum(math.prod(x.shape) * jnp.dtype(x.dtype).itemsize for x in outs)
    return pl.pallas_call(
        body,
        out_shape=tuple(outs),
        scratch_shapes=scratch,
        compiler_params=pltpu.CompilerParams(vmem_limit_bytes=vmem_limit),
        cost_estimate=pl.CostEstimate(flops=flops, bytes_accessed=moved, transcendentals=0),
    )(*args)


def shape(dims, dtype):
    return jax.ShapeDtypeStruct(dims, dtype)


def mm(left, right):
    return lax.dot_general(left, right, (((1,), (0,)), ((), ())), preferred_element_type=f32)


def mm_last(left, right):
    return lax.dot_general(left, right, (((1,), (1,)), ((), ())), preferred_element_type=f32)


def mm_first(left, right):
    return lax.dot_general(left, right, (((0,), (0,)), ((), ())), preferred_element_type=f32)


def slot_pick(seg_col):
    rows = seg_col.shape[0]
    lane = lax.broadcasted_iota(jnp.int32, (rows, SLOT_ROWS), 1)
    return (lane == seg_col).astype(f32).astype(bf16)


def part_of(picked, mod_ref, index, width):
    values = mod_ref[:, index * width : (index + 1) * width]
    high = values.astype(bf16)
    rest = (values - high.astype(f32)).astype(bf16)
    return mm(picked, high) + mm(picked, rest)


def slot_sums(seg_row, slots, values):
    row = lax.broadcasted_iota(jnp.int32, (SLOT_ROWS, seg_row.shape[1]), 0)
    picked = ((row == seg_row) & (row < slots)).astype(f32).astype(bf16)
    return mm(picked, values.astype(bf16))


def normed(values):
    centre = values - jnp.mean(values, axis=-1, keepdims=True)
    spread = jnp.mean(centre * centre, axis=-1, keepdims=True)
    inverse = lax.rsqrt(spread + norm_eps)
    return centre * inverse, inverse


def norm_back(norm, inverse, d_norm):
    mean_d = jnp.mean(d_norm, axis=-1, keepdims=True)
    mean_dn = jnp.mean(d_norm * norm, axis=-1, keepdims=True)
    return inverse * (d_norm - mean_d - norm * mean_dn)


def total(refs):
    value = refs[0][...].astype(f32)
    for ref in refs[1:]:
        value = value + ref[...].astype(f32)
    return value


def first_norm_kernel(width, h_ref, seg_ref, mod_ref, a1_ref):
    picked = slot_pick(seg_ref[...])
    norm, _ = normed(h_ref[...].astype(f32))
    scale = part_of(picked, mod_ref, 1, width)
    shift = part_of(picked, mod_ref, 0, width)
    a1_ref[...] = (norm * (1.0 + scale) + shift).astype(bf16)


def middle_kernel(width, terms, *refs):
    sums = refs[:terms]
    h_ref, bias_ref, seg_ref, mod_ref, z1_ref, h1_ref, a2_ref = refs[terms:]
    picked = slot_pick(seg_ref[...])
    z1 = total(sums) + bias_ref[...]
    z1_ref[...] = z1.astype(bf16)
    h1 = h_ref[...].astype(f32) + part_of(picked, mod_ref, 2, width) * z1
    h1_ref[...] = h1
    norm, _ = normed(h1)
    a2_ref[...] = (
        norm * (1.0 + part_of(picked, mod_ref, 4, width)) + part_of(picked, mod_ref, 3, width)
    ).astype(bf16)


def layer_end_kernel(width, terms, *refs):
    sums = refs[:terms]
    h1_ref, bias_ref, seg_ref, mod_ref, next_ref, z2_ref, y_ref, a1_ref = refs[terms:]
    picked = slot_pick(seg_ref[...])
    z2 = total(sums) + bias_ref[...]
    z2_ref[...] = z2.astype(bf16)
    y = (h1_ref[...] + part_of(picked, mod_ref, 5, width) * z2).astype(bf16)
    y_ref[...] = y
    norm, _ = normed(y.astype(f32))
    a1_ref[...] = (
        norm * (1.0 + part_of(picked, next_ref, 1, width)) + part_of(picked, next_ref, 0, width)
    ).astype(bf16)


def branch_back(width, slots, grad, z2, picked, seg_row, mod_ref, dz2_ref, dgate_ref):
    dz2_ref[...] = (grad * part_of(picked, mod_ref, 5, width)).astype(bf16)
    dgate_ref[...] = slot_sums(seg_row, slots, grad * z2)


def turn_kernel(width, slots, terms, *refs):
    sums = refs[:terms]
    (h1_ref, bias_ref, seg_ref, seg_row_ref, mod_ref, cot_ref) = refs[terms : terms + 6]
    y_ref, c_ref, dz2_ref, dgate_ref = refs[terms + 6 :]
    seg = seg_ref[...]
    picked = slot_pick(seg)
    z2 = total(sums) + bias_ref[...]
    y_ref[...] = (h1_ref[...] + part_of(picked, mod_ref, 5, width) * z2).astype(bf16)
    grad = jnp.where(seg < slots, cot_ref[...].astype(f32), 0.0)
    c_ref[...] = grad.astype(bf16)
    branch_back(width, slots, grad, z2, picked, seg_row_ref[...], mod_ref, dz2_ref, dgate_ref)


def middle_back_kernel(width, slots, terms, *refs):
    sums = refs[:terms]
    h1_ref, c_ref, z1_ref, seg_ref, seg_row_ref, mod_ref = refs[terms : terms + 6]
    dh1_ref, dz1_ref, dgate_ref, dshift_ref, dscale_ref = refs[terms + 6 :]
    picked = slot_pick(seg_ref[...])
    seg_row = seg_row_ref[...]
    da2 = total(sums)
    norm, inverse = normed(h1_ref[...])
    dshift_ref[...] = slot_sums(seg_row, slots, da2)
    dscale_ref[...] = slot_sums(seg_row, slots, da2 * norm)
    d_norm = da2 * (1.0 + part_of(picked, mod_ref, 4, width))
    dh1 = c_ref[...].astype(f32) + norm_back(norm, inverse, d_norm)
    dh1_ref[...] = dh1
    dz1_ref[...] = (dh1 * part_of(picked, mod_ref, 2, width)).astype(bf16)
    dgate_ref[...] = slot_sums(seg_row, slots, dh1 * z1_ref[...].astype(f32))


def layer_back_kernel(width, slots, terms, more, *refs):
    sums = refs[:terms]
    h_ref, dh1_ref, seg_ref, seg_row_ref, mod_ref = refs[terms : terms + 5]
    rest = refs[terms + 5 :]
    if more:
        z2_ref, before_ref = rest[:2]
        rest = rest[2:]
    g_ref, dshift_ref, dscale_ref = rest[:3]
    picked = slot_pick(seg_ref[...])
    seg_row = seg_row_ref[...]
    da1 = total(sums)
    norm, inverse = normed(h_ref[...].astype(f32))
    dshift_ref[...] = slot_sums(seg_row, slots, da1)
    dscale_ref[...] = slot_sums(seg_row, slots, da1 * norm)
    d_norm = da1 * (1.0 + part_of(picked, mod_ref, 1, width))
    grad = (dh1_ref[...] + norm_back(norm, inverse, d_norm)).astype(bf16)
    g_ref[...] = grad
    if more:
        branch_back(
            width,
            slots,
            grad.astype(f32),
            z2_ref[...].astype(f32),
            picked,
            seg_row,
            before_ref,
            *rest[3:],
        )


def turned(values, cos, sin):
    groups = []
    for start in range(0, values.shape[1], 128):
        part = values[:, start : start + 128]
        lane = lax.broadcasted_iota(jnp.int32, part.shape, 1)
        other = jnp.where(lane % 2 == 0, pltpu.roll(part, 127, 1), pltpu.roll(part, 1, 1))
        groups.append(part * cos + other * sin)
    return groups[0] if len(groups) == 1 else jnp.concatenate(groups, axis=1)


def head_mask(lane, head):
    return (lane >= head * HEAD_DIM) & (lane < (head + 1) * HEAD_DIM)


def attend_kernel(blocks, *refs):
    x_refs = refs[:blocks]
    (
        w_ref,
        bias_ref,
        cos_ref,
        sin_ref,
        seg_ref,
        seg_row_ref,
        w_out_ref,
        q_ref,
        k_ref,
        v_ref,
        o_ref,
        lse_ref,
    ) = refs[blocks : blocks + 12]
    part_refs = refs[blocks + 12 :]
    rows, width = x_refs[0].shape
    groups, _, local = w_out_ref.shape[0], 0, w_ref.shape[2]
    depth = width // groups
    heads = local // HEAD_DIM
    weights = [w_ref[:, p * depth : (p + 1) * depth, :].reshape(width, local) for p in range(3)]
    for j in range(blocks):
        here = slice(j * rows, (j + 1) * rows)
        x = x_refs[j][...]
        cos, sin = cos_ref[here, :], sin_ref[here, :]
        q = turned(mm(x, weights[0]) + bias_ref[0:1, :], cos, sin)
        q_ref[here, :] = (q.astype(bf16).astype(f32) * (HEAD_DIM**-0.5)).astype(bf16)
        k_ref[here, :] = turned(mm(x, weights[1]) + bias_ref[1:2, :], cos, sin).astype(bf16)
        v_ref[here, :] = (mm(x, weights[2]) + bias_ref[2:3, :]).astype(bf16)

    def one_block(i, carry):
        here = pl.ds(pl.multiple_of(i * rows, rows), rows)
        q = q_ref[here, :]
        allowed = seg_ref[here, :] == seg_row_ref[...]
        lane = lax.broadcasted_iota(jnp.int32, (rows, local), 1)
        wide_lane = lax.broadcasted_iota(jnp.int32, (rows, 128), 1)
        mixed = jnp.zeros((rows, local), f32)
        lse = jnp.zeros((rows, 128), f32)
        for head in range(heads):
            mine = head_mask(lane, head)
            scores = mm_last(jnp.where(mine, q, jnp.zeros_like(q)), k_ref[...])
            scores = jnp.where(allowed, scores, big_negative)
            top = jnp.max(scores, axis=-1, keepdims=True)
            weight = jnp.exp(scores - top)
            weight_sum = jnp.sum(weight, axis=-1, keepdims=True)
            mixed = jnp.where(mine, mm(weight.astype(bf16), v_ref[...]) / weight_sum, mixed)
            lse = jnp.where(wide_lane == head, top + jnp.log(weight_sum), lse)
        o_ref[here, :] = mixed.astype(bf16)
        lse_ref[here, :] = lse
        return carry

    lax.fori_loop(0, blocks, one_block, 0)
    for j in range(blocks):
        mixed = o_ref[j * rows : (j + 1) * rows, :]
        for g in range(groups):
            part_refs[j][:, g * depth : (g + 1) * depth] = mm(mixed, w_out_ref[g]).astype(bf16)


def attend_back_kernel(blocks, *refs):
    dz_refs = refs[:blocks]
    (
        w_ref,
        w_out_ref,
        q_ref,
        k_ref,
        v_ref,
        lse_ref,
        cos_ref,
        sin_ref,
        seg_ref,
        seg_row_ref,
        dq_ref,
        dk_ref,
        dv_ref,
    ) = refs[blocks : blocks + 13]
    part_refs = refs[blocks + 13 : 2 * blocks + 13]
    do_ref, dk_sum, dv_sum = refs[2 * blocks + 13 :]
    rows, width = dz_refs[0].shape
    groups, local = w_out_ref.shape[0], w_ref.shape[2]
    depth = width // groups
    heads = local // HEAD_DIM
    scale = HEAD_DIM**-0.5
    for j in range(blocks):
        value = jnp.zeros((rows, local), f32)
        for g in range(groups):
            value = value + mm_last(dz_refs[j][:, g * depth : (g + 1) * depth], w_out_ref[g])
        do_ref[j * rows : (j + 1) * rows, :] = value.astype(bf16)
    dk_sum[...] = jnp.zeros_like(dk_sum)
    dv_sum[...] = jnp.zeros_like(dv_sum)

    def one_block(i, carry):
        here = pl.ds(pl.multiple_of(i * rows, rows), rows)
        q, do = q_ref[here, :], do_ref[here, :]
        lse = lse_ref[here, :]
        allowed = seg_ref[here, :] == seg_row_ref[...]
        lane = lax.broadcasted_iota(jnp.int32, (rows, local), 1)
        dq = jnp.zeros((rows, local), f32)
        for head in range(heads):
            mine = head_mask(lane, head)
            q_head = jnp.where(mine, q, jnp.zeros_like(q))
            do_head = jnp.where(mine, do, jnp.zeros_like(do))
            scores = mm_last(q_head, k_ref[...])
            prob = jnp.exp(jnp.where(allowed, scores, big_negative) - lse[:, head : head + 1])
            d_prob = mm_last(do_head, v_ref[...])
            product = prob * d_prob
            centre = jnp.sum(product, axis=-1, keepdims=True)
            d_scores = (product - prob * centre).astype(bf16)
            dv_sum[...] += mm_first(prob.astype(bf16), do_head)
            dk_sum[...] += mm_first(d_scores, q_head)
            dq = jnp.where(mine, mm(d_scores, k_ref[...]), dq)
        dq_ref[here, :] = turned(dq * scale, cos_ref[here, :], -sin_ref[here, :]).astype(bf16)
        return carry

    lax.fori_loop(0, blocks, one_block, 0)
    weights = [w_ref[:, p * depth : (p + 1) * depth, :].reshape(width, local) for p in range(3)]
    for j in range(blocks):
        here = slice(j * rows, (j + 1) * rows)
        dk = turned(dk_sum[here, :], cos_ref[here, :], -sin_ref[here, :]).astype(bf16)
        dv = dv_sum[here, :].astype(bf16)
        dk_ref[here, :] = dk
        dv_ref[here, :] = dv
        part_refs[j][...] = (
            mm_last(dq_ref[here, :], weights[0]) + mm_last(dk, weights[1]) + mm_last(dv, weights[2])
        ).astype(bf16)


def feed_kernel(blocks, *refs):
    a_refs = refs[:blocks]
    w_up_ref, bias_ref, w_down_ref, u_ref, g_ref = refs[blocks : blocks + 5]
    part_refs = refs[blocks + 5 :]
    rows, width = a_refs[0].shape
    groups, units, depth = w_down_ref.shape
    w_up = w_up_ref[...].reshape(width, units)
    for j in range(blocks):
        here = slice(j * rows, (j + 1) * rows)
        u = mm(a_refs[j][...], w_up) + bias_ref[...]
        u_ref[here, :] = u
        inner = math.sqrt(2.0 / math.pi) * (u + 0.044715 * (u * u * u))
        g = (0.5 * u * (1.0 + jnp.tanh(inner))).astype(bf16)
        g_ref[here, :] = g
        for k in range(groups):
            part_refs[j][:, k * depth : (k + 1) * depth] = mm(g, w_down_ref[k]).astype(bf16)


def feed_back_kernel(blocks, *refs):
    dz_refs = refs[:blocks]
    w_up_ref, w_down_ref, u_ref, du_ref = refs[blocks : blocks + 4]
    part_refs = refs[blocks + 4 :]
    rows, width = dz_refs[0].shape
    groups, units, depth = w_down_ref.shape
    w_up = w_up_ref[...].reshape(width, units)
    root = math.sqrt(2.0 / math.pi)
    for j in range(blocks):
        here = slice(j * rows, (j + 1) * rows)
        dg = jnp.zeros((rows, units), f32)
        for k in range(groups):
            dg = dg + mm_last(dz_refs[j][:, k * depth : (k + 1) * depth], w_down_ref[k])
        u = u_ref[here, :]
        square = u * u
        th = jnp.tanh(root * u * (1.0 + 0.044715 * square))
        slope = 0.5 * (1.0 + th) + 0.5 * u * (1.0 - th * th) * (root * (1.0 + 0.134145 * square))
        du = (dg * slope).astype(bf16)
        du_ref[here, :] = du
        part_refs[j][...] = mm_last(du, w_up).astype(bf16)


def feed_grads_kernel(blocks, *refs):
    a_refs, dz_refs = refs[:blocks], refs[blocks : 2 * blocks]
    g_ref, du_ref, up_ref, down_ref, bias_up_ref, bias_down_ref = refs[2 * blocks :]
    rows = a_refs[0].shape[0]
    groups, units, depth = down_ref.shape
    dz = jnp.concatenate([ref[...] for ref in dz_refs], axis=0)
    a2 = jnp.concatenate([ref[...] for ref in a_refs], axis=0)
    for k in range(groups):
        here = slice(k * depth, (k + 1) * depth)
        down_ref[k] = mm_first(g_ref[...], dz[:, here]).astype(bf16)
        up_ref[k] = mm_first(a2[:, here], du_ref[...]).astype(bf16)
    ones = jnp.ones((SLOT_ROWS, rows * blocks), bf16)
    bias_up_ref[...] = mm(ones, du_ref[...])
    bias_down_ref[...] = mm(ones, dz)


def out_grads_kernel(blocks, *refs):
    dz_refs = refs[:blocks]
    o_ref, out_ref, bias_ref = refs[blocks:]
    rows = dz_refs[0].shape[0]
    groups, _, depth = out_ref.shape
    dz = jnp.concatenate([ref[...] for ref in dz_refs], axis=0)
    for k in range(groups):
        out_ref[k] = mm_first(o_ref[...], dz[:, k * depth : (k + 1) * depth]).astype(bf16)
    bias_ref[...] = mm(jnp.ones((SLOT_ROWS, rows * blocks), bf16), dz)


def qkv_grads_kernel(blocks, *refs):
    a_refs = refs[:blocks]
    dq_ref, dk_ref, dv_ref, w_ref, bias_ref = refs[blocks:]
    rows = a_refs[0].shape[0]
    groups, packed, _ = w_ref.shape
    depth = a_refs[0].shape[1] // groups
    a1 = jnp.concatenate([ref[...] for ref in a_refs], axis=0)
    ones = jnp.ones((SLOT_ROWS, rows * blocks), bf16)
    for p, ref in enumerate((dq_ref, dk_ref, dv_ref)):
        bias_ref[p] = mm(ones, ref[...])
        for k in range(groups):
            w_ref[k, p * depth : (p + 1) * depth, :] = mm_first(
                a1[:, k * depth : (k + 1) * depth], ref[...]
            ).astype(bf16)


def per_device(
    endpoints,
    lengths,
    timesteps,
    w_qkv,
    b_qkv,
    w_out,
    b_out,
    w_up,
    b_up,
    w_down,
    b_down,
    w_mod,
    b_mod,
):
    section = lax.axis_index("section")
    tensor = lax.axis_index("tensor")
    group = lax.axis_index("dp")
    tensors, groups = lax.axis_size("tensor"), lax.axis_size("dp")
    micros, rows, width = endpoints.shape[1], endpoints.shape[3], endpoints.shape[4]
    slots = lengths.shape[2]
    frames = rows * tensors
    depth = width // groups
    local = w_qkv.shape[3]
    units = w_up.shape[2]
    first = section == 0
    terms = len(list(bits_of(tensors))) + 1

    def pick(here, other):
        return jnp.where(first, here, other), jnp.where(first, other, here)

    kept = lax.dynamic_index_in_dim(endpoints[0, :, 0], section, 0, keepdims=False)
    given = lax.dynamic_index_in_dim(endpoints[0, :, 0], 1 - section, 0, keepdims=False)
    taken = swap(given, "section", 1)
    h0, cotangent = jnp.where(first, kept, taken), jnp.where(first, taken, kept)

    def lane_row(vector):
        flat = vector.reshape(-1, vector.shape[-1])
        return jnp.pad(flat, ((0, 0), (0, local - flat.shape[1])))

    qkv_pack = jnp.concatenate(
        [
            w_qkv[0].reshape(3 * depth, local),
            lane_row(b_qkv[0]),
            lane_row(b_out),
            lane_row(b_up),
            lane_row(b_down),
            jnp.zeros((2, local), bf16),
        ],
        axis=0,
    )
    shards = [qkv_pack, w_out[0], w_up[0], w_down[0]]
    layer_shards = [pick(shard, swap(shard, "section", 1)) for shard in shards]
    full = []
    for layer in range(2):
        full.append([gather_groups(shard[layer]) for shard in layer_shards])

    def biases(layer):
        tail = full[layer][0][:, 3 * depth :, :].astype(f32)
        qkv = tail[:, :3, : local // groups].transpose(1, 0, 2).reshape(3, local)
        out = tail[:, 3, :depth].reshape(1, width)
        up = tail[:, 4, : units // groups].reshape(1, units)
        down = tail[:, 5, :depth].reshape(1, width)
        return jnp.pad(qkv, ((0, SLOT_ROWS - 3), (0, 0))), out, up, down

    steps = jnp.pad(timesteps[:, 0], ((0, 0), (0, SLOT_ROWS - slots)))
    all_steps = jnp.stack(
        [steps] + [swap(steps, "dp", j) for j in range(1, groups)]
    )
    column = group * depth + jnp.arange(depth, dtype=jnp.int32)
    half = width // 2
    frequency = jnp.exp((column % half).astype(f32) * (-math.log(10000.0) / (half - 1)))
    angle = all_steps.astype(f32)[..., None] * frequency
    codes = jax.nn.silu(jnp.where(column < half, jnp.sin(angle), jnp.cos(angle))).astype(bf16)
    mod_width = w_mod.shape[2]
    strip = mod_width // tensors
    strip_start = tensor * strip
    bias_all = lax.dynamic_update_slice(
        jnp.zeros((mod_width,), f32), b_mod[0].astype(f32), (group * b_mod.shape[1],)
    )
    mod_part = jnp.einsum(
        "zmud,de->zmue",
        codes,
        lax.dynamic_slice_in_dim(w_mod[0], strip_start, strip, 1),
        preferred_element_type=f32,
    ) + lax.dynamic_slice_in_dim(bias_all, strip_start, strip)
    mine = lax.dynamic_index_in_dim(mod_part, section, 1, keepdims=False)
    other = swap(
        lax.dynamic_index_in_dim(mod_part, 1 - section, 1, keepdims=False), "section", 1
    )
    both = jnp.stack(pick(mine, other), axis=1)
    mod_strip = both[0]
    for j in range(1, groups):
        mod_strip = mod_strip + swap(both[j], "dp", j)
    mod_all = jnp.zeros((2, SLOT_ROWS, tensors, strip), f32)
    for j, block in enumerate(gather_rows(mod_strip)):
        mod_all = lax.dynamic_update_slice(mod_all, block[:, :, None], (0, 0, tensor ^ j, 0))
    live_slots = jnp.arange(SLOT_ROWS) < slots
    mod_all = jnp.where(
        live_slots[None, :, None], mod_all.reshape(2, SLOT_ROWS, mod_width), 0.0
    )

    lengths_here = lax.dynamic_index_in_dim(lengths[:, 0], section, 0, keepdims=False)
    block_index = tensor ^ jnp.arange(tensors, dtype=jnp.int32)
    frame = (block_index[:, None] * rows + jnp.arange(rows, dtype=jnp.int32)).reshape(-1)
    ends = jnp.cumsum(lengths_here)
    segment = jnp.sum((frame[:, None] >= ends[None, :]).astype(jnp.int32), axis=1)
    member = segment[:, None] == jnp.arange(slots, dtype=jnp.int32)[None, :]
    begin = jnp.sum(jnp.where(member, (ends - lengths_here)[None, :], 0), axis=1)
    position = (frame - begin).astype(f32)
    lane = jnp.arange(128, dtype=jnp.int32) % HEAD_DIM
    inverse = jnp.exp((lane // 2).astype(f32) * (-2.0 * math.log(10000.0) / HEAD_DIM))
    angles = position[:, None] * inverse[None, :]
    cos_table = jnp.cos(angles)
    sin_table = jnp.sin(angles) * jnp.where(lane % 2 == 0, -1.0, 1.0)
    seg_col, seg_row = segment[:, None], segment[None, :]
    own_col, own_row = seg_col[:rows], seg_row[:, :rows]

    frame_block = shape((rows, width), bf16)
    frame_block32 = shape((rows, width), f32)
    wide_local = shape((frames, local), bf16)
    slot_block = shape((SLOT_ROWS, width), f32)
    project = 2 * frames * width * local

    (a1,) = call(
        functools.partial(first_norm_kernel, width), [frame_block], h0, own_col, mod_all[0]
    )
    layer_in = h0
    saved = []
    outputs = []
    for layer in range(2):
        packed, w_out_all, w_up_all, w_down_all = full[layer]
        bias_qkv, bias_out, bias_up, bias_down = biases(layer)
        a1_all = gather_rows(a1)
        q, k, v, o, lse, *parts = call(
            functools.partial(attend_kernel, tensors),
            [wide_local] * 4 + [shape((frames, 128), f32)] + [frame_block] * tensors,
            *a1_all,
            packed,
            bias_qkv,
            cos_table,
            sin_table,
            seg_col,
            seg_row,
            w_out_all,
            flops=4 * project + 8 * frames * frames * local,
        )
        z1, h1, a2 = call(
            functools.partial(middle_kernel, width, terms),
            [frame_block, frame_block32, frame_block],
            *scatter_rows(parts),
            layer_in,
            bias_out,
            own_col,
            mod_all[layer],
        )
        a2_all = gather_rows(a2)
        u, g, *parts = call(
            functools.partial(feed_kernel, tensors),
            [shape((frames, units), f32), shape((frames, units), bf16)] + [frame_block] * tensors,
            *a2_all,
            w_up_all,
            bias_up,
            w_down_all,
            flops=4 * frames * width * units,
        )
        sums = scatter_rows(parts)
        kept_state = [layer_in, a1_all, q, k, v, o, lse, z1, h1, a2_all, u, g]
        if layer == 0:
            z2, y, a1 = call(
                functools.partial(layer_end_kernel, width, terms),
                [frame_block] * 3,
                *sums,
                h1,
                bias_down,
                own_col,
                mod_all[layer],
                mod_all[layer + 1],
            )
            layer_in = y
        else:
            z2 = None
            y, grad, dz2, dgate_b = call(
                functools.partial(turn_kernel, width, slots, terms),
                [frame_block, frame_block, frame_block, slot_block],
                *sums,
                h1,
                bias_down,
                own_col,
                own_row,
                mod_all[layer],
                cotangent,
            )
        outputs.append(y)
        saved.append(kept_state + [z2])

    grads = [None, None]
    in_grads = [None, None]
    d_mods = [None, None]
    for layer in (1, 0):
        packed, w_out_all, w_up_all, w_down_all = full[layer]
        layer_in, a1_all, q, k, v, o, lse, z1, h1, a2_all, u, g, _ = saved[layer]
        dz2_all = gather_rows(dz2)
        du, *parts = call(
            functools.partial(feed_back_kernel, tensors),
            [shape((frames, units), bf16)] + [frame_block] * tensors,
            *dz2_all,
            w_up_all,
            w_down_all,
            u,
            flops=4 * frames * width * units,
        )
        sums = scatter_rows(parts)
        d_up, d_down, d_bias_up, d_bias_down = call(
            functools.partial(feed_grads_kernel, tensors),
            [
                shape((groups, depth, units), bf16),
                shape((groups, units, depth), bf16),
                shape((SLOT_ROWS, units), f32),
                shape((SLOT_ROWS, width), f32),
            ],
            *a2_all,
            *dz2_all,
            g,
            du,
            flops=4 * frames * width * units,
        )
        dh1, dz1, dgate_a, dshift_b, dscale_b = call(
            functools.partial(middle_back_kernel, width, slots, terms),
            [frame_block32, frame_block] + [slot_block] * 3,
            *sums,
            h1,
            grad,
            z1,
            own_col,
            own_row,
            mod_all[layer],
        )
        dz1_all = gather_rows(dz1)
        dq, dk, dv, *parts = call(
            functools.partial(attend_back_kernel, tensors),
            [wide_local] * 3 + [frame_block] * tensors,
            *dz1_all,
            packed,
            w_out_all,
            q,
            k,
            v,
            lse,
            cos_table,
            sin_table,
            seg_col,
            seg_row,
            scratch=[
                pltpu.VMEM((frames, local), bf16),
                pltpu.VMEM((frames, local), f32),
                pltpu.VMEM((frames, local), f32),
            ],
            flops=4 * project + 20 * frames * frames * local,
        )
        sums = scatter_rows(parts)
        d_out, d_bias_out = call(
            functools.partial(out_grads_kernel, tensors),
            [shape((groups, local, depth), bf16), shape((SLOT_ROWS, width), f32)],
            *dz1_all,
            o,
            flops=project,
        )
        d_qkv, d_bias_qkv = call(
            functools.partial(qkv_grads_kernel, tensors),
            [shape((groups, 3 * depth, local), bf16), shape((3, SLOT_ROWS, local), f32)],
            *a1_all,
            dq,
            dk,
            dv,
            flops=3 * project,
        )
        kernel = functools.partial(layer_back_kernel, width, slots, terms, layer > 0)
        arrays = [*sums, layer_in, dh1, own_col, own_row, mod_all[layer]]
        if layer > 0:
            grad_out, dshift_a, dscale_a, dz2, next_dgate = call(
                kernel,
                [frame_block, slot_block, slot_block, frame_block, slot_block],
                *arrays,
                saved[layer - 1][-1],
                mod_all[layer - 1],
            )
        else:
            grad_out, dshift_a, dscale_a = call(
                kernel, [frame_block, slot_block, slot_block], *arrays
            )
            next_dgate = None
        grad = grad_out
        in_grads[layer] = grad_out
        d_mods[layer] = jnp.concatenate(
            [dshift_a, dscale_a, dgate_a, dshift_b, dscale_b, dgate_b], axis=1
        )
        dgate_b = next_dgate

        def by_group(vector, count):
            return jnp.pad(
                vector.reshape(groups, 1, count), ((0, 0), (0, 0), (0, local - count))
            )

        bias_rows = jnp.concatenate(
            [by_group(d_bias_qkv[p, 0], local // groups) for p in range(3)]
            + [
                by_group(d_bias_out[0], depth),
                by_group(d_bias_up[0], units // groups),
                by_group(d_bias_down[0], depth),
                jnp.zeros((groups, 2, local), f32),
            ],
            axis=1,
        ).astype(bf16)
        grads[layer] = [
            lax.psum_scatter(value, "dp", scatter_dimension=0, tiled=False)
            for value in (
                d_up,
                d_down,
                d_out,
                jnp.concatenate([d_qkv, bias_rows], axis=1),
            )
        ]

    def to_section(pair):
        low, high = pair
        up = lax.ppermute(high, "section", [(0, 1)])
        down = lax.ppermute(low, "section", [(1, 0)])
        return jnp.where(
            first,
            low.astype(f32) + down.astype(f32),
            high.astype(f32) + up.astype(f32),
        )

    def frames_out(pair):
        low, high = pair
        arrived = lax.ppermute(high, "section", [(0, 1)]) + lax.ppermute(
            low, "section", [(1, 0)]
        )
        own = jnp.where(first, low, high)
        return jnp.where(first, jnp.stack([own, arrived]), jnp.stack([arrived, own]))

    activations = frames_out(outputs)
    input_grads = frames_out(in_grads)
    g_up, g_down, g_out, g_qkv = [to_section(pair) for pair in zip(*grads, strict=True)]
    tail = g_qkv[3 * depth :]

    def strips(value):
        return [
            lax.dynamic_slice_in_dim(value, (tensor ^ j) * strip, strip, 1) for j in range(tensors)
        ]

    own_mod = []
    for layer in range(2):
        added = scatter_rows(strips(d_mods[layer]))
        own_mod.append(functools.reduce(jnp.add, added))
    low, high = own_mod
    arrived = lax.ppermute(high, "section", [(0, 1)]) + lax.ppermute(low, "section", [(1, 0)])
    pair = jnp.stack([jnp.where(first, low, high), arrived]).astype(bf16)
    pairs = jnp.stack([pair] + [swap(pair, "dp", j) for j in range(1, groups)])
    d_mod = jnp.zeros((groups, micros, SLOT_ROWS, tensors, strip), bf16)
    for j, block in enumerate(gather_rows(pairs)):
        d_mod = lax.dynamic_update_slice(d_mod, block[:, :, :, None], (0, 0, 0, tensor ^ j, 0))
    d_mod = d_mod.reshape(groups * micros * SLOT_ROWS, mod_width)
    own_first = jnp.where(first, codes, codes[:, ::-1]).reshape(-1, depth)
    g_wmod = lax.dot_general(
        own_first, d_mod, (((0,), (0,)), ((), ())), preferred_element_type=f32
    )
    g_bmod = jnp.sum(
        lax.dynamic_slice_in_dim(d_mod, group * b_mod.shape[1], b_mod.shape[1], 1).astype(f32),
        axis=0,
    )
    return (
        activations[None, :, None],
        input_grads[None, :, None],
        g_qkv[: 3 * depth].reshape(1, 3, depth, local),
        tail[:3, : local // groups][None],
        g_out[None],
        tail[3:4, :depth],
        g_up[None],
        tail[4:5, : units // groups],
        g_down[None],
        tail[5:6, :depth],
        g_wmod[None],
        g_bmod[None],
    )


def solution(mesh):
    return jax.shard_map(
        per_device,
        mesh=mesh,
        in_specs=(
            P("section", None, "dp", "tensor", None),
            P(None, "dp", None),
            P(None, "dp", None),
            P("section", None, "dp", "tensor"),
            P("section", None, ("tensor", "dp")),
            P("section", "tensor", "dp"),
            P("section", "dp"),
            P("section", "dp", "tensor"),
            P("section", ("tensor", "dp")),
            P("section", "tensor", "dp"),
            P("section", "dp"),
            P("section", "dp", None),
            P("section", "dp"),
        ),
        out_specs=(
            P("section", None, "dp", "tensor", None),
            P("section", None, "dp", "tensor", None),
            P("section", None, "dp", "tensor"),
            P("section", None, ("tensor", "dp")),
            P("section", "tensor", "dp"),
            P("section", "dp"),
            P("section", "dp", "tensor"),
            P("section", ("tensor", "dp")),
            P("section", "tensor", "dp"),
            P("section", "dp"),
            P("section", "dp", None),
            P("section", "dp"),
        ),
        check_vma=False,
    )
```

time: 2230 us -> 686 us (0.31)
  waiting for transfers between devices: 1120 us -> 244 us
  matrix products: 308 us -> 5.16 us
  other arithmetic: 328 us -> 32.2 us
  local copies, waits for them, and re-layouts: 338 us -> 87.2 us
  Pallas kernels: 0 us -> 160 us
  starting transfers between devices: 13.1 us -> 92.1 us
  blocking collectives: 83.6 us -> 39 us
    reduce_scatter x17 -> x8, waiting for transfers between devices: 478 us -> 0.09 us  [per_device(): lax.psum_scatter(value, 'dp', scatter_dimension=0, tiled=False)]
    all_gather x16 -> x6, waiting for transfers between devices: 421 us -> 7.03 us  [gather_groups(): return lax.all_gather(block, 'dp', axis=0, tiled=False)]
    dot_general x104 -> x2, matrix products: 308 us -> 5.16 us  [the longest x1 4.61 us: per_device(): lax.dot_general(own_first, d_mod, (((0,), (0,)), ((), ())), preferred_ele...]
    ppermute x4 -> x89, waiting for transfers between devices: 44.8 us -> 236 us  [the longest x75 221 us: swap(): lax.ppermute(block, axis, [(i, i ^ bit) for i in range(lax.axis_size(axis...]
    pallas_call x0 -> x23, Pallas kernels: none -> 160 us  [call(): pl.pallas_call(body, out_shape=tuple(outs), scratch_shapes=scratch, compi...]
    scatter x49 -> x0, other arithmetic: 139 us -> none  [place(): buffer.at[buffer_index]]
    unnamed x44 -> x14, waiting for transfers between devices: 111 us -> 0.75 us
    ppermute x4 -> x89, starting transfers between devices: 9.74 us -> 91 us  [the longest x75 56.3 us: swap(): lax.ppermute(block, axis, [(i, i ^ bit) for i in range(lax.axis_size(axis...]
  transfers between devices with their start and end apart: 43 -> 103, of which waited for: 40 -> 40; matrix products, arithmetic and copies ran while one was open for 18% -> 14% of each run, Pallas kernels for 0% -> 21%
where the time goes in v1:
time: 686 us; the launch traced here: 676 us
  waiting for transfers between devices  244 us (36%)
  Pallas kernels  160 us (23%)
  starting transfers between devices  92.1 us (13%)
  local copies, waits for them, and re-layouts  87.2 us (13%)
  blocking collectives  39 us (6%)
  other arithmetic  32.2 us (5%)
  between operations  15.8 us (2%)
    ppermute x75, waiting for transfers between devices, swap(): lax.ppermute(block, axis, [(i, i ^ bit) for i in range(lax.axis_size(axis...  221 us
    pallas_call x23, Pallas kernels, call(): pl.pallas_call(body, out_shape=tuple(outs), scratch_shapes=scratch, compi...  160 us
    ppermute x75, starting transfers between devices, swap(): lax.ppermute(block, axis, [(i, i ^ bit) for i in range(lax.axis_size(axis...  56.3 us
    all_gather x2, blocking collectives, gather_groups(): return lax.all_gather(block, 'dp', axis=0, tiled=False)  39 us
    dynamic_update_slice x4, local copies, waits for them, and re-layouts, per_device(): lax.dynamic_update_slice(d_mod, block[:, :, :, None], (0, 0, 0, tensor ^...  27.8 us
    unnamed x219, local copies, waits for them, and re-layouts  26 us
    concatenate x2, local copies, waits for them, and re-layouts, per_device(): jnp.concatenate([d_qkv, bias_rows], axis=1)  16 us
    ppermute x4, waiting for transfers between devices, to_section(): down = lax.ppermute(low, 'section', [(1, 0)])  14.9 us
  transfers between devices with their start and end apart: 103, of which 40 were waited for; matrix products, arithmetic and copies ran while one was open for 14% of the time, Pallas kernels for 21%

profile of v1, /device:TPU:0, one launch (start us, length us, event | category | flops | bytes accessed | tf_op | source)
XLA Modules:
  0.0 675.9 jit_solution(14424340089938058152)
XLA Ops:
  26.4 15.2 %collective-permute-done.4 = f32[4,8,1536]{2,1,0:T(8,128)S(1)} collective-permute-done((f32[4,8,1536]{2,1,0:T(8,128)S(1)}, f32[4,8,1536]{2,1,0:T(8,128)S(1)}, u32[]{:S(2)}, u32[]{:S(2)}) %collective-permute-start.4) | collective-permute-done | bytes 196640 | tf_op jit(solution)/shard_map/ppermute | solution.py:21
  69.9 7.5 %collective-permute-done.12.refs_2_ = bf16[256,1024]{1,0:T(8,128)(2,1)S(1)} collective-permute-done((bf16[256,1024]{1,0:T(8,128)(2,1)S(1)}, bf16[256,1024]{1,0:T(8,128)(2,1)S(1)}, u32[]{:S(2)}, u32[]{:S(2)}) %collective-permute-start.12) | collective-permute-done | bytes 524320 | tf_op jit(solution)/shard_map/ppermute | solution.py:21
  77.4 22.2 %all-gather.1 = bf16[1024,256]{1,0:T(8,128)(2,1)} all-gather(bf16[256,256]{1,0:T(8,128)(2,1)S(1)} %get-tuple-element.279), channel_id=3, replica_groups=mesh['section'=2,'tensor'=4,'dp'=4] {'dp'}, dimensions={0}, use_global_device_ids=true | all-gather | bytes 655360 | tf_op jit(solution)/shard_map/all_gather | solution.py:55
  107.6 15.4 %shard_map.221 = (bf16[1024,256]{1,0:T(8,128)(2,1)S(1)}, bf16[1024,256]{1,0:T(8,128)(2,1)S(1)}, bf16[1024,256]{1,0:T(8,128)(2,1)S(1)}, bf16[1024,256]{1,0:T(8,12...) custom-call(bf16[256,1024]{1,0:T(8,128)(2,1)} %copy-done.21, ...), custom_call_target="tpu_custom_call" | custom-call | flops 4294967296 | bytes 9994240 | tf_op jit(solution)/shard_map/pallas_call | solution.py:61
  135.7 12.5 %collective-permute-done.18.refs_2_ = bf16[256,1024]{1,0:T(8,128)(2,1)S(1)} collective-permute-done((bf16[256,1024]{1,0:T(8,128)(2,1)S(1)}, bf16[256,1024]{1,0:T(8,128)(2,1)S(1)}, u32[]{:S(2)}, u32[]{:S(2)}) %collective-permute-start.18) | collective-permute-done | bytes 524320 | tf_op jit(solution)/shard_map/ppermute | solution.py:21
  154.2 12.2 %collective-permute-done.20.refs_2_ = bf16[256,1024]{1,0:T(8,128)(2,1)S(1)} collective-permute-done((bf16[256,1024]{1,0:T(8,128)(2,1)S(1)}, bf16[256,1024]{1,0:T(8,128)(2,1)S(1)}, u32[]{:S(2)}, u32[]{:S(2)}) %collective-permute-start.20) | collective-permute-done | bytes 524320 | tf_op jit(solution)/shard_map/ppermute | solution.py:21
  179.7 12.5 %collective-permute-done.26.refs_2_ = bf16[256,1024]{1,0:T(8,128)(2,1)S(1)} collective-permute-done((bf16[256,1024]{1,0:T(8,128)(2,1)S(1)}, bf16[256,1024]{1,0:T(8,128)(2,1)S(1)}, u32[]{:S(2)}, u32[]{:S(2)}) %collective-permute-start.26) | collective-permute-done | bytes 524320 | tf_op jit(solution)/shard_map/ppermute | solution.py:21
  198.3 12.0 %collective-permute-done.28.refs_2_ = bf16[256,1024]{1,0:T(8,128)(2,1)S(1)} collective-permute-done((bf16[256,1024]{1,0:T(8,128)(2,1)}, bf16[256,1024]{1,0:T(8,128)(2,1)S(1)}, u32[]{:S(2)}, u32[]{:S(2)}) %collective-permute-start.28) | collective-permute-done | bytes 524320 | tf_op jit(solution)/shard_map/ppermute | solution.py:21
  210.2 16.8 %all-gather.5 = bf16[1024,256]{1,0:T(8,128)(2,1)} all-gather(bf16[256,256]{1,0:T(8,128)(2,1)S(1)} %get-tuple-element.278), channel_id=7, replica_groups=mesh['section'=2,'tensor'=4,'dp'=4] {'dp'}, dimensions={0}, use_global_device_ids=true | all-gather | bytes 655360 | tf_op jit(solution)/shard_map/all_gather | solution.py:55
  228.9 15.2 %shard_map.225 = (bf16[1024,256]{1,0:T(8,128)(2,1)S(1)}, bf16[1024,256]{1,0:T(8,128)(2,1)S(1)}, bf16[1024,256]{1,0:T(8,128)(2,1)S(1)}, bf16[1024,256]{1,0:T(8,12...) custom-call(bf16[256,1024]{1,0:T(8,128)(2,1)} %get-tuple-element.124, ...), custom_call_target="tpu_custom_call" | custom-call | flops 4294967296 | bytes 9994240 | tf_op jit(solution)/shard_map/pallas_call | solution.py:61
  251.7 12.4 %collective-permute-done.32.refs_2_ = bf16[256,1024]{1,0:T(8,128)(2,1)S(1)} collective-permute-done((bf16[256,1024]{1,0:T(8,128)(2,1)}, bf16[256,1024]{1,0:T(8,128)(2,1)S(1)}, u32[]{:S(2)}, u32[]{:S(2)}) %collective-permute-start.32) | collective-permute-done | bytes 524320 | tf_op jit(solution)/shard_map/ppermute | solution.py:21
  270.2 11.7 %collective-permute-done.34.refs_2_ = bf16[256,1024]{1,0:T(8,128)(2,1)S(1)} collective-permute-done((bf16[256,1024]{1,0:T(8,128)(2,1)S(1)}, bf16[256,1024]{1,0:T(8,128)(2,1)S(1)}, u32[]{:S(2)}, u32[]{:S(2)}) %collective-permute-start.34) | collective-permute-done | bytes 524320 | tf_op jit(solution)/shard_map/ppermute | solution.py:21
  295.0 12.5 %collective-permute-done.38.refs_2_ = bf16[256,1024]{1,0:T(8,128)(2,1)S(1)} collective-permute-done((bf16[256,1024]{1,0:T(8,128)(2,1)S(1)}, bf16[256,1024]{1,0:T(8,128)(2,1)S(1)}, u32[]{:S(2)}, u32[]{:S(2)}) %collective-permute-start.38) | collective-permute-done | bytes 524320 | tf_op jit(solution)/shard_map/ppermute | solution.py:21
  314.1 11.7 %collective-permute-done.42.refs_2_.refs_6_ = bf16[256,1024]{1,0:T(8,128)(2,1)S(1)} collective-permute-done((bf16[256,1024]{1,0:T(8,128)(2,1)S(1)}, bf16[256,1024]{1,0:T(8,128)(2,1)S(1)}, u32[]{:S(2)}, u32[]{:S(2)}) %collective-permute-start.42) | collective-permute-done | bytes 524320 | tf_op jit(solution)/shard_map/ppermute | solution.py:21
  339.5 12.5 %collective-permute-done.46.refs_2_ = bf16[256,1024]{1,0:T(8,128)(2,1)S(1)} collective-permute-done((bf16[256,1024]{1,0:T(8,128)(2,1)S(1)}, bf16[256,1024]{1,0:T(8,128)(2,1)S(1)}, u32[]{:S(2)}, u32[]{:S(2)}) %collective-permute-start.46) | collective-permute-done | bytes 524320 | tf_op jit(solution)/shard_map/ppermute | solution.py:21
  372.8 22.9 %shard_map.231 = (bf16[1024,256]{1,0:T(8,128)(2,1)S(1)}, bf16[1024,256]{1,0:T(8,128)(2,1)S(1)}, bf16[1024,256]{1,0:T(8,128)(2,1)S(1)}, bf16[256,1024]{1,0:T(8,12...) custom-call(bf16[256,1024]{1,0:T(8,128)(2,1)} %copy-done.10, ...), custom_call_target="tpu_custom_call" | custom-call | flops 7516192768 | bytes 11034624 | tf_op jit(solution)/shard_map/pallas_call | solution.py:61
  400.7 12.5 %collective-permute-done.52.refs_2_ = bf16[256,1024]{1,0:T(8,128)(2,1)S(1)} collective-permute-done((bf16[256,1024]{1,0:T(8,128)(2,1)S(1)}, bf16[256,1024]{1,0:T(8,128)(2,1)S(1)}, u32[]{:S(2)}, u32[]{:S(2)}) %collective-permute-start.52) | collective-permute-done | bytes 524320 | tf_op jit(solution)/shard_map/ppermute | solution.py:21
  419.9 11.7 %collective-permute-done.54.refs_2_.refs_6_ = bf16[256,1024]{1,0:T(8,128)(2,1)S(1)} collective-permute-done((bf16[256,1024]{1,0:T(8,128)(2,1)S(1)}, bf16[256,1024]{1,0:T(8,128)(2,1)S(1)}, u32[]{:S(2)}, u32[]{:S(2)}) %collective-permute-start.54) | collective-permute-done | bytes 524320 | tf_op jit(solution)/shard_map/ppermute | solution.py:21
  452.4 12.5 %collective-permute-done.58.refs_2_ = bf16[256,1024]{1,0:T(8,128)(2,1)S(1)} collective-permute-done((bf16[256,1024]{1,0:T(8,128)(2,1)S(1)}, bf16[256,1024]{1,0:T(8,128)(2,1)S(1)}, u32[]{:S(2)}, u32[]{:S(2)}) %collective-permute-start.58) | collective-permute-done | bytes 524320 | tf_op jit(solution)/shard_map/ppermute | solution.py:21
  474.5 8.7 %collective-permute-done.60.refs_2_ = bf16[256,1024]{1,0:T(8,128)(2,1)} collective-permute-done((bf16[256,1024]{1,0:T(8,128)(2,1)S(1)}, bf16[256,1024]{1,0:T(8,128)(2,1)}, u32[]{:S(2)}, u32[]{:S(2)}) %collective-permute-start.60) | collective-permute-done | bytes 524320 | tf_op jit(solution)/shard_map/ppermute | solution.py:21
  505.9 8.0 %concatenate.63 = bf16[4,776,256]{2,1,0:T(8,128)(2,1)} concatenate(bf16[4,768,256]{2,1,0:T(8,128)(2,1)} %get-tuple-element.188, bf16[4,1,256]{2,1,0:T(2,128)(2,1)S(1)} %pad.62, bf16[4,1,256]{2,1,0:T(2,128)(2,1)S(1)} %pad.63, bf16[4,1,256]{2,1,0:T(2,128)(2,1)S(1)} %pad.64, bf16[4,1,256]{2,1,0:T(2,128)(2,1)S(1)} %bitcast.221, bf16[4,1,256]{2,1,0:T(2,128)(2,1)S(1)} %pad.65, ...), dimensions={1} | concatenate | bytes 3178496 | tf_op jit(solution)/shard_map/concatenate | solution.py:770
  521.2 22.9 %shard_map.235 = (bf16[1024,256]{1,0:T(8,128)(2,1)S(1)}, bf16[1024,256]{1,0:T(8,128)(2,1)S(1)}, bf16[1024,256]{1,0:T(8,128)(2,1)S(1)}, bf16[256,1024]{1,0:T(8,12...) custom-call(bf16[256,1024]{1,0:T(8,128)(2,1)} %copy-done.9, ...), custom_call_target="tpu_custom_call" | custom-call | flops 7516192768 | bytes 11034624 | tf_op jit(solution)/shard_map/pallas_call | solution.py:61
  557.9 8.0 %concatenate.62 = bf16[4,776,256]{2,1,0:T(8,128)(2,1)} concatenate(bf16[4,768,256]{2,1,0:T(8,128)(2,1)} %get-tuple-element.177, bf16[4,1,256]{2,1,0:T(2,128)(2,1)S(1)} %pad.58, bf16[4,1,256]{2,1,0:T(2,128)(2,1)S(1)} %pad.59, bf16[4,1,256]{2,1,0:T(2,128)(2,1)S(1)} %pad.60, bf16[4,1,256]{2,1,0:T(2,128)(2,1)S(1)} %bitcast.219, bf16[4,1,256]{2,1,0:T(2,128)(2,1)S(1)} %pad.61, ...), dimensions={1} | concatenate | bytes 3178496 | tf_op jit(solution)/shard_map/concatenate | solution.py:770
  601.3 8.9 %collective-permute-done.69 = bf16[256,256]{1,0:T(8,128)(2,1)S(1)} collective-permute-done((bf16[256,256]{1,0:T(8,128)(2,1)}, bf16[256,256]{1,0:T(8,128)(2,1)S(1)}, u32[]{:S(2)}, u32[]{:S(2)}) %collective-permute-start.69) | collective-permute-done | bytes 131104 | tf_op jit(solution)/shard_map/ppermute | solution.py:777
  (573 shorter events, 341.9 us)
Async XLA Ops:
  7.2 98.6 %all-gather.15.cloned.1.call-start = ((), (), s32[]{:S(2)}) async-start(), calls=%async_computation.16 | async-start | bytes 1986560 | tf_op jit(solution)/shard_map/all_gather | solution.py:55
  15.6 44.6 %collective-permute-start = (bf16[256,1024]{1,0:T(8,128)(2,1)}, bf16[256,1024]{1,0:T(8,128)(2,1)}, u32[]{:S(2)}, u32[]{:S(2)}) collective-permute-start(bf16[256,1024]{1,0:T(8,128)(2,1)} %dynamic-slice_bitcast_fusion), channel_id=1, source_target_pairs={{0,16},{16,0},{1,17},{17,1},{2,18},{18,2},{3,19},{19,3},{4,20},{20... | collective-permute-start | bytes 1572872 | tf_op jit(solution)/shard_map/ppermute | solution.py:21
  22.5 35.3 %collective-permute-start.14 = (bf16[776,256]{1,0:T(8,128)(2,1)}, bf16[776,256]{1,0:T(8,128)(2,1)}, u32[]{:S(2)}, u32[]{:S(2)}) collective-permute-start(bf16[776,256]{1,0:T(8,128)(2,1)} %concatenate.61), channel_id=1, source_target_pairs={{0,16},{16,0},{1,17},{17,1},{2,18},{18,2},{3,19},{19,3},{4,20},{20... | collective-permute-start | bytes 1191944 | tf_op jit(solution)/shard_map/ppermute | solution.py:21
  60.0 106.7 %all-gather.17.cloned.1.call-start = ((), (), s32[]{:S(2)}) async-start(), calls=%async_computation.17 | async-start | bytes 1310720 | tf_op jit(solution)/shard_map/all_gather | solution.py:55
  69.6 97.2 %all-gather.19.cloned.1.call-start = ((), (), s32[]{:S(2)}) async-start(), calls=%async_computation.18 | async-start | bytes 1310720 | tf_op jit(solution)/shard_map/all_gather | solution.py:55
  69.6 37.0 %collective-permute-start.11 = (bf16[256,1024]{1,0:T(8,128)(2,1)S(1)}, bf16[256,1024]{1,0:T(8,128)(2,1)S(1)}, u32[]{:S(2)}, u32[]{:S(2)}) collective-permute-start(bf16[256,1024]{1,0:T(8,128)(2,1)S(1)} %shard_map.220.refs_0_), channel_id=1, source_target_pairs={{0,4},{4,0},{8,12},{12,8},{1,5},{5,1},{9,13},{13,9},{2,6},{6,2},{1... | collective-permute-start | bytes 1572872 | tf_op jit(solution)/shard_map/ppermute | solution.py:21
  77.4 29.2 %collective-permute-start.13 = (bf16[256,1024]{1,0:T(8,128)(2,1)S(1)}, bf16[256,1024]{1,0:T(8,128)(2,1)S(1)}, u32[]{:S(2)}, u32[]{:S(2)}) collective-permute-start(bf16[256,1024]{1,0:T(8,128)(2,1)S(1)} %collective-permute-done.12.refs_2_), channel_id=1, source_target_pairs={{0,4},{4,0},{8,12},{12,8},{1,5},{5,1},{9,13},{13,9},{2,6},{6,2},{1... | collective-permute-start | bytes 1572872 | tf_op jit(solution)/shard_map/ppermute | solution.py:21
  133.4 93.6 %all-gather.21.cloned.1.call-start = ((), (), s32[]{:S(2)}) async-start(), calls=%async_computation.19 | async-start | bytes 1986560 | tf_op jit(solution)/shard_map/all_gather | solution.py:55
  166.4 115.4 %all-gather.23.cloned.1.call-start = ((), (), s32[]{:S(2)}) async-start(), calls=%async_computation.20 | async-start | bytes 1310720 | tf_op jit(solution)/shard_map/all_gather | solution.py:55
  198.3 29.7 %collective-permute-start.27 = (bf16[256,1024]{1,0:T(8,128)(2,1)}, bf16[256,1024]{1,0:T(8,128)(2,1)S(1)}, u32[]{:S(2)}, u32[]{:S(2)}) collective-permute-start(bf16[256,1024]{1,0:T(8,128)(2,1)} %get-tuple-element.124.refs_0_), channel_id=1, source_target_pairs={{0,4},{4,0},{8,12},{12,8},{1,5},{5,1},{9,13},{13,9},{2,6},{6,2},{1... | collective-permute-start | bytes 1572872 | tf_op jit(solution)/shard_map/ppermute | solution.py:21
  227.0 55.6 %all-gather.25.cloned.1.call-start = ((), (), s32[]{:S(2)}) async-start(), calls=%async_computation.21 | async-start | bytes 1310720 | tf_op jit(solution)/shard_map/all_gather | solution.py:55
  251.4 265.1 %reduce-scatter.23.cloned.1.call-start = ((), (), s32[]{:S(2)}) async-start(), calls=%async_computation.15 | async-start | bytes 1310720 | tf_op jit(solution)/shard_map/reduce_scatter | solution.py:765
  364.9 153.6 %reduce-scatter.19.cloned.1.call-start = ((), (), s32[]{:S(2)}) async-start(), calls=%async_computation.13 | async-start | bytes 1310720 | tf_op jit(solution)/shard_map/reduce_scatter | solution.py:765
  395.9 151.8 %reduce-scatter.21.cloned.1.call-start = ((), (), s32[]{:S(2)}) async-start(), calls=%async_computation.14 | async-start | bytes 1310720 | tf_op jit(solution)/shard_map/reduce_scatter | solution.py:765
  447.8 128.0 %reduce-scatter.17.cloned.1.call-start = ((), (), s32[]{:S(2)}) async-start(), calls=%async_computation.12 | async-start | bytes 1310720 | tf_op jit(solution)/shard_map/reduce_scatter | solution.py:765
  448.4 141.2 %reduce-scatter.15.cloned.1.call-start = ((), (), s32[]{:S(2)}) async-start(), calls=%async_computation.11 | async-start | bytes 655360 | tf_op jit(solution)/shard_map/reduce_scatter | solution.py:765
  474.4 118.2 %reduce-scatter.13.cloned.1.call-start = ((), (), s32[]{:S(2)}) async-start(), calls=%async_computation.10 | async-start | bytes 655360 | tf_op jit(solution)/shard_map/reduce_scatter | solution.py:765
  489.2 127.3 %reduce-scatter.11.cloned.1.call-start = ((), (), s32[]{:S(2)}) async-start(), calls=%async_computation.9 | async-start | bytes 1986560 | tf_op jit(solution)/shard_map/reduce_scatter | solution.py:765
  514.0 133.8 %reduce-scatter.9.cloned.1.call-start = ((), (), s32[]{:S(2)}) async-start(), calls=%async_computation.8 | async-start | bytes 1986560 | tf_op jit(solution)/shard_map/reduce_scatter | solution.py:765
  516.5 49.5 %collective-permute-start.74 = (bf16[512,256]{1,0:T(8,128)(2,1)}, bf16[512,256]{1,0:T(8,128)(2,1)}, u32[]{:S(2)}, u32[]{:S(2)}) collective-permute-start(bf16[512,256]{1,0:T(8,128)(2,1)} %bitcast.201), channel_id=1, source_target_pairs={{0,16},{1,17},{2,18},{3,19},{4,20},{5,21},{6,22},{7,23},{8,24},{9,... | collective-permute-start | bytes 786440 | tf_op jit(solution)/shard_map/ppermute | solution.py:776
  518.5 61.5 %collective-permute-start.72 = (bf16[256,512]{1,0:T(8,128)(2,1)}, bf16[256,512]{1,0:T(8,128)(2,1)}, u32[]{:S(2)}, u32[]{:S(2)}) collective-permute-start(bf16[256,512]{1,0:T(8,128)(2,1)} %bitcast.200), channel_id=1, source_target_pairs={{0,16},{1,17},{2,18},{3,19},{4,20},{5,21},{6,22},{7,23},{8,24},{9,... | collective-permute-start | bytes 786440 | tf_op jit(solution)/shard_map/ppermute | solution.py:776
  567.0 82.0 %collective-permute-start.65 = (bf16[256,1024]{1,0:T(8,128)(2,1)S(1)}, bf16[256,1024]{1,0:T(8,128)(2,1)}, u32[]{:S(2)}, u32[]{:S(2)}) collective-permute-start(bf16[256,1024]{1,0:T(8,128)(2,1)S(1)} %copy-done.6), channel_id=1, source_target_pairs={{0,16},{1,17},{2,18},{3,19},{4,20},{5,21},{6,22},{7,23},{8,24},{9,... | collective-permute-start | bytes 1572872 | tf_op jit(solution)/shard_map/ppermute | solution.py:786
  591.2 57.8 %collective-permute-start.66 = (bf16[256,1024]{1,0:T(8,128)(2,1)S(1)}, bf16[256,1024]{1,0:T(8,128)(2,1)}, u32[]{:S(2)}, u32[]{:S(2)}) collective-permute-start(bf16[256,1024]{1,0:T(8,128)(2,1)S(1)} %get-tuple-element.173), channel_id=1, source_target_pairs={{16,0},{17,1},{18,2},{19,3},{20,4},{21,5},{22,6},{23,7},{24,8},{25... | collective-permute-start | bytes 1572872 | tf_op jit(solution)/shard_map/ppermute | solution.py:786
  619.2 45.9 %collective-permute-start.68 = (bf16[776,256]{1,0:T(8,128)(2,1)}, bf16[776,256]{1,0:T(8,128)(2,1)}, u32[]{:S(2)}, u32[]{:S(2)}) collective-permute-start(bf16[776,256]{1,0:T(8,128)(2,1)} %bitcast.192), channel_id=1, source_target_pairs={{0,16},{1,17},{2,18},{3,19},{4,20},{5,21},{6,22},{7,23},{8,24},{9,... | collective-permute-start | bytes 1191944 | tf_op jit(solution)/shard_map/ppermute | solution.py:776
  (182 other events, 1652.2 us)
Sparse Core Ops, SparseCore 0:
  60.1 45.6 all-gather.14
  107.4 26.8 all-gather.16
  135.8 27.4 all-gather.18
  166.6 36.3 all-gather.20
  227.1 26.6 all-gather.22
  255.2 27.3 all-gather.24
  365.1 24.9 reduce-scatter.22
  396.0 25.8 reduce-scatter.18
  447.9 25.8 reduce-scatter.20
  476.1 25.9 reduce-scatter.16
  504.3 20.2 reduce-scatter.14
  526.8 19.9 reduce-scatter.12
  549.6 34.0 reduce-scatter.10
  585.8 37.8 reduce-scatter.8

commit v2 on v1

v2 whole, which is shorter than its diff:
```python
import functools
import math

import jax
import jax.numpy as jnp
from jax import lax
from jax.experimental import pallas as pl
from jax.experimental.pallas import tpu as pltpu
from jax.sharding import PartitionSpec as P

HEAD_DIM = 64
SLOT_ROWS = 8
norm_eps = 1e-06
big_negative = -1e30
f32 = jnp.float32
bf16 = jnp.bfloat16
vmem_limit = 52 * 1024 * 1024


def swap(block, axis, bit):
    return lax.ppermute(block, axis, [(i, i ^ bit) for i in range(lax.axis_size(axis))])


def after(value, *others):
    return lax.optimization_barrier((value, *others))[0]


def bits_of(count):
    bit = 1
    while bit < count:
        yield bit
        bit *= 2


def gather_near(block):
    blocks = {0: block}
    for bit in reversed(list(bits_of(lax.axis_size("tensor") // 2))):
        blocks.update({j | bit: swap(part, "tensor", bit) for j, part in list(blocks.items())})
    return [blocks[j] for j in range(len(blocks))]


def cross(block):
    return swap(block, "tensor", lax.axis_size("tensor") // 2)


def gather_rows(block):
    far = cross(block)
    return gather_near(block) + gather_near(far)


def reduce_rows(parts, bits):
    kept = dict(enumerate(parts))
    addends = [parts[0]]
    for bit in bits:
        arrived = {j: swap(kept[j | bit], "tensor", bit) for j in kept if not j & bit}
        addends.append(arrived.pop(0))
        kept = {
            0: parts[0],
            **{
                j: (kept[j].astype(f32) + part.astype(f32)).astype(parts[0].dtype)
                for j, part in arrived.items()
            },
        }
    return addends


def near_sum(parts):
    near = reduce_rows(parts, list(bits_of(len(parts))))
    summed = functools.reduce(jnp.add, [part.astype(f32) for part in near])
    return summed.astype(parts[0].dtype)


def scatter_near(parts):
    return reduce_rows(parts, list(bits_of(len(parts))))


def absolute(blocks, index):
    for bit in bits_of(len(blocks)):
        blocks = [
            jnp.where(index & bit, blocks[b ^ bit], blocks[b]) for b in range(len(blocks))
        ]
    return blocks


def gather_groups(block):
    return lax.all_gather(block, "dp", axis=0, tiled=False)


def tie(*values):
    return lax.optimization_barrier(values)


class Half:
    def __init__(self, array, index):
        self.array, self.index = array, index


def spec_of(arg):
    if isinstance(arg, Half):
        dims = arg.array.shape
        place = (arg.index,) + (0,) * (len(dims) - 1)
        return pl.BlockSpec((dims[0] // 2, *dims[1:]), lambda i: place)
    return pl.BlockSpec(memory_space=pltpu.VMEM)


def call(name, body, outs, *args, scratch=(), flops=0):
    whole = pl.BlockSpec(memory_space=pltpu.VMEM)
    grid = {"grid": (1,)} if any(isinstance(arg, Half) for arg in args) else {}
    return pl.pallas_call(
        body,
        in_specs=[spec_of(arg) for arg in args],
        out_specs=(whole,) * len(outs),
        **grid,
        out_shape=tuple(outs),
        name=name,
        scratch_shapes=scratch,
        compiler_params=pltpu.CompilerParams(vmem_limit_bytes=vmem_limit),
        cost_estimate=pl.CostEstimate(flops=flops, bytes_accessed=0, transcendentals=0),
    )(*[arg.array if isinstance(arg, Half) else arg for arg in args])


def shape(dims, dtype):
    return jax.ShapeDtypeStruct(dims, dtype)


def mm(left, right):
    return lax.dot_general(left, right, (((1,), (0,)), ((), ())), preferred_element_type=f32)


def mm_last(left, right):
    return lax.dot_general(left, right, (((1,), (1,)), ((), ())), preferred_element_type=f32)


def mm_first(left, right):
    return lax.dot_general(left, right, (((0,), (0,)), ((), ())), preferred_element_type=f32)


def slot_pick(seg_col):
    rows = seg_col.shape[0]
    lane = lax.broadcasted_iota(jnp.int32, (rows, SLOT_ROWS), 1)
    return (lane == seg_col).astype(f32).astype(bf16)


def part_of(picked, mod_ref, index, width):
    values = mod_ref[:, index * width : (index + 1) * width]
    high = values.astype(bf16)
    rest = (values - high.astype(f32)).astype(bf16)
    return mm(picked, high) + mm(picked, rest)


def slot_sums(seg_row, slots, values):
    row = lax.broadcasted_iota(jnp.int32, (SLOT_ROWS, seg_row.shape[1]), 0)
    picked = ((row == seg_row) & (row < slots)).astype(f32).astype(bf16)
    return mm(picked, values.astype(bf16))


def normed(values):
    centre = values - jnp.mean(values, axis=-1, keepdims=True)
    spread = jnp.mean(centre * centre, axis=-1, keepdims=True)
    inverse = lax.rsqrt(spread + norm_eps)
    return centre * inverse, inverse


def norm_back(norm, inverse, d_norm):
    mean_d = jnp.mean(d_norm, axis=-1, keepdims=True)
    mean_dn = jnp.mean(d_norm * norm, axis=-1, keepdims=True)
    return inverse * (d_norm - mean_d - norm * mean_dn)


def total(refs):
    value = refs[0][...].astype(f32)
    for ref in refs[1:]:
        value = value + ref[...].astype(f32)
    return value


def first_norm_kernel(width, blocks, *refs):
    seg_ref, mod_ref = refs[blocks : blocks + 2]
    rows = refs[0].shape[0]
    for j in range(blocks):
        picked = slot_pick(seg_ref[j * rows : (j + 1) * rows, :])
        norm, _ = normed(refs[j][...].astype(f32))
        scale = part_of(picked, mod_ref, 1, width)
        shift = part_of(picked, mod_ref, 0, width)
        refs[blocks + 2 + j][...] = (norm * (1.0 + scale) + shift).astype(bf16)


def middle_kernel(width, terms, *refs):
    sums = refs[:terms]
    h_ref, bias_ref, seg_ref, mod_ref, z1_ref, h1_ref, a2_ref = refs[terms:]
    picked = slot_pick(seg_ref[...])
    z1 = total(sums) + bias_ref[...]
    z1_ref[...] = z1.astype(bf16)
    h1 = h_ref[...].astype(f32) + part_of(picked, mod_ref, 2, width) * z1
    h1_ref[...] = h1
    norm, _ = normed(h1)
    a2_ref[...] = (
        norm * (1.0 + part_of(picked, mod_ref, 4, width)) + part_of(picked, mod_ref, 3, width)
    ).astype(bf16)


def layer_end_kernel(width, terms, *refs):
    sums = refs[:terms]
    h1_ref, bias_ref, seg_ref, mod_ref, next_ref, z2_ref, y_ref, a1_ref = refs[terms:]
    picked = slot_pick(seg_ref[...])
    z2 = total(sums) + bias_ref[...]
    z2_ref[...] = z2.astype(bf16)
    y = (h1_ref[...] + part_of(picked, mod_ref, 5, width) * z2).astype(bf16)
    y_ref[...] = y
    norm, _ = normed(y.astype(f32))
    a1_ref[...] = (
        norm * (1.0 + part_of(picked, next_ref, 1, width)) + part_of(picked, next_ref, 0, width)
    ).astype(bf16)


def column_sums(values):
    return mm(jnp.ones((SLOT_ROWS, values.shape[0]), bf16), values)


def branch_back(width, slots, grad, z2, picked, seg_row, mod_ref, dz2_ref, dgate_ref, bias_ref):
    dz2 = (grad * part_of(picked, mod_ref, 5, width)).astype(bf16)
    dz2_ref[...] = dz2
    dgate_ref[...] = slot_sums(seg_row, slots, grad * z2)
    bias_ref[...] = column_sums(dz2)


def turn_kernel(width, slots, terms, *refs):
    sums = refs[:terms]
    (h1_ref, bias_ref, seg_ref, seg_row_ref, mod_ref, cot_ref) = refs[terms : terms + 6]
    y_ref, c_ref = refs[terms + 6 : terms + 8]
    seg = seg_ref[...]
    picked = slot_pick(seg)
    z2 = total(sums) + bias_ref[...]
    y_ref[...] = (h1_ref[...] + part_of(picked, mod_ref, 5, width) * z2).astype(bf16)
    grad = jnp.where(seg < slots, cot_ref[...].astype(f32), 0.0)
    c_ref[...] = grad.astype(bf16)
    branch_back(width, slots, grad, z2, picked, seg_row_ref[...], mod_ref, *refs[terms + 8 :])


def middle_back_kernel(width, slots, terms, *refs):
    sums = refs[:terms]
    h1_ref, c_ref, z1_ref, seg_ref, seg_row_ref, mod_ref = refs[terms : terms + 6]
    dh1_ref, dz1_ref, d_mod_ref, bias_ref = refs[terms + 6 :]
    picked = slot_pick(seg_ref[...])
    seg_row = seg_row_ref[...]
    da2 = total(sums)
    norm, inverse = normed(h1_ref[...])
    d_mod_ref[:, width : 2 * width] = slot_sums(seg_row, slots, da2)
    d_mod_ref[:, 2 * width :] = slot_sums(seg_row, slots, da2 * norm)
    d_norm = da2 * (1.0 + part_of(picked, mod_ref, 4, width))
    dh1 = c_ref[...].astype(f32) + norm_back(norm, inverse, d_norm)
    dh1_ref[...] = dh1
    dz1 = (dh1 * part_of(picked, mod_ref, 2, width)).astype(bf16)
    dz1_ref[...] = dz1
    d_mod_ref[:, :width] = slot_sums(seg_row, slots, dh1 * z1_ref[...].astype(f32))
    bias_ref[...] = column_sums(dz1)


def layer_back_kernel(width, slots, terms, more, *refs):
    sums = refs[:terms]
    h_ref, dh1_ref, seg_ref, seg_row_ref, mod_ref = refs[terms : terms + 5]
    rest = refs[terms + 5 :]
    if more:
        z2_ref, before_ref = rest[:2]
        rest = rest[2:]
    g_ref, d_mod_ref = rest[:2]
    picked = slot_pick(seg_ref[...])
    seg_row = seg_row_ref[...]
    da1 = total(sums)
    norm, inverse = normed(h_ref[...].astype(f32))
    d_mod_ref[:, :width] = slot_sums(seg_row, slots, da1)
    d_mod_ref[:, width:] = slot_sums(seg_row, slots, da1 * norm)
    d_norm = da1 * (1.0 + part_of(picked, mod_ref, 1, width))
    grad = (dh1_ref[...] + norm_back(norm, inverse, d_norm)).astype(bf16)
    g_ref[...] = grad
    if more:
        branch_back(
            width,
            slots,
            grad.astype(f32),
            z2_ref[...].astype(f32),
            picked,
            seg_row,
            before_ref,
            *rest[2:],
        )


def turned(values, cos, sin):
    groups = []
    for start in range(0, values.shape[1], 128):
        part = values[:, start : start + 128]
        lane = lax.broadcasted_iota(jnp.int32, part.shape, 1)
        other = jnp.where(lane % 2 == 0, pltpu.roll(part, 127, 1), pltpu.roll(part, 1, 1))
        groups.append(part * cos + other * sin)
    return groups[0] if len(groups) == 1 else jnp.concatenate(groups, axis=1)


def head_mask(lane, head):
    return (lane >= head * HEAD_DIM) & (lane < (head + 1) * HEAD_DIM)


class Attention:
    def __init__(self, refs, width):
        self.refs, self.width = refs, width
        self.groups, _, self.local = refs[0].shape
        self.depth = width // self.groups
        self.offset = 3 * self.depth if len(refs) == 1 else 0

    def project(self, p):
        part = self.refs[0][:, p * self.depth : (p + 1) * self.depth, :]
        return part.reshape(self.width, self.local)

    def out(self, g):
        return self.refs[-1][g, self.offset : self.offset + self.local, :]


class Feed:
    def __init__(self, refs, width, units):
        self.refs, self.width, self.units = refs, width, units
        self.groups, _, lanes = refs[0].shape
        self.depth = width // self.groups
        self.chunks = units // lanes
        self.offset = self.chunks * self.depth if len(refs) == 1 else 0

    def up(self):
        parts = [
            self.refs[0][:, i * self.depth : (i + 1) * self.depth, :].reshape(self.width, -1)
            for i in range(self.chunks)
        ]
        return parts

    def down(self, g):
        return self.refs[-1][g, self.offset : self.offset + self.units, :]


def qkv_of(x, weights, bias_ref, cos, sin):
    q = turned(mm(x, weights[0]) + bias_ref[0:1, :], cos, sin).astype(bf16)
    k = turned(mm(x, weights[1]) + bias_ref[1:2, :], cos, sin).astype(bf16)
    v = (mm(x, weights[2]) + bias_ref[2:3, :]).astype(bf16)
    return (q.astype(f32) * (HEAD_DIM**-0.5)).astype(bf16), k, v


def attend_rows(q, allowed, k_ref, v_ref):
    rows, local = q.shape
    lane = lax.broadcasted_iota(jnp.int32, (rows, local), 1)
    wide_lane = lax.broadcasted_iota(jnp.int32, (rows, 128), 1)
    mixed = jnp.zeros((rows, local), f32)
    lse = jnp.zeros((rows, 128), f32)
    for head in range(local // HEAD_DIM):
        mine = head_mask(lane, head)
        scores = mm_last(jnp.where(mine, q, jnp.zeros_like(q)), k_ref[...])
        scores = jnp.where(allowed, scores, big_negative)
        top = jnp.max(scores, axis=-1, keepdims=True)
        weight = jnp.exp(scores - top)
        weight_sum = jnp.sum(weight, axis=-1, keepdims=True)
        mixed = jnp.where(mine, mm(weight.astype(bf16), v_ref[...]) / weight_sum, mixed)
        lse = jnp.where(wide_lane == head, top + jnp.log(weight_sum), lse)
    return mixed.astype(bf16), lse


def project_kernel(blocks, parts, *refs):
    x_refs = refs[:blocks]
    weights = Attention(refs[blocks : blocks + parts], x_refs[0].shape[1])
    bias_ref, cos_ref, sin_ref, q_ref, k_ref, v_ref = refs[blocks + parts :]
    rows = x_refs[0].shape[0]
    mats = [weights.project(p) for p in range(3)]
    for j in range(blocks):
        here = slice(j * rows, (j + 1) * rows)
        q, k, v = qkv_of(x_refs[j][...], mats, bias_ref, cos_ref[here, :], sin_ref[here, :])
        q_ref[here, :] = q
        k_ref[here, :] = k
        v_ref[here, :] = v


def attend_far_kernel(blocks, parts, *refs):
    x_refs = refs[:blocks]
    rows, width = x_refs[0].shape
    weights = Attention(refs[blocks : blocks + parts], width)
    (
        bias_ref,
        cos_ref,
        sin_ref,
        seg_ref,
        seg_row_ref,
        near_k_ref,
        near_v_ref,
        q_ref,
        k_ref,
        v_ref,
        o_ref,
        lse_ref,
    ) = refs[blocks + parts : blocks + parts + 12]
    part_refs = refs[blocks + parts + 12 :]
    half = rows * blocks
    mats = [weights.project(p) for p in range(3)]
    k_ref[:half, :] = near_k_ref[...]
    v_ref[:half, :] = near_v_ref[...]
    for j in range(blocks):
        here = slice(j * rows, (j + 1) * rows)
        there = slice(half + j * rows, half + (j + 1) * rows)
        q, k, v = qkv_of(x_refs[j][...], mats, bias_ref, cos_ref[there, :], sin_ref[there, :])
        q_ref[here, :] = q
        k_ref[there, :] = k
        v_ref[there, :] = v
    attend_blocks(blocks, half, weights, seg_ref, seg_row_ref, q_ref, k_ref, v_ref, o_ref, lse_ref, part_refs)


def attend_blocks(blocks, start, weights, seg_ref, seg_row_ref, q_ref, k_ref, v_ref, o_ref, lse_ref, part_refs):
    rows = q_ref.shape[0] // blocks
    for j in reversed(range(blocks)):
        here = slice(j * rows, (j + 1) * rows)
        there = slice(start + j * rows, start + (j + 1) * rows)
        allowed = seg_ref[there, :] == seg_row_ref[...]
        mixed, lse = attend_rows(q_ref[here, :], allowed, k_ref, v_ref)
        o_ref[here, :] = mixed
        lse_ref[here, :] = lse
        for g in range(weights.groups):
            columns = slice(g * weights.depth, (g + 1) * weights.depth)
            part_refs[j][:, columns] = mm(mixed, weights.out(g)).astype(bf16)


def attend_near_kernel(blocks, parts, width, *refs):
    weights = Attention(refs[:parts], width)
    seg_ref, seg_row_ref, q_ref, k_ref, v_ref, o_ref, lse_ref = refs[parts : parts + 7]
    attend_blocks(
        blocks, 0, weights, seg_ref, seg_row_ref, q_ref, k_ref, v_ref, o_ref, lse_ref, refs[parts + 7 :]
    )


def input_terms(weights, dq, dk, dv):
    return (
        mm_last(dq, weights.project(0))
        + mm_last(dk, weights.project(1))
        + mm_last(dv, weights.project(2))
    ).astype(bf16)


def attend_back_kernel(blocks, parts, *refs):
    dz_refs = refs[:blocks]
    rows, width = dz_refs[0].shape
    weights = Attention(refs[blocks : blocks + parts], width)
    (
        near_q_ref,
        far_q_ref,
        k_ref,
        v_ref,
        near_lse_ref,
        far_lse_ref,
        cos_ref,
        sin_ref,
        seg_ref,
        seg_row_ref,
        dq_ref,
        dk_ref,
        dv_ref,
    ) = refs[blocks + parts : blocks + parts + 13]
    part_refs = refs[blocks + parts + 13 : -3]
    do_ref, dk_sum, dv_sum = refs[-3:]
    local, depth = weights.local, weights.depth
    half = blocks // 2
    for j in range(blocks):
        value = jnp.zeros((rows, local), f32)
        for g in range(weights.groups):
            value = value + mm_last(dz_refs[j][:, g * depth : (g + 1) * depth], weights.out(g))
        do_ref[j * rows : (j + 1) * rows, :] = value.astype(bf16)
    dk_sum[...] = jnp.zeros_like(dk_sum)
    dv_sum[...] = jnp.zeros_like(dv_sum)

    def one_side(start, q_ref, lse_ref):
        def one_block(i, carry):
            here = pl.ds(pl.multiple_of(i * rows, rows), rows)
            there = pl.ds(pl.multiple_of(start + i * rows, rows), rows)
            q, do, lse = q_ref[here, :], do_ref[there, :], lse_ref[here, :]
            allowed = seg_ref[there, :] == seg_row_ref[...]
            lane = lax.broadcasted_iota(jnp.int32, (rows, local), 1)
            dq = jnp.zeros((rows, local), f32)
            for head in range(local // HEAD_DIM):
                mine = head_mask(lane, head)
                q_head = jnp.where(mine, q, jnp.zeros_like(q))
                do_head = jnp.where(mine, do, jnp.zeros_like(do))
                scores = mm_last(q_head, k_ref[...])
                prob = jnp.exp(jnp.where(allowed, scores, big_negative) - lse[:, head : head + 1])
                d_prob = mm_last(do_head, v_ref[...])
                product = prob * d_prob
                centre = jnp.sum(product, axis=-1, keepdims=True)
                d_scores = (product - prob * centre).astype(bf16)
                dv_sum[...] += mm_first(prob.astype(bf16), do_head)
                dk_sum[...] += mm_first(d_scores, q_head)
                dq = jnp.where(mine, mm(d_scores, k_ref[...]), dq)
            dq = turned(dq * (HEAD_DIM**-0.5), cos_ref[there, :], -sin_ref[there, :])
            dq_ref[there, :] = dq.astype(bf16)
            return carry

        lax.fori_loop(0, half, one_block, 0)

    one_side(0, near_q_ref, near_lse_ref)
    one_side(half * rows, far_q_ref, far_lse_ref)
    for j in reversed(range(blocks)):
        here = slice(j * rows, (j + 1) * rows)
        dk_ref[here, :] = turned(dk_sum[here, :], cos_ref[here, :], -sin_ref[here, :]).astype(bf16)
        dv_ref[here, :] = dv_sum[here, :].astype(bf16)
        if j >= half:
            part_refs[j - half][...] = input_terms(
                weights, dq_ref[here, :], dk_ref[here, :], dv_ref[here, :]
            )


def gelu_parts(u):
    root = math.sqrt(2.0 / math.pi)
    square = u * u
    th = jnp.tanh(root * u * (1.0 + 0.044715 * square))
    return root, square, th


def feed_kernel(blocks, parts, *refs):
    a_refs = refs[:blocks]
    rows, width = a_refs[0].shape
    bias_ref, u_ref, g_ref = refs[blocks + parts : blocks + parts + 3]
    weights = Feed(refs[blocks : blocks + parts], width, bias_ref.shape[1])
    part_refs = refs[blocks + parts + 3 :]
    depth = weights.depth
    ups = weights.up()
    lanes = ups[0].shape[1]
    for j in reversed(range(blocks)):
        here = slice(j * rows, (j + 1) * rows)
        for i, w_up in enumerate(ups):
            columns = slice(i * lanes, (i + 1) * lanes)
            u = mm(a_refs[j][...], w_up) + bias_ref[:, columns]
            u_ref[here, columns] = u
            _, _, th = gelu_parts(u)
            g_ref[here, columns] = (0.5 * u * (1.0 + th)).astype(bf16)
        for k in range(weights.groups):
            part_refs[j][:, k * depth : (k + 1) * depth] = mm(
                g_ref[here, :], weights.down(k)
            ).astype(bf16)


def feed_back_kernel(blocks, parts, *refs):
    dz_refs = refs[:blocks]
    rows, width = dz_refs[0].shape
    u_ref, du_ref = refs[blocks + parts : blocks + parts + 2]
    weights = Feed(refs[blocks : blocks + parts], width, u_ref.shape[1])
    part_refs = refs[blocks + parts + 2 :]
    depth = weights.depth
    ups = weights.up()
    lanes = ups[0].shape[1]
    for j in reversed(range(blocks)):
        here = slice(j * rows, (j + 1) * rows)
        dg = jnp.zeros((rows, weights.units), f32)
        for k in range(weights.groups):
            dg = dg + mm_last(dz_refs[j][:, k * depth : (k + 1) * depth], weights.down(k))
        u = u_ref[here, :]
        root, square, th = gelu_parts(u)
        slope = 0.5 * (1.0 + th) + 0.5 * u * (1.0 - th * th) * (root * (1.0 + 0.134145 * square))
        du = (dg * slope).astype(bf16)
        du_ref[here, :] = du
        part_refs[j][...] = sum(
            mm_last(du[:, i * lanes : (i + 1) * lanes], w_up) for i, w_up in enumerate(ups)
        ).astype(bf16)


def feed_grads_kernel(blocks, *refs):
    a_refs, dz_refs = refs[:blocks], refs[blocks : 2 * blocks]
    near_g_ref, far_g_ref, near_du_ref, far_du_ref = refs[2 * blocks : 2 * blocks + 4]
    outs = refs[2 * blocks + 4 : -1]
    bias_up_ref = refs[-1]
    width, units = a_refs[0].shape[1], near_g_ref.shape[1]
    groups, _, lanes = outs[0].shape
    depth = width // groups
    chunks = units // lanes
    offset = chunks * depth if len(outs) == 1 else 0
    dz = jnp.concatenate([ref[...] for ref in dz_refs], axis=0)
    a2 = jnp.concatenate([ref[...] for ref in a_refs], axis=0)
    g = jnp.concatenate([near_g_ref[...], far_g_ref[...]], axis=0)
    du = jnp.concatenate([near_du_ref[...], far_du_ref[...]], axis=0)
    for k in range(groups):
        here = slice(k * depth, (k + 1) * depth)
        outs[-1][k, offset : offset + units, :] = mm_first(g, dz[:, here]).astype(bf16)
        for i in range(chunks):
            outs[0][k, i * depth : (i + 1) * depth, :] = mm_first(
                a2[:, here], du[:, i * lanes : (i + 1) * lanes]
            ).astype(bf16)
    bias_up_ref[...] = column_sums(du)


def attention_grads_kernel(blocks, parts, *refs):
    a_refs, dz_refs = refs[:blocks], refs[blocks : 2 * blocks]
    rows, width = a_refs[0].shape
    weights = Attention(refs[2 * blocks : 2 * blocks + parts], width)
    rest = refs[2 * blocks + parts :]
    dq_ref, dk_ref, dv_ref, near_o_ref, far_o_ref = rest[:5]
    half = blocks // 2
    part_refs, outs, bias_ref = rest[5 : 5 + half], rest[5 + half : -1], rest[-1]
    depth, local = weights.depth, weights.local
    for j in reversed(range(half)):
        here = slice(j * rows, (j + 1) * rows)
        part_refs[j][...] = input_terms(
            weights, dq_ref[here, :], dk_ref[here, :], dv_ref[here, :]
        )
    dz = jnp.concatenate([ref[...] for ref in dz_refs], axis=0)
    a1 = jnp.concatenate([ref[...] for ref in a_refs], axis=0)
    o = jnp.concatenate([near_o_ref[...], far_o_ref[...]], axis=0)
    for p, ref in enumerate((dq_ref, dk_ref, dv_ref)):
        bias_ref[p] = column_sums(ref[...])
        for k in range(weights.groups):
            outs[0][k, p * depth : (p + 1) * depth, :] = mm_first(
                a1[:, k * depth : (k + 1) * depth], ref[...]
            ).astype(bf16)
    for k in range(weights.groups):
        outs[-1][k, weights.offset : weights.offset + local, :] = mm_first(
            o, dz[:, k * depth : (k + 1) * depth]
        ).astype(bf16)


def mod_grads_kernel(blocks, codes_ref, place_ref, *refs):
    out_ref = refs[-1]
    strip = refs[0].shape[1]
    for j in range(blocks):
        here = pl.ds(pl.multiple_of(place_ref[j] * strip, 128), strip)
        out_ref[:, here] = mm_first(codes_ref[...], refs[j][...])


def per_device(
    endpoints,
    lengths,
    timesteps,
    w_qkv,
    b_qkv,
    w_out,
    b_out,
    w_up,
    b_up,
    w_down,
    b_down,
    w_mod,
    b_mod,
):
    section = lax.axis_index("section")
    tensor = lax.axis_index("tensor")
    group = lax.axis_index("dp")
    tensors, groups = lax.axis_size("tensor"), lax.axis_size("dp")
    half = tensors // 2
    rows, width = endpoints.shape[3], endpoints.shape[4]
    slots = lengths.shape[2]
    frames = rows * tensors
    depth = width // groups
    local = w_qkv.shape[3]
    units = w_up.shape[2]
    mod_width = w_mod.shape[2]
    strip = mod_width // tensors
    first = section == 0
    terms = len(list(bits_of(tensors))) + 1
    packed = depth == local

    def pick(here, other):
        return jnp.where(first, here, other), jnp.where(first, other, here)

    def mine_of(array):
        return jnp.where(first, array[0], array[1])

    def others_of(array):
        return jnp.where(first, array[1], array[0])

    flat_qkv = w_qkv[0].reshape(3 * depth, local)
    packs = [jnp.concatenate([flat_qkv, w_out[0]], axis=0)] if packed else [flat_qkv, w_out[0]]
    wholes = [lax.all_gather(pack, ("section", "dp"), axis=0, tiled=False) for pack in packs]
    attention = [[Half(pack, layer) for pack in wholes] for layer in range(2)]
    steps = jnp.pad(timesteps[:, 0], ((0, 0), (0, SLOT_ROWS - slots)))
    steps = after(steps, *packs)
    all_steps = jnp.stack([steps] + [swap(steps, "dp", j) for j in range(1, groups)])
    taken = swap(others_of(endpoints[0, :, 0]), "section", 1)
    kept = mine_of(endpoints[0, :, 0])
    h0, cotangent = pick(kept, taken)
    h_all = gather_rows(h0)

    column = group * depth + jnp.arange(depth, dtype=jnp.int32)
    frequency = jnp.exp(
        (column % (width // 2)).astype(f32) * (-math.log(10000.0) / (width // 2 - 1))
    )
    angle = all_steps.astype(f32)[..., None] * frequency
    codes = jax.nn.silu(
        jnp.where(column < width // 2, jnp.sin(angle), jnp.cos(angle))
    ).astype(bf16)
    share = b_mod.shape[1]
    bias_all = jnp.where(
        jnp.arange(mod_width)[None] // share == group,
        jnp.concatenate([b_mod] * groups, axis=1),
        jnp.zeros((), bf16),
    )
    mod_part = jnp.dot(
        codes.reshape(-1, depth),
        lax.dynamic_slice_in_dim(w_mod[0], tensor * strip, strip, 1),
        preferred_element_type=f32,
    ) + lax.dynamic_slice_in_dim(bias_all, tensor * strip, strip, 1).astype(f32)
    bias_sizes = [local // groups] * 3 + [depth, units // groups, depth]
    bias_row = jnp.concatenate([b_qkv[:, p] for p in range(3)] + [b_out, b_up, b_down], axis=1)
    bias_row = jnp.pad(bias_row, ((0, 0), (0, strip - bias_row.shape[1]))).astype(f32)
    slot_row = jnp.arange(SLOT_ROWS)[:, None]
    mod_part = jnp.where(
        slot_row < slots, mod_part.reshape(groups, 2, SLOT_ROWS, strip), bias_row
    )
    own_layer, other_layer = [], []
    for j in range(groups):
        for across, terms_of in enumerate((own_layer, other_layer)):
            term = (others_of if across else mine_of)(mod_part[j])
            here = across * groups + j
            route = [(i, i ^ here) for i in range(2 * groups)]
            terms_of.append(lax.ppermute(term, ("section", "dp"), route) if here else term)

    def with_biases(parts):
        biases_of = jnp.stack([part[slots] for part in parts])
        return jnp.concatenate([functools.reduce(jnp.add, parts), biases_of], axis=0)

    layer_mods = jnp.stack(pick(with_biases(own_layer), with_biases(other_layer)))
    other_up = swap(after(w_up[0], layer_mods), "section", 1)
    other_down = swap(after(w_down[0], layer_mods), "section", 1)
    own_strip = layer_mods[:, :SLOT_ROWS]
    strips_all = [own_strip] + [swap(own_strip, "tensor", j) for j in range(1, tensors)]
    strips_all = absolute(strips_all, tensor)
    mod_all = jnp.where(slot_row < slots, jnp.concatenate(strips_all, axis=-1), 0.0)

    def biases(layer):
        rel = [layer_mods[layer, SLOT_ROWS + j].astype(f32) for j in range(groups)]
        full = jnp.stack(absolute(rel, group))
        pieces, start = [], 0
        for size in bias_sizes:
            pieces.append(full[:, start : start + size].reshape(1, groups * size))
            start += size
        qkv = jnp.concatenate(pieces[:3] + [jnp.zeros((SLOT_ROWS - 3, local), f32)], axis=0)
        return qkv, *pieces[3:]

    lengths_here = mine_of(lengths[:, 0])
    block_index = tensor ^ jnp.arange(tensors, dtype=jnp.int32)
    frame = (block_index[:, None] * rows + jnp.arange(rows, dtype=jnp.int32)).reshape(-1)
    ends = jnp.cumsum(lengths_here)
    segment = jnp.sum((frame[:, None] >= ends[None, :]).astype(jnp.int32), axis=1)
    member = segment[:, None] == jnp.arange(slots, dtype=jnp.int32)[None, :]
    begin = jnp.sum(jnp.where(member, (ends - lengths_here)[None, :], 0), axis=1)
    position = (frame - begin).astype(f32)
    lane = jnp.arange(128, dtype=jnp.int32) % HEAD_DIM
    inverse = jnp.exp((lane // 2).astype(f32) * (-2.0 * math.log(10000.0) / HEAD_DIM))
    angles = position[:, None] * inverse[None, :]
    cos_table = jnp.cos(angles)
    sin_table = jnp.sin(angles) * jnp.where(lane % 2 == 0, -1.0, 1.0)
    seg_col, seg_row = segment[:, None], segment[None, :]
    own_col, own_row = seg_col[:rows], seg_row[:, :rows]

    block = shape((rows, width), bf16)
    block32 = shape((rows, width), f32)
    half_local = shape((frames // 2, local), bf16)
    wide_local = shape((frames, local), bf16)
    half_lse = shape((frames // 2, 128), f32)
    slot_block = shape((SLOT_ROWS, width), f32)
    project = 2 * frames * width * local
    scores = 2 * frames * frames * max(local, 256)

    a1_all = call(
        "first_norm",
        functools.partial(first_norm_kernel, width, tensors),
        [block] * tensors,
        *h_all,
        seg_col,
        mod_all[0],
    )
    a1_near, a1_far = list(a1_all[:half]), a1_all[half:]


    def feed_packs(layer, layer_up, layer_down):
        if packed:
            chunks = [layer_up[layer][:, i : i + local] for i in range(0, units, local)]
            return [jnp.concatenate([*chunks, layer_down[layer]], axis=0)]
        return [layer_up[layer], layer_down[layer]]

    other_up, other_down, a1_near[0] = tie(other_up, other_down, a1_near[0])
    pairs = pick(w_up[0], other_up), pick(w_down[0], other_down)
    feed = [[gather_groups(pack) for pack in feed_packs(layer, *pairs)] for layer in range(2)]

    layer_in = h0
    saved = []
    outputs = []
    for layer in range(2):
        mods = mod_all[layer]
        bias_qkv, bias_out, bias_up, bias_down = biases(layer)
        w_att = attention[layer]
        near_q, near_k, near_v = call(
            "project_near",
            functools.partial(project_kernel, half, len(w_att)),
            [half_local] * 3,
            *a1_near,
            *w_att,
            bias_qkv,
            cos_table,
            sin_table,
            flops=3 * project // 2,
        )
        a1_all = a1_near + (
            gather_near(after(a1_far, near_k)) if layer else list(a1_far)
        )
        far_q, k, v, far_o, far_lse, *parts = call(
            "attend_far",
            functools.partial(attend_far_kernel, half, len(w_att)),
            [half_local, wide_local, wide_local, half_local, half_lse] + [block] * half,
            *a1_all[half:],
            *w_att,
            bias_qkv,
            cos_table,
            sin_table,
            seg_col,
            seg_row,
            near_k,
            near_v,
        )
        summed, near_q = tie(near_sum(parts), near_q)
        far = cross(summed)
        near_o, near_lse, *parts = call(
            "attend_near",
            functools.partial(attend_near_kernel, half, len(w_att), width),
            [half_local, half_lse] + [block] * half,
            *w_att,
            seg_col,
            seg_row,
            near_q,
            k,
            v,
            flops=project // 2 + scores,
        )
        far = after(far, near_o)
        z1, h1, a2 = call(
            "middle",
            functools.partial(middle_kernel, width, terms),
            [block, block32, block],
            *scatter_near(parts),
            far,
            layer_in,
            bias_out,
            own_col,
            mods,
        )
        w_feed = feed[layer]
        a2_near, a2_far = gather_near(a2), cross(a2)

        def feed_half(blocks_of):
            return call(
                "feed",
                functools.partial(feed_kernel, half, len(w_feed)),
                [shape((frames // 2, units), f32), shape((frames // 2, units), bf16)]
                + [block] * half,
                *blocks_of,
                *w_feed,
                bias_up,
                flops=2 * frames * width * units,
            )

        near_u, near_g, *near_parts = feed_half(a2_near)
        a2_all = a2_near + gather_near(after(a2_far, near_u))
        far_u, far_g, *far_parts = feed_half(a2_all[half:])
        sums = [*scatter_near(near_parts), cross(near_sum(far_parts))]
        kept_state = (layer_in, a1_all, near_q, far_q, k, v, near_o, far_o, near_lse, far_lse)
        kept_state += (z1, h1, a2_all, near_u, far_u, near_g, far_g)
        if layer == 0:
            z2, y, a1 = call(
                "layer_end",
                functools.partial(layer_end_kernel, width, terms),
                [block] * 3,
                *sums,
                h1,
                bias_down,
                own_col,
                mods,
                mod_all[layer + 1],
            )
            layer_in = y
            a1_near, a1_far = gather_near(a1), cross(a1)
        else:
            z2 = None
            y, grad, dz2, dgate_b, d_bias_down = call(
                "turn",
                functools.partial(turn_kernel, width, slots, terms),
                [block, block, block, slot_block, slot_block],
                *sums,
                h1,
                bias_down,
                own_col,
                own_row,
                mods,
                cotangent,
            )
        outputs.append(y)
        saved.append((*kept_state, z2))

    attention_shards, feed_shards, in_grads, d_mods, d_biases = ([None, None] for _ in range(5))
    strip_index = jnp.arange(SLOT_ROWS)[:, None]
    for layer in (1, 0):
        mods = mod_all[layer]
        w_att, w_feed = attention[layer], feed[layer]
        (layer_in, a1_all, near_q, far_q, k, v, near_o, far_o, near_lse, far_lse) = saved[layer][:10]
        (z1, h1, a2_all, near_u, far_u, near_g, far_g, _) = saved[layer][10:]
        dz2_near, dz2_far = gather_near(dz2), cross(dz2)

        def feed_back_half(blocks_of, u):
            return call(
                "feed_back",
                functools.partial(feed_back_kernel, half, len(w_feed)),
                [shape((frames // 2, units), bf16)] + [block] * half,
                *blocks_of,
                *w_feed,
                u,
            )

        near_du, *near_parts = feed_back_half(dz2_near, near_u)
        dz2_all = dz2_near + gather_near(after(dz2_far, near_du))
        far_du, *far_parts = feed_back_half(dz2_all[half:], far_u)
        summed, far_du = tie(near_sum(far_parts), far_du)
        sums = [*scatter_near(near_parts), cross(summed)]
        feed_outs = (
            [(groups, units // local * depth + units, local)]
            if packed
            else [(groups, depth, units), (groups, units, depth)]
        )
        *d_feed, d_bias_up = call(
            "feed_grads",
            functools.partial(feed_grads_kernel, tensors),
            [shape(dims, bf16) for dims in feed_outs] + [shape((SLOT_ROWS, units), f32)],
            *a2_all,
            *dz2_all,
            near_g,
            far_g,
            near_du,
            far_du,
            flops=4 * frames * width * units,
        )
        feed_shards[layer] = [
            lax.psum_scatter(value, "dp", scatter_dimension=0, tiled=False) for value in d_feed
        ]
        sums = [*sums[:-1], after(sums[-1], d_bias_up)]
        dh1, dz1, d_mod_middle, d_bias_out = call(
            "middle_back",
            functools.partial(middle_back_kernel, width, slots, terms),
            [block32, block, shape((SLOT_ROWS, 3 * width), f32), slot_block],
            *sums,
            h1,
            grad,
            z1,
            own_col,
            own_row,
            mods,
        )
        dz1_all = gather_rows(dz1)
        dq, dk, dv, *far_parts = call(
            "attend_back",
            functools.partial(attend_back_kernel, tensors, len(w_att)),
            [wide_local] * 3 + [block] * half,
            *dz1_all,
            *w_att,
            near_q,
            far_q,
            k,
            v,
            near_lse,
            far_lse,
            cos_table,
            sin_table,
            seg_col,
            seg_row,
            scratch=[
                pltpu.VMEM((frames, local), bf16),
                pltpu.VMEM((frames, local), f32),
                pltpu.VMEM((frames, local), f32),
            ],
        )
        summed, dk = tie(near_sum(far_parts), dk)
        far = cross(summed)
        att_outs = (
            [(groups, 3 * depth + local, local)]
            if packed
            else [(groups, 3 * depth, local), (groups, local, depth)]
        )
        results = call(
            "attention_grads",
            functools.partial(attention_grads_kernel, tensors, len(w_att)),
            [block] * half
            + [shape(dims, bf16) for dims in att_outs]
            + [shape((3, SLOT_ROWS, local), f32)],
            *a1_all,
            *dz1_all,
            *w_att,
            dq,
            dk,
            dv,
            near_o,
            far_o,
            flops=11 * project // 2,
        )
        near_parts, d_att, d_bias_qkv = results[:half], results[half:-1], results[-1]
        far = after(far, d_bias_qkv)
        tied = tie(*d_att, *feed_shards[layer])
        d_att, feed_shards[layer] = tied[: len(d_att)], tied[len(d_att) :]
        attention_shards[layer] = [
            lax.psum_scatter(value, "dp", scatter_dimension=0, tiled=False) for value in d_att
        ]
        sums = [*scatter_near(near_parts), far]
        kernel = functools.partial(layer_back_kernel, width, slots, terms, layer > 0)
        arrays = [*sums, layer_in, dh1, own_col, own_row, mods]
        outs = [block, shape((SLOT_ROWS, 2 * width), f32)]
        bias_sums = jnp.concatenate([d_bias_out[:1], d_bias_down[:1]], axis=1)
        gate_sums = dgate_b
        if layer > 0:
            grad, d_mod_first, dz2, dgate_b, d_bias_down = call(
                "layer_back",
                kernel,
                outs + [block, slot_block, slot_block],
                *arrays,
                saved[layer - 1][-1],
                mod_all[layer - 1],
            )
        else:
            grad, d_mod_first = call("first_back", kernel, outs, *arrays)
        in_grads[layer] = grad
        bias_sums = jnp.pad(bias_sums, ((0, 0), (0, mod_width - bias_sums.shape[1])))
        d_mod = jnp.concatenate([d_mod_first, d_mod_middle, gate_sums], axis=1)
        d_mod = jnp.where(strip_index == slots, bias_sums, d_mod)
        blocks = [d_mod[:, b * strip : (b + 1) * strip] for b in range(tensors)]
        own = functools.reduce(
            jnp.add, reduce_rows(absolute(blocks, tensor), list(bits_of(tensors)))
        )
        own_bias = jnp.concatenate([d_bias_qkv[p, :1] for p in range(3)] + [d_bias_up[:1]], axis=1)
        own_bias = jnp.pad(own_bias, ((0, 0), (0, strip - own_bias.shape[1])))
        d_mods[layer] = jnp.where(strip_index == slots + 1, own_bias, own)

    def to_section(low, high):
        own = jnp.where(first, low, high)
        return own, swap(jnp.where(first, high, low), "section", 1)

    def add_sections(low, high):
        own, arrived = to_section(low, high)
        return own.astype(f32) + arrived.astype(f32)

    def frames_out(low, high):
        own, arrived = to_section(low, high)
        return jnp.where(first, jnp.stack([own, arrived]), jnp.stack([arrived, own]))

    activations = frames_out(*outputs)
    g_feed = [add_sections(*pair) for pair in zip(*feed_shards, strict=True)]
    input_grads = frames_out(*in_grads)
    d_mod, d_mod_other = to_section(*d_mods)
    pair = jnp.stack([d_mod, d_mod_other]).astype(bf16)
    pairs = jnp.stack([pair] + [swap(pair, "dp", j) for j in range(1, groups)])
    g_attention = [add_sections(*pair) for pair in zip(*attention_shards, strict=True)]
    everything = gather_rows(pairs.reshape(-1, strip))
    own_first = jnp.where(first, codes, codes[:, ::-1])
    live = jnp.where(slot_row < slots, own_first, jnp.zeros_like(own_first))
    places = tensor ^ jnp.arange(tensors, dtype=jnp.int32)
    (g_wmod,) = pl.pallas_call(
        functools.partial(mod_grads_kernel, tensors),
        name="mod_grads",
        out_shape=(shape((depth, mod_width), f32),),
        in_specs=[
            pl.BlockSpec(memory_space=pltpu.VMEM),
            pl.BlockSpec(memory_space=pltpu.SMEM),
        ]
        + [pl.BlockSpec(memory_space=pltpu.VMEM)] * tensors,
        compiler_params=pltpu.CompilerParams(vmem_limit_bytes=vmem_limit),
    )(live.reshape(-1, depth), places, *everything)
    row_sums = [
        jnp.sum(part.reshape(2 * groups, SLOT_ROWS, strip).astype(f32), axis=0)
        for part in everything
    ]
    own_sums = row_sums[0][slots + 1]
    all_sums = jnp.concatenate(absolute(row_sums, tensor), axis=1)

    def my_share(vector):
        count = vector.shape[-1] // groups
        return lax.dynamic_slice_in_dim(vector, group * count, count, vector.ndim - 1)

    g_bmod = my_share(jnp.sum(all_sums[:slots], axis=0))
    g_bqkv = my_share(own_sums[: 3 * local].reshape(3, local))
    g_bup = my_share(own_sums[3 * local : 3 * local + units])
    g_bout = my_share(all_sums[slots, :width])
    g_bdown = my_share(all_sums[slots, width : 2 * width])
    chunks = units // local * depth
    if packed:
        g_qkv, g_out = g_attention[0][: 3 * depth], g_attention[0][3 * depth :]
        g_up = jnp.concatenate(
            [g_feed[0][i : i + depth] for i in range(0, chunks, depth)], axis=1
        )
        g_down = g_feed[0][chunks:]
    else:
        g_qkv, g_out = g_attention
        g_up, g_down = g_feed
    return (
        activations[None, :, None],
        input_grads[None, :, None],
        g_qkv.reshape(1, 3, depth, local),
        g_bqkv[None],
        g_out[None],
        g_bout[None],
        g_up[None],
        g_bup[None],
        g_down[None],
        g_bdown[None],
        g_wmod[None],
        g_bmod[None],
    )


def solution(mesh):
    return jax.shard_map(
        per_device,
        mesh=mesh,
        in_specs=(
            P("section", None, "dp", "tensor", None),
            P(None, "dp", None),
            P(None, "dp", None),
            P("section", None, "dp", "tensor"),
            P("section", None, ("tensor", "dp")),
            P("section", "tensor", "dp"),
            P("section", "dp"),
            P("section", "dp", "tensor"),
            P("section", ("tensor", "dp")),
            P("section", "tensor", "dp"),
            P("section", "dp"),
            P("section", "dp", None),
            P("section", "dp"),
        ),
        out_specs=(
            P("section", None, "dp", "tensor", None),
            P("section", None, "dp", "tensor", None),
            P("section", None, "dp", "tensor"),
            P("section", None, ("tensor", "dp")),
            P("section", "tensor", "dp"),
            P("section", "dp"),
            P("section", "dp", "tensor"),
            P("section", ("tensor", "dp")),
            P("section", "tensor", "dp"),
            P("section", "dp"),
            P("section", "dp", None),
            P("section", "dp"),
        ),
        check_vma=False,
    )
```

time: 686 us -> 575 us (0.84)
  blocking collectives: 39 us -> 0 us
  local copies, waits for them, and re-layouts: 87.2 us -> 48.9 us
  starting transfers between devices: 92.1 us -> 61.1 us
  Pallas kernels: 160 us -> 180 us
  waiting for transfers between devices: 244 us -> 228 us
    all_gather x2 -> x0, blocking collectives: 39 us -> none  [gather_groups(): return lax.all_gather(block, 'dp', axis=0, tiled=False)]
    ppermute x75 -> x74, waiting for transfers between devices: 221 us -> 186 us  [swap(): lax.ppermute(block, axis, [(i, i ^ bit) for i in range(lax.axis_size(axis...]
    dynamic_update_slice x8 -> x0, local copies, waits for them, and re-layouts: 28.2 us -> none  [the longest x4 27.8 us: per_device(): lax.dynamic_update_slice(d_mod, block[:, :, :, None], (0, 0, 0, tensor ^...]
    ppermute x14 -> x7, starting transfers between devices: 34.7 us -> 11.2 us  [per_device(): lax.ppermute(term, ('section', 'dp'), route)]
    concatenate x5 -> x12, local copies, waits for them, and re-layouts: 19.9 us -> 0.35 us  [the longest x10 0.17 us: with_biases(): jnp.concatenate([functools.reduce(jnp.add, parts), biases_of], axis=0)]
    pallas_call x23 -> x30, Pallas kernels: 160 us -> 180 us  [the longest x29 176 us: call(): pl.pallas_call(body, in_specs=[spec_of(arg) for arg in args], out_specs=(...]
    all_gather x0 -> x1, waiting for transfers between devices: none -> 18.1 us  [per_device(): lax.all_gather(pack, ('section', 'dp'), axis=0, tiled=False)]
    ppermute x14 -> x7, waiting for transfers between devices: 14.9 us -> 5.97 us  [per_device(): lax.ppermute(term, ('section', 'dp'), route)]
  transfers between devices with their start and end apart: 103 -> 88, of which waited for: 40 -> 49; matrix products, arithmetic and copies ran while one was open for 14% -> 8% of each run, Pallas kernels for 21% -> 28%
where the time goes in v2:
time: 575 us; the launch traced here: 568 us
  waiting for transfers between devices  228 us (40%)
  Pallas kernels  180 us (31%)
  starting transfers between devices  61.1 us (11%)
  local copies, waits for them, and re-layouts  48.9 us (9%)
  other arithmetic  33.8 us (6%)
  between operations  15.6 us (3%)
    ppermute x74, waiting for transfers between devices, swap(): lax.ppermute(block, axis, [(i, i ^ bit) for i in range(lax.axis_size(axis...  186 us
    pallas_call x29, Pallas kernels, call(): pl.pallas_call(body, in_specs=[spec_of(arg) for arg in args], out_specs=(...  176 us
    ppermute x74, starting transfers between devices, swap(): lax.ppermute(block, axis, [(i, i ^ bit) for i in range(lax.axis_size(axis...  49.3 us
    unnamed x237, local copies, waits for them, and re-layouts  34.7 us
    all_gather x1, waiting for transfers between devices, per_device(): lax.all_gather(pack, ('section', 'dp'), axis=0, tiled=False)  18.1 us
  transfers between devices with their start and end apart: 88, of which 49 were waited for; matrix products, arithmetic and copies ran while one was open for 8% of the time, Pallas kernels for 28%

profile of v2, /device:TPU:0, one launch (start us, length us, event | category | flops | bytes accessed | tf_op | source)
XLA Modules:
  0.0 568.2 jit_solution(1425928162010847830)
XLA Ops:
  53.5 13.2 %collective-permute-done.2.refs_2_ = bf16[256,1024]{1,0:T(8,128)(2,1)S(1)} collective-permute-done((bf16[256,1024]{1,0:T(8,128)(2,1)S(1)}, bf16[256,1024]{1,0:T(8,128)(2,1)S(1)}, u32[]{:S(2)}, u32[]{:S(2)}) %collective-permute-start.2) | collective-permute-done | bytes 524320 | tf_op jit(solution)/shard_map/ppermute | solution.py:21
  79.6 18.1 %all-gather.7.cloned.1.call-done = bf16[8192,256]{1,0:T(8,128)(2,1)} async-done(((bf16[1024,256]{1,0:T(8,128)(2,1)}), bf16[8192,256]{1,0:T(8,128)(2,1)}) %all-gather.7.cloned.1.call-update) | async-done | bytes 4194320 | tf_op jit(solution)/shard_map/all_gather | solution.py:667
  100.7 8.7 %attend_far.2 = (bf16[512,256]{1,0:T(8,128)(2,1)S(1)}, bf16[1024,256]{1,0:T(8,128)(2,1)S(1)}, bf16[1024,256]{1,0:T(8,128)(2,1)}, bf16[512,256]{1,0:T(8,128)(2,1)...) custom-call(bf16[256,1024]{1,0:T(8,128)(2,1)} %copy-done.21, ...), custom_call_target="tpu_custom_call" | custom-call | tf_op jit(solution)/shard_map/attend_far/pallas_call | solution.py:109
  115.6 6.4 %attend_near.2 = (bf16[512,256]{1,0:T(8,128)(2,1)S(1)}, f32[512,128]{1,0:T(8,128)S(1)}, bf16[256,1024]{1,0:T(8,128)(2,1)S(1)}, bf16[256,1024]{1,0:T(8,128)(2,1)S(1)}) custom-call(bf16[8,1024,256]{2,1,0:T(8,128)(2,1)} %bitcast.208, s32[1024,1]{1,0:T(8,128)} %copy.42.refs_4_.refs_6_.refs_1_.refs_13_, s32[1,1024]{1,0:T(1,128)S(1)} %bitcast.191, ...), custom_call_target="tpu_custom_call" | custom-call | flops 805306368 | tf_op jit(solution)/shard_map/attend_near/pallas_call | solution.py:109
  134.4 11.0 %all-gather.9.cloned.1.call-done = bf16[4096,256]{1,0:T(8,128)(2,1)} async-done(((bf16[1024,256]{1,0:T(8,128)(2,1)}), bf16[4096,256]{1,0:T(8,128)(2,1)}) %all-gather.9.cloned.1.call-update) | async-done | bytes 2097168 | tf_op jit(solution)/shard_map/all_gather | solution.py:86
  163.6 11.6 %collective-permute-done.27.refs_2_ = bf16[256,1024]{1,0:T(8,128)(2,1)S(1)} collective-permute-done((bf16[256,1024]{1,0:T(8,128)(2,1)S(1)}, bf16[256,1024]{1,0:T(8,128)(2,1)S(1)}, u32[]{:S(2)}, u32[]{:S(2)}) %collective-permute-start.27) | collective-permute-done | bytes 524320 | tf_op jit(solution)/shard_map/ppermute | solution.py:21
  187.7 8.2 %collective-permute-done.28.refs_0_.refs_2_ = bf16[256,1024]{1,0:T(8,128)(2,1)S(1)} collective-permute-done((bf16[256,1024]{1,0:T(8,128)(2,1)}, bf16[256,1024]{1,0:T(8,128)(2,1)S(1)}, u32[]{:S(2)}, u32[]{:S(2)}) %collective-permute-start.28) | collective-permute-done | bytes 524320 | tf_op jit(solution)/shard_map/ppermute | solution.py:21
  198.7 8.7 %attend_far.3 = (bf16[512,256]{1,0:T(8,128)(2,1)S(1)}, bf16[1024,256]{1,0:T(8,128)(2,1)S(1)}, bf16[1024,256]{1,0:T(8,128)(2,1)}, bf16[512,256]{1,0:T(8,128)(2,1)...) custom-call(bf16[256,1024]{1,0:T(8,128)(2,1)} %copy-done.95, ...), custom_call_target="tpu_custom_call" | custom-call | tf_op jit(solution)/shard_map/attend_far/pallas_call | solution.py:109
  213.1 6.5 %attend_near.3 = (bf16[512,256]{1,0:T(8,128)(2,1)S(1)}, f32[512,128]{1,0:T(8,128)S(1)}, bf16[256,1024]{1,0:T(8,128)(2,1)S(1)}, bf16[256,1024]{1,0:T(8,128)(2,1)S(1)}) custom-call(bf16[8,1024,256]{2,1,0:T(8,128)(2,1)} %bitcast.211, s32[1024,1]{1,0:T(8,128)} %copy.42.refs_4_.refs_6_.refs_1_.refs_13_, s32[1,1024]{1,0:T(1,128)S(1)} %bitcast.193, ...), custom_call_target="tpu_custom_call" | custom-call | flops 805306368 | tf_op jit(solution)/shard_map/attend_near/pallas_call | solution.py:109
  255.7 12.5 %collective-permute-done.39.refs_2_ = bf16[256,1024]{1,0:T(8,128)(2,1)S(1)} collective-permute-done((bf16[256,1024]{1,0:T(8,128)(2,1)S(1)}, bf16[256,1024]{1,0:T(8,128)(2,1)S(1)}, u32[]{:S(2)}, u32[]{:S(2)}) %collective-permute-start.39) | collective-permute-done | bytes 524320 | tf_op jit(solution)/shard_map/ppermute | solution.py:21
  280.0 6.8 %collective-permute-done.43.refs_0_.refs_6_ = bf16[256,1024]{1,0:T(8,128)(2,1)S(1)} collective-permute-done((bf16[256,1024]{1,0:T(8,128)(2,1)S(1)}, bf16[256,1024]{1,0:T(8,128)(2,1)S(1)}, u32[]{:S(2)}, u32[]{:S(2)}) %collective-permute-start.43) | collective-permute-done | bytes 524320 | tf_op jit(solution)/shard_map/ppermute | solution.py:21
  297.4 6.2 %feed_grads.2 = (bf16[4,1024,256]{2,1,0:T(8,128)(2,1)}, f32[8,512]{1,0:T(8,128)S(1)}) custom-call(bf16[256,1024]{1,0:T(8,128)(2,1)S(1)} %copy-done.44, bf16[256,1024]{1,0:T(8,128)(2,1)S(1)} %copy-done.46, bf16[256,1024]{1,0:T(8,128)(2,1)} %collective-permute-done.36.refs_0_.refs_2_, bf16[256,1024]{1,0:T(8,128)(2,1)} %copy-done.115, ...), custom_call_target="tpu_custom_call" | custom-call | flops 2147483648 | tf_op jit(solution)/shard_map/feed_grads/pallas_call | solution.py:109
  303.6 6.2 %collective-permute-done.46.refs_2_ = bf16[256,1024]{1,0:T(8,128)(2,1)S(1)} collective-permute-done((bf16[256,1024]{1,0:T(8,128)(2,1)S(1)}, bf16[256,1024]{1,0:T(8,128)(2,1)S(1)}, u32[]{:S(2)}, u32[]{:S(2)}) %collective-permute-start.46) | collective-permute-done | bytes 524320 | tf_op jit(solution)/shard_map/ppermute | solution.py:21
  316.9 11.6 %collective-permute-done.48.refs_2_.refs_6_ = bf16[256,1024]{1,0:T(8,128)(2,1)} collective-permute-done((bf16[256,1024]{1,0:T(8,128)(2,1)S(1)}, bf16[256,1024]{1,0:T(8,128)(2,1)}, u32[]{:S(2)}, u32[]{:S(2)}) %collective-permute-start.48) | collective-permute-done | bytes 524320 | tf_op jit(solution)/shard_map/ppermute | solution.py:21
  332.4 22.7 %attend_back.2 = (bf16[1024,256]{1,0:T(8,128)(2,1)S(1)}, bf16[1024,256]{1,0:T(8,128)(2,1)}, bf16[1024,256]{1,0:T(8,128)(2,1)}, bf16[256,1024]{1,0:T(8,128)(2,1)}, bf16[256,1024]{1,0:T(8,128)(2,1)}) custom-call(bf16[256,1024]{1,0:T(8,128)(2,1)} %copy-done.17, bf16[256,1024]{1,0:T(8,128)(2,1)} %copy-done.76, ...), custom_call_target="tpu_custom_call" | custom-call | tf_op jit(solution)/shard_map/attend_back/pallas_call | solution.py:109
  360.1 7.9 %attention_grads.2 = (bf16[256,1024]{1,0:T(8,128)(2,1)S(1)}, bf16[256,1024]{1,0:T(8,128)(2,1)S(1)}, bf16[4,1024,256]{2,1,0:T(8,128)(2,1)}, f32[3,8,256]{2,1,0:T(8,128)S(1)}) custom-call(bf16[256,1024]{1,0:T(8,128)(2,1)} %get-tuple-element.188.refs_0_, bf16[256,1024]{1,0:T(8,128)(2,1)} %copy-done.13, bf16[256,1024]{1,0:T(8,128)(2,1)} %copy-done.95, ...), custom_call_target="tpu_custom_call" | custom-call | flops 2952790016 | tf_op jit(solution)/shard_map/attention_grads/pallas_call | solution.py:109
  402.2 6.0 %feed_grads.3 = (bf16[4,1024,256]{2,1,0:T(8,128)(2,1)}, f32[8,512]{1,0:T(8,128)S(1)}) custom-call(bf16[256,1024]{1,0:T(8,128)(2,1)S(1)} %copy-done.38, bf16[256,1024]{1,0:T(8,128)(2,1)S(1)} %copy-done.40, bf16[256,1024]{1,0:T(8,128)(2,1)S(1)} %copy-done.42, bf16[256,1024]{1,0:T(8,128)(2,1)} %copy-done.114, bf16[256,1024]{1,0:T(8,128)(2,1)} %copy-done.23, ...), custom_call_target="tpu_custom_call" | custom-call | flops 2147483648 | tf_op jit(solution)/shard_map/feed_grads/pallas_call | solution.py:109
  410.8 12.5 %collective-permute-done.58.refs_2_ = bf16[256,1024]{1,0:T(8,128)(2,1)S(1)} collective-permute-done((bf16[256,1024]{1,0:T(8,128)(2,1)S(1)}, bf16[256,1024]{1,0:T(8,128)(2,1)S(1)}, u32[]{:S(2)}, u32[]{:S(2)}) %collective-permute-start.58) | collective-permute-done | bytes 524320 | tf_op jit(solution)/shard_map/ppermute | solution.py:21
  431.3 11.1 %collective-permute-done.60.refs_2_.refs_6_ = bf16[256,1024]{1,0:T(8,128)(2,1)} collective-permute-done((bf16[256,1024]{1,0:T(8,128)(2,1)S(1)}, bf16[256,1024]{1,0:T(8,128)(2,1)}, u32[]{:S(2)}, u32[]{:S(2)}) %collective-permute-start.60) | collective-permute-done | bytes 524320 | tf_op jit(solution)/shard_map/ppermute | solution.py:21
  448.4 22.5 %attend_back.3 = (bf16[1024,256]{1,0:T(8,128)(2,1)S(1)}, bf16[1024,256]{1,0:T(8,128)(2,1)}, bf16[1024,256]{1,0:T(8,128)(2,1)}, bf16[256,1024]{1,0:T(8,128)(2,1)}, bf16[256,1024]{1,0:T(8,128)(2,1)}) custom-call(bf16[256,1024]{1,0:T(8,128)(2,1)} %copy-done.14, bf16[256,1024]{1,0:T(8,128)(2,1)} %collective-permute-done.59.refs_1_.refs_5_, ...), custom_call_target="tpu_custom_call" | custom-call | tf_op jit(solution)/shard_map/attend_back/pallas_call | solution.py:109
  477.0 8.0 %attention_grads.3 = (bf16[256,1024]{1,0:T(8,128)(2,1)S(1)}, bf16[256,1024]{1,0:T(8,128)(2,1)S(1)}, bf16[4,1024,256]{2,1,0:T(8,128)(2,1)}, f32[3,8,256]{2,1,0:T(8,128)S(1)}) custom-call(bf16[256,1024]{1,0:T(8,128)(2,1)} %copy-done.8, bf16[256,1024]{1,0:T(8,128)(2,1)} %copy-done.9, bf16[256,1024]{1,0:T(8,128)(2,1)} %copy-done.21, ...), custom_call_target="tpu_custom_call" | custom-call | flops 2952790016 | tf_op jit(solution)/shard_map/attention_grads/pallas_call | solution.py:109
  530.8 6.7 %collective-permute-done.80 = bf16[1024,256]{1,0:T(8,128)(2,1)S(1)} collective-permute-done((bf16[1024,256]{1,0:T(8,128)(2,1)S(1)}, bf16[1024,256]{1,0:T(8,128)(2,1)S(1)}, u32[]{:S(2)}, u32[]{:S(2)}) %collective-permute-start.80) | collective-permute-done | bytes 524320 | tf_op jit(solution)/shard_map/ppermute | solution.py:21
  537.7 6.5 %reduce-scatter.7.cloned.1.call-done = bf16[1,1024,256]{2,1,0:T(8,128)(2,1)} async-done(((bf16[4,1024,256]{2,1,0:T(8,128)(2,1)}), bf16[1,1024,256]{2,1,0:T(8,128)(2,1)}) %reduce-scatter.7.cloned.1.call-update) | async-done | bytes 524304 | tf_op jit(solution)/shard_map/reduce_scatter | solution.py:1000
  549.7 9.5 %collective-permute-done.66 = bf16[1024,256]{1,0:T(8,128)(2,1)S(1)} collective-permute-done((bf16[1024,256]{1,0:T(8,128)(2,1)S(1)}, bf16[1024,256]{1,0:T(8,128)(2,1)S(1)}, u32[]{:S(2)}, u32[]{:S(2)}) %collective-permute-start.66) | collective-permute-done | bytes 524320 | tf_op jit(solution)/shard_map/ppermute | solution.py:21
  (559 shorter events, 303.4 us)
Async XLA Ops:
  7.3 90.5 %all-gather.7.cloned.1.call-start = ((), (), s32[]{:S(2)}) async-start(), calls=%async_computation.8 | async-start | bytes 4718592 | tf_op jit(solution)/shard_map/all_gather | solution.py:667
  15.7 129.8 %all-gather.9.cloned.1.call-start = ((), (), s32[]{:S(2)}) async-start(), calls=%async_computation.9 | async-start | bytes 2621440 | tf_op jit(solution)/shard_map/all_gather | solution.py:86
  17.8 33.1 %collective-permute-start = (bf16[256,1024]{1,0:T(8,128)(2,1)}, bf16[256,1024]{1,0:T(8,128)(2,1)}, u32[]{:S(2)}, u32[]{:S(2)}) collective-permute-start(bf16[256,1024]{1,0:T(8,128)(2,1)} %select_bitcast_fusion.3), channel_id=1, source_target_pairs={{0,16},{16,0},{1,17},{17,1},{2,18},{18,2},{3,19},{19,3},{4,20},{20... | collective-permute-start | bytes 1572872 | tf_op jit(solution)/shard_map/ppermute | solution.py:21
  45.5 29.3 %collective-permute-start.17 = (bf16[256,512]{1,0:T(8,128)(2,1)}, bf16[256,512]{1,0:T(8,128)(2,1)S(1)}, u32[]{:S(2)}, u32[]{:S(2)}) collective-permute-start(bf16[256,512]{1,0:T(8,128)(2,1)} %bitcast.43), channel_id=1, source_target_pairs={{0,16},{16,0},{1,17},{17,1},{2,18},{18,2},{3,19},{19,3},{4,20},{20... | collective-permute-start | bytes 786440 | tf_op jit(solution)/shard_map/ppermute | solution.py:21
  48.7 26.1 %collective-permute-start.18 = (bf16[512,256]{1,0:T(8,128)(2,1)}, bf16[512,256]{1,0:T(8,128)(2,1)S(1)}, u32[]{:S(2)}, u32[]{:S(2)}) collective-permute-start(bf16[512,256]{1,0:T(8,128)(2,1)} %bitcast.44), channel_id=1, source_target_pairs={{0,16},{16,0},{1,17},{17,1},{2,18},{18,2},{3,19},{19,3},{4,20},{20... | collective-permute-start | bytes 786440 | tf_op jit(solution)/shard_map/ppermute | solution.py:21
  78.6 153.3 %all-gather.11.cloned.1.call-start = ((), (), s32[]{:S(2)}) async-start(), calls=%async_computation.10 | async-start | bytes 2621440 | tf_op jit(solution)/shard_map/all_gather | solution.py:86
  114.3 14.2 %collective-permute-start.21 = (bf16[256,1024]{1,0:T(8,128)(2,1)}, bf16[256,1024]{1,0:T(8,128)(2,1)S(1)}, u32[]{:S(2)}, u32[]{:S(2)}) collective-permute-start(bf16[256,1024]{1,0:T(8,128)(2,1)} %add_convert_fusion.7), channel_id=1, source_target_pairs={{0,8},{4,12},{8,0},{12,4},{1,9},{5,13},{9,1},{13,5},{2,10},{6,14},... | collective-permute-start | bytes 1572872 | tf_op jit(solution)/shard_map/ppermute | solution.py:21
  133.2 18.9 %collective-permute-start.24 = (bf16[256,1024]{1,0:T(8,128)(2,1)S(1)}, bf16[256,1024]{1,0:T(8,128)(2,1)S(1)}, u32[]{:S(2)}, u32[]{:S(2)}) collective-permute-start(bf16[256,1024]{1,0:T(8,128)(2,1)S(1)} %get-tuple-element.177.refs_0_), channel_id=1, source_target_pairs={{0,8},{4,12},{8,0},{12,4},{1,9},{5,13},{9,1},{13,5},{2,10},{6,14},... | collective-permute-start | bytes 1572872 | tf_op jit(solution)/shard_map/ppermute | solution.py:21
  161.1 14.0 %collective-permute-start.27 = (bf16[256,1024]{1,0:T(8,128)(2,1)S(1)}, bf16[256,1024]{1,0:T(8,128)(2,1)S(1)}, u32[]{:S(2)}, u32[]{:S(2)}) collective-permute-start(bf16[256,1024]{1,0:T(8,128)(2,1)S(1)} %add_convert_fusion.6), channel_id=1, source_target_pairs={{0,8},{4,12},{8,0},{12,4},{1,9},{5,13},{9,1},{13,5},{2,10},{6,14},... | collective-permute-start | bytes 1572872 | tf_op jit(solution)/shard_map/ppermute | solution.py:21
  163.5 284.8 %reduce-scatter.9.cloned.1.call-start = ((), (), s32[]{:S(2)}) async-start(), calls=%async_computation.6 | async-start | bytes 2621440 | tf_op jit(solution)/shard_map/reduce_scatter | solution.py:934
  181.4 14.5 %collective-permute-start.28 = (bf16[256,1024]{1,0:T(8,128)(2,1)}, bf16[256,1024]{1,0:T(8,128)(2,1)S(1)}, u32[]{:S(2)}, u32[]{:S(2)}) collective-permute-start(bf16[256,1024]{1,0:T(8,128)(2,1)} %get-tuple-element.188.refs_0_), channel_id=1, source_target_pairs={{0,8},{4,12},{8,0},{12,4},{1,9},{5,13},{9,1},{13,5},{2,10},{6,14},... | collective-permute-start | bytes 1572872 | tf_op jit(solution)/shard_map/ppermute | solution.py:21
  211.6 14.0 %collective-permute-start.33 = (bf16[256,1024]{1,0:T(8,128)(2,1)S(1)}, bf16[256,1024]{1,0:T(8,128)(2,1)S(1)}, u32[]{:S(2)}, u32[]{:S(2)}) collective-permute-start(bf16[256,1024]{1,0:T(8,128)(2,1)S(1)} %add_convert_fusion.5), channel_id=1, source_target_pairs={{0,8},{4,12},{8,0},{12,4},{1,9},{5,13},{9,1},{13,5},{2,10},{6,14},... | collective-permute-start | bytes 1572872 | tf_op jit(solution)/shard_map/ppermute | solution.py:21
  230.4 14.4 %collective-permute-start.36 = (bf16[256,1024]{1,0:T(8,128)(2,1)S(1)}, bf16[256,1024]{1,0:T(8,128)(2,1)}, u32[]{:S(2)}, u32[]{:S(2)}) collective-permute-start(bf16[256,1024]{1,0:T(8,128)(2,1)S(1)} %get-tuple-element.203.refs_0_), channel_id=1, source_target_pairs={{0,8},{4,12},{8,0},{12,4},{1,9},{5,13},{9,1},{13,5},{2,10},{6,14},... | collective-permute-start | bytes 1572872 | tf_op jit(solution)/shard_map/ppermute | solution.py:21
  254.1 14.0 %collective-permute-start.39 = (bf16[256,1024]{1,0:T(8,128)(2,1)S(1)}, bf16[256,1024]{1,0:T(8,128)(2,1)S(1)}, u32[]{:S(2)}, u32[]{:S(2)}) collective-permute-start(bf16[256,1024]{1,0:T(8,128)(2,1)S(1)} %add_convert_fusion.4), channel_id=1, source_target_pairs={{0,8},{4,12},{8,0},{12,4},{1,9},{5,13},{9,1},{13,5},{2,10},{6,14},... | collective-permute-start | bytes 1572872 | tf_op jit(solution)/shard_map/ppermute | solution.py:21
  272.5 14.3 %collective-permute-start.43 = (bf16[256,1024]{1,0:T(8,128)(2,1)S(1)}, bf16[256,1024]{1,0:T(8,128)(2,1)S(1)}, u32[]{:S(2)}, u32[]{:S(2)}) collective-permute-start(bf16[256,1024]{1,0:T(8,128)(2,1)S(1)} %get-tuple-element.212.refs_0_.refs_4_), channel_id=1, source_target_pairs={{0,8},{4,12},{8,0},{12,4},{1,9},{5,13},{9,1},{13,5},{2,10},{6,14},... | collective-permute-start | bytes 1572872 | tf_op jit(solution)/shard_map/ppermute | solution.py:21
  316.8 179.6 %reduce-scatter.5.cloned.1.call-start = ((), (), s32[]{:S(2)}) async-start(), calls=%async_computation.4 | async-start | bytes 2621440 | tf_op jit(solution)/shard_map/reduce_scatter | solution.py:934
  358.5 14.0 %collective-permute-start.52 = (bf16[256,1024]{1,0:T(8,128)(2,1)S(1)}, bf16[256,1024]{1,0:T(8,128)(2,1)S(1)}, u32[]{:S(2)}, u32[]{:S(2)}) collective-permute-start(bf16[256,1024]{1,0:T(8,128)(2,1)S(1)} %add_convert_fusion.2), channel_id=1, source_target_pairs={{0,8},{4,12},{8,0},{12,4},{1,9},{5,13},{9,1},{13,5},{2,10},{6,14},... | collective-permute-start | bytes 1572872 | tf_op jit(solution)/shard_map/ppermute | solution.py:21
  378.0 14.3 %collective-permute-start.55 = (bf16[256,1024]{1,0:T(8,128)(2,1)S(1)}, bf16[256,1024]{1,0:T(8,128)(2,1)S(1)}, u32[]{:S(2)}, u32[]{:S(2)}) collective-permute-start(bf16[256,1024]{1,0:T(8,128)(2,1)S(1)} %get-tuple-element.247.refs_0_.refs_4_), channel_id=1, source_target_pairs={{0,8},{4,12},{8,0},{12,4},{1,9},{5,13},{9,1},{13,5},{2,10},{6,14},... | collective-permute-start | bytes 1572872 | tf_op jit(solution)/shard_map/ppermute | solution.py:21
  408.3 129.4 %reduce-scatter.11.cloned.1.call-start = ((), (), s32[]{:S(2)}) async-start(), calls=%async_computation.7 | async-start | bytes 2621440 | tf_op jit(solution)/shard_map/reduce_scatter | solution.py:1000
  431.3 17.1 %collective-permute-start.59 = (bf16[256,1024]{1,0:T(8,128)(2,1)S(1)}, bf16[256,1024]{1,0:T(8,128)(2,1)}, u32[]{:S(2)}, u32[]{:S(2)}) collective-permute-start(bf16[256,1024]{1,0:T(8,128)(2,1)S(1)} %get-tuple-element.264.refs_0_.refs_4_), channel_id=1, source_target_pairs={{0,4},{4,0},{8,12},{12,8},{1,5},{5,1},{9,13},{13,9},{2,6},{6,2},{1... | collective-permute-start | bytes 1572872 | tf_op jit(solution)/shard_map/ppermute | solution.py:21
  445.3 56.1 %collective-permute-start.40 = (bf16[256,1024]{1,0:T(8,128)(2,1)}, bf16[256,1024]{1,0:T(8,128)(2,1)}, u32[]{:S(2)}, u32[]{:S(2)}) collective-permute-start(bf16[256,1024]{1,0:T(8,128)(2,1)} %get-tuple-element.314), channel_id=1, source_target_pairs={{0,16},{16,0},{1,17},{17,1},{2,18},{18,2},{3,19},{19,3},{4,20},{20... | collective-permute-start | bytes 1572872 | tf_op jit(solution)/shard_map/ppermute | solution.py:21
  448.3 95.9 %reduce-scatter.7.cloned.1.call-start = ((), (), s32[]{:S(2)}) async-start(), calls=%async_computation.5 | async-start | bytes 2621440 | tf_op jit(solution)/shard_map/reduce_scatter | solution.py:1000
  475.5 14.2 %collective-permute-start.64 = (bf16[256,1024]{1,0:T(8,128)(2,1)S(1)}, bf16[256,1024]{1,0:T(8,128)(2,1)S(1)}, u32[]{:S(2)}, u32[]{:S(2)}) collective-permute-start(bf16[256,1024]{1,0:T(8,128)(2,1)S(1)} %add_convert_fusion), channel_id=1, source_target_pairs={{0,8},{4,12},{8,0},{12,4},{1,9},{5,13},{9,1},{13,5},{2,10},{6,14},... | collective-permute-start | bytes 1572872 | tf_op jit(solution)/shard_map/ppermute | solution.py:21
  523.0 14.4 %collective-permute-start.80 = (bf16[1024,256]{1,0:T(8,128)(2,1)S(1)}, bf16[1024,256]{1,0:T(8,128)(2,1)S(1)}, u32[]{:S(2)}, u32[]{:S(2)}) collective-permute-start(bf16[1024,256]{1,0:T(8,128)(2,1)S(1)} %broadcast_select_fusion), channel_id=1, source_target_pairs={{0,16},{16,0},{1,17},{17,1},{2,18},{18,2},{3,19},{19,3},{4,20},{20... | collective-permute-start | bytes 1572872 | tf_op jit(solution)/shard_map/ppermute | solution.py:21
  (180 other events, 1265.7 us)
Sparse Core Ops, SparseCore 0:
  15.8 81.8 all-gather.6
  99.9 45.5 all-gather.8
  163.7 43.7 all-gather.10
  316.9 41.6 reduce-scatter.8
  408.4 42.5 reduce-scatter.4
  453.2 43.1 reduce-scatter.10
  498.8 45.3 reduce-scatter.6

commit v3 on v2

--- a/solution.py
+++ b/solution.py
@@ -316,22 +316,33 @@
 
 
 class Feed:
-    def __init__(self, refs, width, units):
-        self.refs, self.width, self.units = refs, width, units
-        self.groups, _, lanes = refs[0].shape
+    def __init__(self, refs, width, units, copies):
+        self.refs, self.width, self.units, self.copies = refs, width, units, copies
+        self.groups, _, self.lanes = refs[0].shape
         self.depth = width // self.groups
-        self.chunks = units // lanes
-        self.offset = self.chunks * self.depth if len(refs) == 1 else 0
-
-    def up(self):
-        parts = [
-            self.refs[0][:, i * self.depth : (i + 1) * self.depth, :].reshape(self.width, -1)
-            for i in range(self.chunks)
-        ]
-        return parts
-
-    def down(self, g):
-        return self.refs[-1][g, self.offset : self.offset + self.units, :]
+        self.chunks = units // self.lanes
+        self.packed = len(refs) == 1
+
+    def up_place(self, copy, chunk):
+        if self.packed:
+            return self.refs[0], copy * (self.chunks * self.depth + self.units) + chunk * self.depth
+        return self.refs[2 * copy], 0
+
+    def down_place(self, copy):
+        if self.packed:
+            return self.refs[0], self.up_place(copy, self.chunks)[1]
+        return self.refs[2 * copy + 1], 0
+
+    def ups(self):
+        for copy in range(self.copies):
+            for chunk in range(self.chunks):
+                ref, row = self.up_place(copy, chunk)
+                block = ref[:, row : row + self.depth, :].reshape(self.width, self.lanes)
+                yield copy * self.units + chunk * self.lanes, block
+
+    def down(self, copy, g):
+        ref, row = self.down_place(copy)
+        return ref[g, row : row + self.units, :]
 
 
 def qkv_of(x, weights, bias_ref, cos, sin):
@@ -513,74 +524,82 @@
     return root, square, th
 
 
-def feed_kernel(blocks, parts, *refs):
+def feed_kernel(blocks, parts, copies, *refs):
     a_refs = refs[:blocks]
     rows, width = a_refs[0].shape
     bias_ref, u_ref, g_ref = refs[blocks + parts : blocks + parts + 3]
-    weights = Feed(refs[blocks : blocks + parts], width, bias_ref.shape[1])
+    units = bias_ref.shape[1] // copies
+    weights = Feed(refs[blocks : blocks + parts], width, units, copies)
     part_refs = refs[blocks + parts + 3 :]
     depth = weights.depth
-    ups = weights.up()
-    lanes = ups[0].shape[1]
     for j in reversed(range(blocks)):
         here = slice(j * rows, (j + 1) * rows)
-        for i, w_up in enumerate(ups):
-            columns = slice(i * lanes, (i + 1) * lanes)
+        for start, w_up in weights.ups():
+            columns = slice(start, start + weights.lanes)
             u = mm(a_refs[j][...], w_up) + bias_ref[:, columns]
             u_ref[here, columns] = u
             _, _, th = gelu_parts(u)
             g_ref[here, columns] = (0.5 * u * (1.0 + th)).astype(bf16)
         for k in range(weights.groups):
-            part_refs[j][:, k * depth : (k + 1) * depth] = mm(
-                g_ref[here, :], weights.down(k)
+            part_refs[j][:, k * depth : (k + 1) * depth] = sum(
+                mm(g_ref[here, copy * units : (copy + 1) * units], weights.down(copy, k))
+                for copy in range(copies)
             ).astype(bf16)
 
 
-def feed_back_kernel(blocks, parts, *refs):
+def feed_back_kernel(blocks, parts, copies, *refs):
     dz_refs = refs[:blocks]
     rows, width = dz_refs[0].shape
     u_ref, du_ref = refs[blocks + parts : blocks + parts + 2]
-    weights = Feed(refs[blocks : blocks + parts], width, u_ref.shape[1])
+    units = u_ref.shape[1] // copies
+    weights = Feed(refs[blocks : blocks + parts], width, units, copies)
     part_refs = refs[blocks + parts + 2 :]
     depth = weights.depth
-    ups = weights.up()
-    lanes = ups[0].shape[1]
     for j in reversed(range(blocks)):
         here = slice(j * rows, (j + 1) * rows)
-        dg = jnp.zeros((rows, weights.units), f32)
-        for k in range(weights.groups):
-            dg = dg + mm_last(dz_refs[j][:, k * depth : (k + 1) * depth], weights.down(k))
-        u = u_ref[here, :]
-        root, square, th = gelu_parts(u)
-        slope = 0.5 * (1.0 + th) + 0.5 * u * (1.0 - th * th) * (root * (1.0 + 0.134145 * square))
-        du = (dg * slope).astype(bf16)
-        du_ref[here, :] = du
+        for copy in range(copies):
+            columns = slice(copy * units, (copy + 1) * units)
+            dg = sum(
+                mm_last(dz_refs[j][:, k * depth : (k + 1) * depth], weights.down(copy, k))
+                for k in range(weights.groups)
+            )
+            u = u_ref[here, columns]
+            root, square, th = gelu_parts(u)
+            slope = 0.5 * (1.0 + th) + 0.5 * u * (1.0 - th * th) * (
+                root * (1.0 + 0.134145 * square)
+            )
+            du_ref[here, columns] = (dg * slope).astype(bf16)
         part_refs[j][...] = sum(
-            mm_last(du[:, i * lanes : (i + 1) * lanes], w_up) for i, w_up in enumerate(ups)
+            mm_last(du_ref[here, start : start + weights.lanes], w_up)
+            for start, w_up in weights.ups()
         ).astype(bf16)
 
 
-def feed_grads_kernel(blocks, *refs):
+def feed_grads_kernel(blocks, sides, copies, *refs):
     a_refs, dz_refs = refs[:blocks], refs[blocks : 2 * blocks]
-    near_g_ref, far_g_ref, near_du_ref, far_du_ref = refs[2 * blocks : 2 * blocks + 4]
-    outs = refs[2 * blocks + 4 : -1]
-    bias_up_ref = refs[-1]
-    width, units = a_refs[0].shape[1], near_g_ref.shape[1]
-    groups, _, lanes = outs[0].shape
-    depth = width // groups
-    chunks = units // lanes
-    offset = chunks * depth if len(outs) == 1 else 0
+    g_refs = refs[2 * blocks : 2 * blocks + sides]
+    du_refs = refs[2 * blocks + sides : 2 * blocks + 2 * sides]
+    outs, bias_up_ref = refs[2 * blocks + 2 * sides : -1], refs[-1]
+    width, units = a_refs[0].shape[1], g_refs[0].shape[1] // copies
+    places = Feed(outs, width, units, copies)
+    depth, lanes = places.depth, places.lanes
     dz = jnp.concatenate([ref[...] for ref in dz_refs], axis=0)
     a2 = jnp.concatenate([ref[...] for ref in a_refs], axis=0)
-    g = jnp.concatenate([near_g_ref[...], far_g_ref[...]], axis=0)
-    du = jnp.concatenate([near_du_ref[...], far_du_ref[...]], axis=0)
-    for k in range(groups):
+    g = jnp.concatenate([ref[...] for ref in g_refs], axis=0)
+    du = jnp.concatenate([ref[...] for ref in du_refs], axis=0)
+    for k in range(places.groups):
         here = slice(k * depth, (k + 1) * depth)
-        outs[-1][k, offset : offset + units, :] = mm_first(g, dz[:, here]).astype(bf16)
-        for i in range(chunks):
-            outs[0][k, i * depth : (i + 1) * depth, :] = mm_first(
-                a2[:, here], du[:, i * lanes : (i + 1) * lanes]
+        for copy in range(copies):
+            ref, row = places.down_place(copy)
+            ref[k, row : row + units, :] = mm_first(
+                g[:, copy * units : (copy + 1) * units], dz[:, here]
             ).astype(bf16)
+            for chunk in range(places.chunks):
+                ref, row = places.up_place(copy, chunk)
+                start = copy * units + chunk * lanes
+                ref[k, row : row + depth, :] = mm_first(
+                    a2[:, here], du[:, start : start + lanes]
+                ).astype(bf16)
     bias_up_ref[...] = column_sums(du)
 
 
@@ -774,7 +793,14 @@
 
     other_up, other_down, a1_near[0] = tie(other_up, other_down, a1_near[0])
     pairs = pick(w_up[0], other_up), pick(w_down[0], other_down)
-    feed = [[gather_groups(pack) for pack in feed_packs(layer, *pairs)] for layer in range(2)]
+    feed = [[gather_groups(pack) for pack in feed_packs(0, *pairs)]]
+    last_packs = feed_packs(1, *pairs)
+    partner_packs = [cross(pack) for pack in last_packs]
+    if packed:
+        last_packs = [jnp.concatenate(last_packs + partner_packs, axis=0)]
+    else:
+        last_packs = last_packs + partner_packs
+    feed.append([gather_groups(pack) for pack in last_packs])
 
     layer_in = h0
     saved = []
@@ -838,13 +864,17 @@
             mods,
         )
         w_feed = feed[layer]
-        a2_near, a2_far = gather_near(a2), cross(a2)
+        copies = layer + 1
+        a2_near = gather_near(a2)
+        if copies == 2:
+            bias_up = jnp.concatenate([bias_up, cross(bias_up)], axis=1)
 
         def feed_half(blocks_of):
+            columns = units * copies
             return call(
                 "feed",
-                functools.partial(feed_kernel, half, len(w_feed)),
-                [shape((frames // 2, units), f32), shape((frames // 2, units), bf16)]
+                functools.partial(feed_kernel, half, len(w_feed), copies),
+                [shape((frames // 2, columns), f32), shape((frames // 2, columns), bf16)]
                 + [block] * half,
                 *blocks_of,
                 *w_feed,
@@ -852,16 +882,24 @@
                 flops=2 * frames * width * units,
             )
 
-        near_u, near_g, *near_parts = feed_half(a2_near)
-        a2_all = a2_near + gather_near(after(a2_far, near_u))
-        far_u, far_g, *far_parts = feed_half(a2_all[half:])
-        sums = [*scatter_near(near_parts), cross(near_sum(far_parts))]
+        if copies == 1:
+            a2_far = cross(a2)
+            near_u, near_g, *near_parts = feed_half(a2_near)
+            a2_far = gather_near(after(a2_far, near_u))
+            far_u, far_g, *far_parts = feed_half(a2_far)
+            sums = [*scatter_near(near_parts), cross(near_sum(far_parts))]
+            a2_all = a2_near + a2_far
+            u_all, g_all = (near_u, far_u), (near_g, far_g)
+        else:
+            near_u, near_g, *near_parts = feed_half(a2_near)
+            sums = scatter_near(near_parts)
+            a2_all, u_all, g_all = a2_near, (near_u,), (near_g,)
         kept_state = (layer_in, a1_all, near_q, far_q, k, v, near_o, far_o, near_lse, far_lse)
-        kept_state += (z1, h1, a2_all, near_u, far_u, near_g, far_g)
+        kept_state += (z1, h1, a2_all, u_all, g_all)
         if layer == 0:
             z2, y, a1 = call(
                 "layer_end",
-                functools.partial(layer_end_kernel, width, terms),
+                functools.partial(layer_end_kernel, width, len(sums)),
                 [block] * 3,
                 *sums,
                 h1,
@@ -876,7 +914,7 @@
             z2 = None
             y, grad, dz2, dgate_b, d_bias_down = call(
                 "turn",
-                functools.partial(turn_kernel, width, slots, terms),
+                functools.partial(turn_kernel, width, slots, len(sums)),
                 [block, block, block, slot_block, slot_block],
                 *sums,
                 h1,
@@ -895,48 +933,60 @@
         mods = mod_all[layer]
         w_att, w_feed = attention[layer], feed[layer]
         (layer_in, a1_all, near_q, far_q, k, v, near_o, far_o, near_lse, far_lse) = saved[layer][:10]
-        (z1, h1, a2_all, near_u, far_u, near_g, far_g, _) = saved[layer][10:]
-        dz2_near, dz2_far = gather_near(dz2), cross(dz2)
+        (z1, h1, a2_all, u_all, g_all, _) = saved[layer][10:]
+        copies = layer + 1
+        dz2_near = gather_near(dz2)
 
         def feed_back_half(blocks_of, u):
             return call(
                 "feed_back",
-                functools.partial(feed_back_kernel, half, len(w_feed)),
-                [shape((frames // 2, units), bf16)] + [block] * half,
+                functools.partial(feed_back_kernel, half, len(w_feed), copies),
+                [shape((frames // 2, units * copies), bf16)] + [block] * half,
                 *blocks_of,
                 *w_feed,
                 u,
             )
 
-        near_du, *near_parts = feed_back_half(dz2_near, near_u)
-        dz2_all = dz2_near + gather_near(after(dz2_far, near_du))
-        far_du, *far_parts = feed_back_half(dz2_all[half:], far_u)
-        summed, far_du = tie(near_sum(far_parts), far_du)
-        sums = [*scatter_near(near_parts), cross(summed)]
-        feed_outs = (
-            [(groups, units // local * depth + units, local)]
-            if packed
-            else [(groups, depth, units), (groups, units, depth)]
-        )
-        *d_feed, d_bias_up = call(
-            "feed_grads",
-            functools.partial(feed_grads_kernel, tensors),
-            [shape(dims, bf16) for dims in feed_outs] + [shape((SLOT_ROWS, units), f32)],
-            *a2_all,
-            *dz2_all,
-            near_g,
-            far_g,
-            near_du,
-            far_du,
-            flops=4 * frames * width * units,
-        )
-        feed_shards[layer] = [
-            lax.psum_scatter(value, "dp", scatter_dimension=0, tiled=False) for value in d_feed
-        ]
-        sums = [*sums[:-1], after(sums[-1], d_bias_up)]
+        if copies == 1:
+            dz2_far = cross(dz2)
+            near_du, *near_parts = feed_back_half(dz2_near, u_all[0])
+            dz2_all = dz2_near + gather_near(after(dz2_far, near_du))
+            far_du, *far_parts = feed_back_half(dz2_all[half:], u_all[1])
+            summed, far_du = tie(near_sum(far_parts), far_du)
+            sums = [*scatter_near(near_parts), cross(summed)]
+            du_all = (near_du, far_du)
+        else:
+            dz2_all = dz2_near
+            near_du, *near_parts = feed_back_half(dz2_near, u_all[0])
+            sums = scatter_near(near_parts)
+            du_all = (near_du,)
+
+        def feed_grads(du_all):
+            pack_rows = units // local * depth + units
+            feed_outs = (
+                [(groups, copies * pack_rows, local)]
+                if packed
+                else [(groups, depth, units), (groups, units, depth)] * copies
+            )
+            return call(
+                "feed_grads",
+                functools.partial(feed_grads_kernel, len(a2_all), len(du_all), copies),
+                [shape(dims, bf16) for dims in feed_outs]
+                + [shape((SLOT_ROWS, units * copies), f32)],
+                *a2_all,
+                *dz2_all,
+                *g_all,
+                *du_all,
+                flops=4 * frames * width * units,
+            )
+
+        if copies == 1:
+            *d_feed, d_bias_up = feed_grads(du_all)
+            sums = [*sums[:-1], after(sums[-1], d_bias_up)]
+            sums[-1], *feed_shards[1] = tie(sums[-1], *feed_shards[1])
         dh1, dz1, d_mod_middle, d_bias_out = call(
             "middle_back",
-            functools.partial(middle_back_kernel, width, slots, terms),
+            functools.partial(middle_back_kernel, width, slots, len(sums)),
             [block32, block, shape((SLOT_ROWS, 3 * width), f32), slot_block],
             *sums,
             h1,
@@ -946,7 +996,16 @@
             own_row,
             mods,
         )
-        dz1_all = gather_rows(dz1)
+        dz1_far = cross(dz1)
+        if copies == 2:
+            dz1, *du_all = tie(dz1, *du_all)
+            *d_feed, d_bias_up = feed_grads(du_all)
+            dz1_far = after(dz1_far, d_bias_up)
+            d_bias_up = d_bias_up[:, :units] + cross(d_bias_up[:, units:])
+        feed_shards[layer] = [
+            lax.psum_scatter(value, "dp", scatter_dimension=0, tiled=False) for value in d_feed
+        ]
+        dz1_all = gather_near(dz1) + gather_near(dz1_far)
         dq, dk, dv, *far_parts = call(
             "attend_back",
             functools.partial(attend_back_kernel, tensors, len(w_att)),
@@ -971,6 +1030,8 @@
         )
         summed, dk = tie(near_sum(far_parts), dk)
         far = cross(summed)
+        if layer == 0:
+            dq, *attention_shards[1] = tie(dq, *attention_shards[1])
         att_outs = (
             [(groups, 3 * depth + local, local)]
             if packed
@@ -994,8 +1055,8 @@
         )
         near_parts, d_att, d_bias_qkv = results[:half], results[half:-1], results[-1]
         far = after(far, d_bias_qkv)
-        tied = tie(*d_att, *feed_shards[layer])
-        d_att, feed_shards[layer] = tied[: len(d_att)], tied[len(d_att) :]
+        if layer == 0:
+            far, *feed_shards[0] = tie(far, *feed_shards[0])
         attention_shards[layer] = [
             lax.psum_scatter(value, "dp", scatter_dimension=0, tiled=False) for value in d_att
         ]
@@ -1027,6 +1088,20 @@
         own_bias = jnp.concatenate([d_bias_qkv[p, :1] for p in range(3)] + [d_bias_up[:1]], axis=1)
         own_bias = jnp.pad(own_bias, ((0, 0), (0, strip - own_bias.shape[1])))
         d_mods[layer] = jnp.where(strip_index == slots + 1, own_bias, own)
+
+    count = len(feed_shards[1])
+    if packed:
+        shard = feed_shards[1][0]
+        pack_rows = shard.shape[0] // 2
+        pieces = [(shard[:pack_rows], shard[pack_rows:])]
+    else:
+        pieces = list(
+            zip(feed_shards[1][: count // 2], feed_shards[1][count // 2 :])
+        )
+    feed_shards[1] = [
+        (own.astype(f32) + cross(partner).astype(f32)).astype(bf16)
+        for own, partner in pieces
+    ]
 
     def to_section(low, high):
         own = jnp.where(first, low, high)

time: 575 us -> 534 us (0.929)
  waiting for transfers between devices: 228 us -> 194 us
    ppermute x74 -> x70, waiting for transfers between devices: 186 us -> 162 us  [swap(): lax.ppermute(block, axis, [(i, i ^ bit) for i in range(lax.axis_size(axis...]
    reduce_scatter x4, waiting for transfers between devices: 6.55 us -> 0.03 us  [per_device(): lax.psum_scatter(value, 'dp', scatter_dimension=0, tiled=False)]
    pallas_call x29 -> x27, Pallas kernels: 176 us -> 172 us  [call(): pl.pallas_call(body, in_specs=[spec_of(arg) for arg in args], out_specs=(...]
    unnamed x237 -> x263, local copies, waits for them, and re-layouts: 34.7 us -> 31.5 us
    ppermute x74 -> x70, starting transfers between devices: 49.3 us -> 49.5 us  [swap(): lax.ppermute(block, axis, [(i, i ^ bit) for i in range(lax.axis_size(axis...]
  transfers between devices with their start and end apart: 88 -> 84, of which waited for: 49 -> 44; matrix products, arithmetic and copies ran while one was open for 8% -> 8% of each run, Pallas kernels for 28% -> 28%
where the time goes in v3:
time: 534 us; the launch traced here: 528 us
  waiting for transfers between devices  194 us (36%)
  Pallas kernels  176 us (33%)
  starting transfers between devices  62 us (12%)
  local copies, waits for them, and re-layouts  43.9 us (8%)
  other arithmetic  35.6 us (7%)
  between operations  16 us (3%)
    pallas_call x27, Pallas kernels, call(): pl.pallas_call(body, in_specs=[spec_of(arg) for arg in args], out_specs=(...  172 us
    ppermute x70, waiting for transfers between devices, swap(): lax.ppermute(block, axis, [(i, i ^ bit) for i in range(lax.axis_size(axis...  162 us
    ppermute x70, starting transfers between devices, swap(): lax.ppermute(block, axis, [(i, i ^ bit) for i in range(lax.axis_size(axis...  49.5 us
    unnamed x263, local copies, waits for them, and re-layouts  31.5 us
    all_gather x1, waiting for transfers between devices, per_device(): lax.all_gather(pack, ('section', 'dp'), axis=0, tiled=False)  16.3 us
    ppermute x7, starting transfers between devices, per_device(): lax.ppermute(term, ('section', 'dp'), route)  11.1 us
  transfers between devices with their start and end apart: 84, of which 44 were waited for; matrix products, arithmetic and copies ran while one was open for 8% of the time, Pallas kernels for 28%

profile of v3, /device:TPU:0, one launch (start us, length us, event | category | flops | bytes accessed | tf_op | source)
XLA Modules:
  0.0 528.2 jit_solution(4994387514735730472)
XLA Ops:
  51.1 13.3 %collective-permute-done.2.refs_2_ = bf16[256,1024]{1,0:T(8,128)(2,1)S(1)} collective-permute-done((bf16[256,1024]{1,0:T(8,128)(2,1)S(1)}, bf16[256,1024]{1,0:T(8,128)(2,1)S(1)}, u32[]{:S(2)}, u32[]{:S(2)}) %collective-permute-start.2) | collective-permute-done | bytes 524320 | tf_op jit(solution)/shard_map/ppermute | solution.py:21
  79.4 16.3 %all-gather.7.cloned.1.call-done = bf16[8192,256]{1,0:T(8,128)(2,1)} async-done(((bf16[1024,256]{1,0:T(8,128)(2,1)}), bf16[8192,256]{1,0:T(8,128)(2,1)}) %all-gather.7.cloned.1.call-update) | async-done | bytes 4194320 | tf_op jit(solution)/shard_map/all_gather | solution.py:686
  98.7 8.7 %attend_far.2 = (bf16[512,256]{1,0:T(8,128)(2,1)S(1)}, bf16[1024,256]{1,0:T(8,128)(2,1)S(1)}, bf16[1024,256]{1,0:T(8,128)(2,1)}, bf16[512,256]{1,0:T(8,128)(2,1)...) custom-call(bf16[256,1024]{1,0:T(8,128)(2,1)} %copy-done.23, ...), custom_call_target="tpu_custom_call" | custom-call | tf_op jit(solution)/shard_map/attend_far/pallas_call | solution.py:109
  114.1 6.4 %attend_near.2 = (bf16[512,256]{1,0:T(8,128)(2,1)S(1)}, f32[512,128]{1,0:T(8,128)S(1)}, bf16[256,1024]{1,0:T(8,128)(2,1)S(1)}, bf16[256,1024]{1,0:T(8,128)(2,1)S(1)}) custom-call(bf16[8,1024,256]{2,1,0:T(8,128)(2,1)} %bitcast.207, s32[1024,1]{1,0:T(8,128)} %copy.42.refs_4_.refs_6_.refs_1_.refs_13_, s32[1,1024]{1,0:T(1,128)S(1)} %bitcast.192, ...), custom_call_target="tpu_custom_call" | custom-call | flops 805306368 | tf_op jit(solution)/shard_map/attend_near/pallas_call | solution.py:109
  121.0 6.1 %collective-permute-done.21.refs_2_ = bf16[256,1024]{1,0:T(8,128)(2,1)S(1)} collective-permute-done((bf16[256,1024]{1,0:T(8,128)(2,1)}, bf16[256,1024]{1,0:T(8,128)(2,1)S(1)}, u32[]{:S(2)}, u32[]{:S(2)}) %collective-permute-start.21) | collective-permute-done | bytes 524320 | tf_op jit(solution)/shard_map/ppermute | solution.py:21
  133.2 8.9 %all-gather.9.cloned.1.call-done = bf16[4096,256]{1,0:T(8,128)(2,1)} async-done(((bf16[1024,256]{1,0:T(8,128)(2,1)}), bf16[4096,256]{1,0:T(8,128)(2,1)}) %all-gather.9.cloned.1.call-update) | async-done | bytes 2097168 | tf_op jit(solution)/shard_map/all_gather | solution.py:86
  159.7 12.5 %collective-permute-done.27.refs_2_ = bf16[256,1024]{1,0:T(8,128)(2,1)S(1)} collective-permute-done((bf16[256,1024]{1,0:T(8,128)(2,1)S(1)}, bf16[256,1024]{1,0:T(8,128)(2,1)S(1)}, u32[]{:S(2)}, u32[]{:S(2)}) %collective-permute-start.27) | collective-permute-done | bytes 524320 | tf_op jit(solution)/shard_map/ppermute | solution.py:21
  184.7 8.2 %collective-permute-done.28.refs_0_.refs_2_ = bf16[256,1024]{1,0:T(8,128)(2,1)S(1)} collective-permute-done((bf16[256,1024]{1,0:T(8,128)(2,1)}, bf16[256,1024]{1,0:T(8,128)(2,1)S(1)}, u32[]{:S(2)}, u32[]{:S(2)}) %collective-permute-start.28) | collective-permute-done | bytes 524320 | tf_op jit(solution)/shard_map/ppermute | solution.py:21
  195.6 9.0 %attend_far.3 = (bf16[512,256]{1,0:T(8,128)(2,1)S(1)}, bf16[1024,256]{1,0:T(8,128)(2,1)S(1)}, bf16[1024,256]{1,0:T(8,128)(2,1)}, bf16[512,256]{1,0:T(8,128)(2,1)...) custom-call(bf16[256,1024]{1,0:T(8,128)(2,1)} %copy-done.99, ...), custom_call_target="tpu_custom_call" | custom-call | tf_op jit(solution)/shard_map/attend_far/pallas_call | solution.py:109
  210.3 6.4 %attend_near.3 = (bf16[512,256]{1,0:T(8,128)(2,1)S(1)}, f32[512,128]{1,0:T(8,128)S(1)}, bf16[256,1024]{1,0:T(8,128)(2,1)S(1)}, bf16[256,1024]{1,0:T(8,128)(2,1)S(1)}) custom-call(bf16[8,1024,256]{2,1,0:T(8,128)(2,1)} %bitcast.210, s32[1024,1]{1,0:T(8,128)} %copy.42.refs_4_.refs_6_.refs_1_.refs_13_, s32[1,1024]{1,0:T(1,128)S(1)} %bitcast.194, ...), custom_call_target="tpu_custom_call" | custom-call | flops 805306368 | tf_op jit(solution)/shard_map/attend_near/pallas_call | solution.py:109
  232.1 6.6 %feed.5 = (f32[512,1024]{1,0:T(8,128)}, bf16[512,1024]{1,0:T(8,128)(2,1)}, bf16[256,1024]{1,0:T(8,128)(2,1)S(1)}, bf16[256,1024]{1,0:T(8,128)(2,1)S(1)}) custom-call(bf16[256,1024]{1,0:T(8,128)(2,1)S(1)} %get-tuple-element.196.refs_0_, bf16[256,1024]{1,0:T(8,128)(2,1)} %copy-done.15, bf16[4,2048,256]{2,1,0:T(8,128)(2,1)} %bitcast.215, ...), custom_call_target="tpu_custom_call" | custom-call | flops 1073741824 | tf_op jit(solution)/shard_map/feed/pallas_call | solution.py:109
  248.3 6.6 %feed_back.3 = (bf16[512,1024]{1,0:T(8,128)(2,1)}, bf16[256,1024]{1,0:T(8,128)(2,1)S(1)}, bf16[256,1024]{1,0:T(8,128)(2,1)S(1)}) custom-call(bf16[256,1024]{1,0:T(8,128)(2,1)S(1)} %get-tuple-element.201.refs_0_.refs_2_, bf16[256,1024]{1,0:T(8,128)(2,1)} %copy-done.77, bf16[4,2048,256]{2,1,0:T(8,128)(2,1)} %bitcast.216, f32[512,1024]{1,0:T(8,128)} %get-tuple-element.202.refs_3_), custom_call_target="tpu_custom_call" | custom-call | tf_op jit(solution)/shard_map/feed_back/pallas_call | solution.py:109
  262.3 6.4 %feed_grads.2 = (bf16[4,2048,256]{2,1,0:T(8,128)(2,1)}, f32[8,1024]{1,0:T(8,128)S(1)}) custom-call(bf16[256,1024]{1,0:T(8,128)(2,1)S(1)} %get-tuple-element.196.refs_0_, bf16[256,1024]{1,0:T(8,128)(2,1)S(1)} %copy-done.16, bf16[256,1024]{1,0:T(8,128)(2,1)S(1)} %get-tuple-element.201.refs_0_.refs_2_, bf16[256,1024]{1,0:T(8,128)(2,1)} %copy-done.77, ...), custom_call_target="tpu_custom_call" | custom-call | flops 2147483648 | tf_op jit(solution)/shard_map/feed_grads/pallas_call | solution.py:109
  271.3 12.5 %collective-permute-done.42.refs_2_.refs_6_ = bf16[256,1024]{1,0:T(8,128)(2,1)S(1)} collective-permute-done((bf16[256,1024]{1,0:T(8,128)(2,1)S(1)}, bf16[256,1024]{1,0:T(8,128)(2,1)S(1)}, u32[]{:S(2)}, u32[]{:S(2)}) %collective-permute-start.42) | collective-permute-done | bytes 524320 | tf_op jit(solution)/shard_map/ppermute | solution.py:21
  287.4 22.5 %attend_back.2 = (bf16[1024,256]{1,0:T(8,128)(2,1)S(1)}, bf16[1024,256]{1,0:T(8,128)(2,1)}, bf16[1024,256]{1,0:T(8,128)(2,1)}, bf16[256,1024]{1,0:T(8,128)(2,1)}, bf16[256,1024]{1,0:T(8,128)(2,1)}) custom-call(bf16[256,1024]{1,0:T(8,128)(2,1)} %copy-done.17, bf16[256,1024]{1,0:T(8,128)(2,1)} %copy-done.83, bf16[256,1024]{1,0:T(8,128)(2,1)} %copy-done.82, ...), custom_call_target="tpu_custom_call" | custom-call | tf_op jit(solution)/shard_map/attend_back/pallas_call | solution.py:109
  314.2 8.1 %attention_grads.2 = (bf16[256,1024]{1,0:T(8,128)(2,1)S(1)}, bf16[256,1024]{1,0:T(8,128)(2,1)S(1)}, bf16[4,1024,256]{2,1,0:T(8,128)(2,1)}, f32[3,8,256]{2,1,0:T(8,128)S(1)}) custom-call(bf16[256,1024]{1,0:T(8,128)(2,1)} %get-tuple-element.181.refs_0_, bf16[256,1024]{1,0:T(8,128)(2,1)} %copy-done.13, bf16[256,1024]{1,0:T(8,128)(2,1)} %copy-done.99, ...), custom_call_target="tpu_custom_call" | custom-call | flops 2952790016 | tf_op jit(solution)/shard_map/attention_grads/pallas_call | solution.py:109
  325.6 12.5 %collective-permute-done.46.refs_2_ = bf16[256,1024]{1,0:T(8,128)(2,1)S(1)} collective-permute-done((bf16[256,1024]{1,0:T(8,128)(2,1)S(1)}, bf16[256,1024]{1,0:T(8,128)(2,1)S(1)}, u32[]{:S(2)}, u32[]{:S(2)}) %collective-permute-start.46) | collective-permute-done | bytes 524320 | tf_op jit(solution)/shard_map/ppermute | solution.py:21
  351.8 6.1 %collective-permute-done.49.refs_0_.refs_6_ = bf16[256,1024]{1,0:T(8,128)(2,1)S(1)} collective-permute-done((bf16[256,1024]{1,0:T(8,128)(2,1)S(1)}, bf16[256,1024]{1,0:T(8,128)(2,1)S(1)}, u32[]{:S(2)}, u32[]{:S(2)}) %collective-permute-start.49) | collective-permute-done | bytes 524320 | tf_op jit(solution)/shard_map/ppermute | solution.py:21
  367.7 6.1 %feed_grads.3 = (bf16[4,1024,256]{2,1,0:T(8,128)(2,1)}, f32[8,512]{1,0:T(8,128)S(1)}) custom-call(bf16[256,1024]{1,0:T(8,128)(2,1)S(1)} %copy-done.47, bf16[256,1024]{1,0:T(8,128)(2,1)S(1)} %copy-done.49, bf16[256,1024]{1,0:T(8,128)(2,1)S(1)} %copy-done.51, bf16[256,1024]{1,0:T(8,128)(2,1)} %copy-done.128, bf16[256,1024]{1,0:T(8,128)(2,1)} %copy-done.24, ...), custom_call_target="tpu_custom_call" | custom-call | flops 2147483648 | tf_op jit(solution)/shard_map/feed_grads/pallas_call | solution.py:109
  377.3 11.7 %collective-permute-done.52.refs_2_ = bf16[256,1024]{1,0:T(8,128)(2,1)} collective-permute-done((bf16[256,1024]{1,0:T(8,128)(2,1)}, bf16[256,1024]{1,0:T(8,128)(2,1)}, u32[]{:S(2)}, u32[]{:S(2)}) %collective-permute-start.52) | collective-permute-done | bytes 524320 | tf_op jit(solution)/shard_map/ppermute | solution.py:21
  396.8 9.7 %collective-permute-done.54.refs_2_.refs_6_ = bf16[256,1024]{1,0:T(8,128)(2,1)S(1)} collective-permute-done((bf16[256,1024]{1,0:T(8,128)(2,1)S(1)}, bf16[256,1024]{1,0:T(8,128)(2,1)S(1)}, u32[]{:S(2)}, u32[]{:S(2)}) %collective-permute-start.54) | collective-permute-done | bytes 524320 | tf_op jit(solution)/shard_map/ppermute | solution.py:21
  411.8 22.6 %attend_back.3 = (bf16[1024,256]{1,0:T(8,128)(2,1)S(1)}, bf16[1024,256]{1,0:T(8,128)(2,1)}, bf16[1024,256]{1,0:T(8,128)(2,1)}, bf16[256,1024]{1,0:T(8,128)(2,1)}, bf16[256,1024]{1,0:T(8,128)(2,1)}) custom-call(bf16[256,1024]{1,0:T(8,128)(2,1)} %copy-done.14, bf16[256,1024]{1,0:T(8,128)(2,1)} %copy-done.79, bf16[256,1024]{1,0:T(8,128)(2,1)} %copy-done.78, ...), custom_call_target="tpu_custom_call" | custom-call | tf_op jit(solution)/shard_map/attend_back/pallas_call | solution.py:109
  441.2 7.9 %attention_grads.3 = (bf16[256,1024]{1,0:T(8,128)(2,1)S(1)}, bf16[256,1024]{1,0:T(8,128)(2,1)S(1)}, bf16[4,1024,256]{2,1,0:T(8,128)(2,1)}, f32[3,8,256]{2,1,0:T(8,128)S(1)}) custom-call(bf16[256,1024]{1,0:T(8,128)(2,1)} %copy-done.8, bf16[256,1024]{1,0:T(8,128)(2,1)} %copy-done.9, bf16[256,1024]{1,0:T(8,128)(2,1)} %copy-done.23, ...), custom_call_target="tpu_custom_call" | custom-call | flops 2952790016 | tf_op jit(solution)/shard_map/attention_grads/pallas_call | solution.py:109
  449.2 14.2 %collective-permute-done.58.refs_2_ = bf16[256,1024]{1,0:T(8,128)(2,1)S(1)} collective-permute-done((bf16[256,1024]{1,0:T(8,128)(2,1)S(1)}, bf16[256,1024]{1,0:T(8,128)(2,1)S(1)}, u32[]{:S(2)}, u32[]{:S(2)}) %collective-permute-start.58) | collective-permute-done | bytes 524320 | tf_op jit(solution)/shard_map/ppermute | solution.py:21
  (577 shorter events, 263.1 us)
Async XLA Ops:
  7.3 88.5 %all-gather.7.cloned.1.call-start = ((), (), s32[]{:S(2)}) async-start(), calls=%async_computation.8 | async-start | bytes 4718592 | tf_op jit(solution)/shard_map/all_gather | solution.py:686
  15.7 126.4 %all-gather.9.cloned.1.call-start = ((), (), s32[]{:S(2)}) async-start(), calls=%async_computation.9 | async-start | bytes 2621440 | tf_op jit(solution)/shard_map/all_gather | solution.py:86
  17.8 30.6 %collective-permute-start = (bf16[256,1024]{1,0:T(8,128)(2,1)}, bf16[256,1024]{1,0:T(8,128)(2,1)}, u32[]{:S(2)}, u32[]{:S(2)}) collective-permute-start(bf16[256,1024]{1,0:T(8,128)(2,1)} %select_bitcast_fusion.2), channel_id=1, source_target_pairs={{0,16},{16,0},{1,17},{17,1},{2,18},{18,2},{3,19},{19,3},{4,20},{20... | collective-permute-start | bytes 1572872 | tf_op jit(solution)/shard_map/ppermute | solution.py:21
  43.0 29.3 %collective-permute-start.17 = (bf16[256,512]{1,0:T(8,128)(2,1)S(1)}, bf16[256,512]{1,0:T(8,128)(2,1)S(1)}, u32[]{:S(2)}, u32[]{:S(2)}) collective-permute-start(bf16[256,512]{1,0:T(8,128)(2,1)S(1)} %bitcast.233), channel_id=1, source_target_pairs={{0,16},{16,0},{1,17},{17,1},{2,18},{18,2},{3,19},{19,3},{4,20},{20... | collective-permute-start | bytes 786440 | tf_op jit(solution)/shard_map/ppermute | solution.py:21
  46.2 26.2 %collective-permute-start.18 = (bf16[512,256]{1,0:T(8,128)(2,1)S(1)}, bf16[512,256]{1,0:T(8,128)(2,1)S(1)}, u32[]{:S(2)}, u32[]{:S(2)}) collective-permute-start(bf16[512,256]{1,0:T(8,128)(2,1)S(1)} %bitcast.234), channel_id=1, source_target_pairs={{0,16},{16,0},{1,17},{17,1},{2,18},{18,2},{3,19},{19,3},{4,20},{20... | collective-permute-start | bytes 786440 | tf_op jit(solution)/shard_map/ppermute | solution.py:21
  73.6 157.7 %all-gather.11.cloned.1.call-start = ((), (), s32[]{:S(2)}) async-start(), calls=%async_computation.10 | async-start | bytes 5242880 | tf_op jit(solution)/shard_map/all_gather | solution.py:86
  78.7 30.3 %collective-permute-start.35 = (bf16[1024,256]{1,0:T(8,128)(2,1)}, bf16[1024,256]{1,0:T(8,128)(2,1)}, u32[]{:S(2)}, u32[]{:S(2)}) collective-permute-start(bf16[1024,256]{1,0:T(8,128)(2,1)} %pad_maximum_fusion.3), channel_id=1, source_target_pairs={{0,8},{4,12},{8,0},{12,4},{1,9},{5,13},{9,1},{13,5},{2,10},{6,14},... | collective-permute-start | bytes 1572872 | tf_op jit(solution)/shard_map/ppermute | solution.py:21
  111.1 277.8 %reduce-scatter.5.cloned.1.call-start = ((), (), s32[]{:S(2)}) async-start(), calls=%async_computation.4 | async-start | bytes 5242880 | tf_op jit(solution)/shard_map/reduce_scatter | solution.py:1006
  112.6 14.5 %collective-permute-start.21 = (bf16[256,1024]{1,0:T(8,128)(2,1)}, bf16[256,1024]{1,0:T(8,128)(2,1)S(1)}, u32[]{:S(2)}, u32[]{:S(2)}) collective-permute-start(bf16[256,1024]{1,0:T(8,128)(2,1)} %add_convert_fusion.6), channel_id=1, source_target_pairs={{0,8},{4,12},{8,0},{12,4},{1,9},{5,13},{9,1},{13,5},{2,10},{6,14},... | collective-permute-start | bytes 1572872 | tf_op jit(solution)/shard_map/ppermute | solution.py:21
  131.6 17.1 %collective-permute-start.24 = (bf16[256,1024]{1,0:T(8,128)(2,1)S(1)}, bf16[256,1024]{1,0:T(8,128)(2,1)S(1)}, u32[]{:S(2)}, u32[]{:S(2)}) collective-permute-start(bf16[256,1024]{1,0:T(8,128)(2,1)S(1)} %get-tuple-element.170.refs_0_), channel_id=1, source_target_pairs={{0,8},{4,12},{8,0},{12,4},{1,9},{5,13},{9,1},{13,5},{2,10},{6,14},... | collective-permute-start | bytes 1572872 | tf_op jit(solution)/shard_map/ppermute | solution.py:21
  178.4 14.5 %collective-permute-start.28 = (bf16[256,1024]{1,0:T(8,128)(2,1)}, bf16[256,1024]{1,0:T(8,128)(2,1)S(1)}, u32[]{:S(2)}, u32[]{:S(2)}) collective-permute-start(bf16[256,1024]{1,0:T(8,128)(2,1)} %get-tuple-element.181.refs_0_), channel_id=1, source_target_pairs={{0,8},{4,12},{8,0},{12,4},{1,9},{5,13},{9,1},{13,5},{2,10},{6,14},... | collective-permute-start | bytes 1572872 | tf_op jit(solution)/shard_map/ppermute | solution.py:21
  208.8 14.0 %collective-permute-start.33 = (bf16[256,1024]{1,0:T(8,128)(2,1)S(1)}, bf16[256,1024]{1,0:T(8,128)(2,1)S(1)}, u32[]{:S(2)}, u32[]{:S(2)}) collective-permute-start(bf16[256,1024]{1,0:T(8,128)(2,1)S(1)} %add_convert_fusion.4), channel_id=1, source_target_pairs={{0,8},{4,12},{8,0},{12,4},{1,9},{5,13},{9,1},{13,5},{2,10},{6,14},... | collective-permute-start | bytes 1572872 | tf_op jit(solution)/shard_map/ppermute | solution.py:21
  269.3 169.5 %reduce-scatter.7.cloned.1.call-start = ((), (), s32[]{:S(2)}) async-start(), calls=%async_computation.5 | async-start | bytes 2621440 | tf_op jit(solution)/shard_map/reduce_scatter | solution.py:1061
  323.1 140.4 %reduce-scatter.9.cloned.1.call-start = ((), (), s32[]{:S(2)}) async-start(), calls=%async_computation.6 | async-start | bytes 2621440 | tf_op jit(solution)/shard_map/reduce_scatter | solution.py:1006
  343.5 14.3 %collective-permute-start.49 = (bf16[256,1024]{1,0:T(8,128)(2,1)S(1)}, bf16[256,1024]{1,0:T(8,128)(2,1)S(1)}, u32[]{:S(2)}, u32[]{:S(2)}) collective-permute-start(bf16[256,1024]{1,0:T(8,128)(2,1)S(1)} %get-tuple-element.231.refs_0_.refs_4_), channel_id=1, source_target_pairs={{0,8},{4,12},{8,0},{12,4},{1,9},{5,13},{9,1},{13,5},{2,10},{6,14},... | collective-permute-start | bytes 1572872 | tf_op jit(solution)/shard_map/ppermute | solution.py:21
  374.4 131.2 %reduce-scatter.11.cloned.1.call-start = ((), (), s32[]{:S(2)}) async-start(), calls=%async_computation.7 | async-start | bytes 2621440 | tf_op jit(solution)/shard_map/reduce_scatter | solution.py:1061
  374.6 14.3 %collective-permute-start.52 = (bf16[256,1024]{1,0:T(8,128)(2,1)}, bf16[256,1024]{1,0:T(8,128)(2,1)}, u32[]{:S(2)}, u32[]{:S(2)}) collective-permute-start(bf16[256,1024]{1,0:T(8,128)(2,1)} %add_convert_fusion.2), channel_id=1, source_target_pairs={{0,8},{4,12},{8,0},{12,4},{1,9},{5,13},{9,1},{13,5},{2,10},{6,14},... | collective-permute-start | bytes 1572872 | tf_op jit(solution)/shard_map/ppermute | solution.py:21
  396.7 14.1 %collective-permute-start.53 = (bf16[256,1024]{1,0:T(8,128)(2,1)S(1)}, bf16[256,1024]{1,0:T(8,128)(2,1)S(1)}, u32[]{:S(2)}, u32[]{:S(2)}) collective-permute-start(bf16[256,1024]{1,0:T(8,128)(2,1)S(1)} %get-tuple-element.250.refs_0_.refs_4_), channel_id=1, source_target_pairs={{0,4},{4,0},{8,12},{12,8},{1,5},{5,1},{9,13},{13,9},{2,6},{6,2},{1... | collective-permute-start | bytes 1572872 | tf_op jit(solution)/shard_map/ppermute | solution.py:21
  409.0 25.8 %collective-permute-start.64 = (f32[8,512]{1,0:T(8,128)S(1)}, f32[8,512]{1,0:T(8,128)S(1)}, u32[]{:S(2)}, u32[]{:S(2)}) collective-permute-start(f32[8,512]{1,0:T(8,128)S(1)} %get-tuple-element.341), channel_id=1, source_target_pairs={{0,8},{4,12},{8,0},{12,4},{1,9},{5,13},{9,1},{13,5},{2,10},{6,14},... | collective-permute-start | bytes 49160 | tf_op jit(solution)/shard_map/ppermute | solution.py:21
  437.9 37.6 %collective-permute-start.75 = (bf16[1024,256]{1,0:T(8,128)(2,1)}, bf16[1024,256]{1,0:T(8,128)(2,1)}, u32[]{:S(2)}, u32[]{:S(2)}) collective-permute-start(bf16[1024,256]{1,0:T(8,128)(2,1)} %slice.391), channel_id=1, source_target_pairs={{0,8},{4,12},{8,0},{12,4},{1,9},{5,13},{9,1},{13,5},{2,10},{6,14},... | collective-permute-start | bytes 1572872 | tf_op jit(solution)/shard_map/ppermute | solution.py:21
  440.1 23.4 %collective-permute-start.58 = (bf16[256,1024]{1,0:T(8,128)(2,1)S(1)}, bf16[256,1024]{1,0:T(8,128)(2,1)S(1)}, u32[]{:S(2)}, u32[]{:S(2)}) collective-permute-start(bf16[256,1024]{1,0:T(8,128)(2,1)S(1)} %add_convert_fusion.1), channel_id=1, source_target_pairs={{0,8},{4,12},{8,0},{12,4},{1,9},{5,13},{9,1},{13,5},{2,10},{6,14},... | collective-permute-start | bytes 1572872 | tf_op jit(solution)/shard_map/ppermute | solution.py:21
  449.1 14.3 %collective-permute-start.57 = (bf16[256,1024]{1,0:T(8,128)(2,1)S(1)}, bf16[256,1024]{1,0:T(8,128)(2,1)S(1)}, u32[]{:S(2)}, u32[]{:S(2)}) collective-permute-start(bf16[256,1024]{1,0:T(8,128)(2,1)S(1)} %get-tuple-element.264), channel_id=1, source_target_pairs={{0,4},{4,0},{8,12},{12,8},{1,5},{5,1},{9,13},{13,9},{2,6},{6,2},{1... | collective-permute-start | bytes 1572872 | tf_op jit(solution)/shard_map/ppermute | solution.py:21
  477.6 17.9 %collective-permute-start.76 = (bf16[1024,256]{1,0:T(8,128)(2,1)}, bf16[1024,256]{1,0:T(8,128)(2,1)}, u32[]{:S(2)}, u32[]{:S(2)}) collective-permute-start(bf16[1024,256]{1,0:T(8,128)(2,1)} %broadcast_select_fusion), channel_id=1, source_target_pairs={{0,16},{16,0},{1,17},{17,1},{2,18},{18,2},{3,19},{19,3},{4,20},{20... | collective-permute-start | bytes 1572872 | tf_op jit(solution)/shard_map/ppermute | solution.py:21
  483.6 18.8 %collective-permute-start.59 = (bf16[256,1024]{1,0:T(8,128)(2,1)}, bf16[256,1024]{1,0:T(8,128)(2,1)}, u32[]{:S(2)}, u32[]{:S(2)}) collective-permute-start(bf16[256,1024]{1,0:T(8,128)(2,1)} %get-tuple-element.298), channel_id=1, source_target_pairs={{0,16},{16,0},{1,17},{17,1},{2,18},{18,2},{3,19},{19,3},{4,20},{20... | collective-permute-start | bytes 1572872 | tf_op jit(solution)/shard_map/ppermute | solution.py:21
  (189 other events, 1478.5 us)
Sparse Core Ops, SparseCore 0:
  15.8 79.8 all-gather.6
  97.3 44.7 all-gather.8
  144.2 79.4 all-gather.10
  268.9 75.5 reduce-scatter.4
  346.7 44.3 reduce-scatter.6
  393.3 43.1 reduce-scatter.8
  449.3 45.4 reduce-scatter.10

commit v4 on v3

--- a/solution.py
+++ b/solution.py
@@ -103,7 +103,8 @@
     return pl.BlockSpec(memory_space=pltpu.VMEM)
 
 
-def call(name, body, outs, *args, scratch=(), flops=0):
+def call(name, body, outs, *args, scratch=(), flops=0, micros=0):
+    flops = flops or micros * 1_150_000_000
     whole = pl.BlockSpec(memory_space=pltpu.VMEM)
     grid = {"grid": (1,)} if any(isinstance(arg, Half) for arg in args) else {}
     return pl.pallas_call(
@@ -945,6 +946,7 @@
                 *blocks_of,
                 *w_feed,
                 u,
+                micros=4 * copies,
             )
 
         if copies == 1:
@@ -977,13 +979,11 @@
                 *dz2_all,
                 *g_all,
                 *du_all,
-                flops=4 * frames * width * units,
+                micros=6,
             )
 
-        if copies == 1:
-            *d_feed, d_bias_up = feed_grads(du_all)
-            sums = [*sums[:-1], after(sums[-1], d_bias_up)]
-            sums[-1], *feed_shards[1] = tie(sums[-1], *feed_shards[1])
+        *d_feed, d_bias_up = feed_grads(du_all)
+        sums = [*sums[:-1], after(sums[-1], d_bias_up)]
         dh1, dz1, d_mod_middle, d_bias_out = call(
             "middle_back",
             functools.partial(middle_back_kernel, width, slots, len(sums)),
@@ -995,16 +995,24 @@
             own_col,
             own_row,
             mods,
+            micros=4,
         )
         dz1_far = cross(dz1)
         if copies == 2:
-            dz1, *du_all = tie(dz1, *du_all)
-            *d_feed, d_bias_up = feed_grads(du_all)
-            dz1_far = after(dz1_far, d_bias_up)
             d_bias_up = d_bias_up[:, :units] + cross(d_bias_up[:, units:])
         feed_shards[layer] = [
             lax.psum_scatter(value, "dp", scatter_dimension=0, tiled=False) for value in d_feed
         ]
+        if layer == 0:
+            count = len(feed_shards[1])
+            if packed:
+                shard = feed_shards[1][0]
+                kept_units = [shard[: shard.shape[0] // 2]]
+                given_units = [shard[shard.shape[0] // 2 :]]
+            else:
+                kept_units, given_units = feed_shards[1][: count // 2], feed_shards[1][count // 2 :]
+            dz1_far, *given_units = tie(dz1_far, *given_units)
+            arrived_units = [cross(part) for part in given_units]
         dz1_all = gather_near(dz1) + gather_near(dz1_far)
         dq, dk, dv, *far_parts = call(
             "attend_back",
@@ -1027,11 +1035,12 @@
                 pltpu.VMEM((frames, local), f32),
                 pltpu.VMEM((frames, local), f32),
             ],
+            micros=22,
         )
         summed, dk = tie(near_sum(far_parts), dk)
         far = cross(summed)
         if layer == 0:
-            dq, *attention_shards[1] = tie(dq, *attention_shards[1])
+            dq, *arrived_units = tie(dq, *arrived_units)
         att_outs = (
             [(groups, 3 * depth + local, local)]
             if packed
@@ -1051,11 +1060,12 @@
             dv,
             near_o,
             far_o,
-            flops=11 * project // 2,
+            micros=8,
         )
         near_parts, d_att, d_bias_qkv = results[:half], results[half:-1], results[-1]
         far = after(far, d_bias_qkv)
         if layer == 0:
+            far, *attention_shards[1] = tie(far, *attention_shards[1])
             far, *feed_shards[0] = tie(far, *feed_shards[0])
         attention_shards[layer] = [
             lax.psum_scatter(value, "dp", scatter_dimension=0, tiled=False) for value in d_att
@@ -1074,6 +1084,7 @@
                 *arrays,
                 saved[layer - 1][-1],
                 mod_all[layer - 1],
+                micros=4,
             )
         else:
             grad, d_mod_first = call("first_back", kernel, outs, *arrays)
@@ -1089,18 +1100,9 @@
         own_bias = jnp.pad(own_bias, ((0, 0), (0, strip - own_bias.shape[1])))
         d_mods[layer] = jnp.where(strip_index == slots + 1, own_bias, own)
 
-    count = len(feed_shards[1])
-    if packed:
-        shard = feed_shards[1][0]
-        pack_rows = shard.shape[0] // 2
-        pieces = [(shard[:pack_rows], shard[pack_rows:])]
-    else:
-        pieces = list(
-            zip(feed_shards[1][: count // 2], feed_shards[1][count // 2 :])
-        )
     feed_shards[1] = [
-        (own.astype(f32) + cross(partner).astype(f32)).astype(bf16)
-        for own, partner in pieces
+        (own.astype(f32) + partner.astype(f32)).astype(bf16)
+        for own, partner in zip(kept_units, arrived_units, strict=True)
     ]
 
     def to_section(low, high):
@@ -1121,7 +1123,13 @@
     d_mod, d_mod_other = to_section(*d_mods)
     pair = jnp.stack([d_mod, d_mod_other]).astype(bf16)
     pairs = jnp.stack([pair] + [swap(pair, "dp", j) for j in range(1, groups)])
-    g_attention = [add_sections(*pair) for pair in zip(*attention_shards, strict=True)]
+    g_attention = []
+    for low, high in zip(*attention_shards, strict=True):
+        up = lax.ppermute(high, "section", [(0, 1)])
+        down = lax.ppermute(low, "section", [(1, 0)])
+        g_attention.append(
+            jnp.where(first, low, high).astype(f32) + jnp.where(first, down, up).astype(f32)
+        )
     everything = gather_rows(pairs.reshape(-1, strip))
     own_first = jnp.where(first, codes, codes[:, ::-1])
     live = jnp.where(slot_row < slots, own_first, jnp.zeros_like(own_first))

time: 534 us -> 515 us (0.964)
  waiting for transfers between devices: 194 us -> 181 us
    ppermute x70 -> x69, waiting for transfers between devices: 162 us -> 141 us  [swap(): lax.ppermute(block, axis, [(i, i ^ bit) for i in range(lax.axis_size(axis...]
    ppermute x0 -> x2, waiting for transfers between devices: none -> 7.52 us  [the longest x1 7.51 us: per_device(): down = lax.ppermute(low, 'section', [(1, 0)])]
    ppermute x70 -> x69, starting transfers between devices: 49.5 us -> 45.2 us  [swap(): lax.ppermute(block, axis, [(i, i ^ bit) for i in range(lax.axis_size(axis...]
    unnamed x263 -> x201, local copies, waits for them, and re-layouts: 31.5 us -> 30.1 us
  transfers between devices with their start and end apart: 84 -> 85, of which waited for: 44 -> 45; matrix products, arithmetic and copies ran while one was open for 8% -> 7% of each run, Pallas kernels for 28% -> 31%
where the time goes in v4:
time: 515 us; the launch traced here: 510 us
  waiting for transfers between devices  181 us (35%)
  Pallas kernels  178 us (35%)
  starting transfers between devices  63.1 us (12%)
  local copies, waits for them, and re-layouts  39.8 us (8%)
  other arithmetic  32.2 us (6%)
  between operations  15.6 us (3%)
    pallas_call x27, Pallas kernels, call(): pl.pallas_call(body, in_specs=[spec_of(arg) for arg in args], out_specs=(...  173 us
    ppermute x69, waiting for transfers between devices, swap(): lax.ppermute(block, axis, [(i, i ^ bit) for i in range(lax.axis_size(axis...  141 us
    ppermute x69, starting transfers between devices, swap(): lax.ppermute(block, axis, [(i, i ^ bit) for i in range(lax.axis_size(axis...  45.2 us
    unnamed x201, local copies, waits for them, and re-layouts  30.1 us
    all_gather x1, waiting for transfers between devices, per_device(): lax.all_gather(pack, ('section', 'dp'), axis=0, tiled=False)  15.3 us
    ppermute x7, starting transfers between devices, per_device(): lax.ppermute(term, ('section', 'dp'), route)  11.1 us
  transfers between devices with their start and end apart: 85, of which 45 were waited for; matrix products, arithmetic and copies ran while one was open for 7% of the time, Pallas kernels for 31%

profile of v4, /device:TPU:0, one launch (start us, length us, event | category | flops | bytes accessed | tf_op | source)
XLA Modules:
  0.0 509.6 jit_solution(4979977337864910372)
XLA Ops:
  34.2 5.8 %collective-permute-done.13 = f32[8,1536]{1,0:T(8,128)S(1)} collective-permute-done((f32[8,1536]{1,0:T(8,128)S(1)}, f32[8,1536]{1,0:T(8,128)S(1)}, u32[]{:S(2)}, u32[]{:S(2)}) %collective-permute-start.13) | collective-permute-done | bytes 49184 | tf_op jit(solution)/shard_map/ppermute | solution.py:729
  51.0 13.3 %collective-permute-done.2.refs_2_ = bf16[256,1024]{1,0:T(8,128)(2,1)S(1)} collective-permute-done((bf16[256,1024]{1,0:T(8,128)(2,1)S(1)}, bf16[256,1024]{1,0:T(8,128)(2,1)S(1)}, u32[]{:S(2)}, u32[]{:S(2)}) %collective-permute-start.2) | collective-permute-done | bytes 524320 | tf_op jit(solution)/shard_map/ppermute | solution.py:21
  80.4 15.3 %all-gather.7.cloned.1.call-done = bf16[8192,256]{1,0:T(8,128)(2,1)} async-done(((bf16[1024,256]{1,0:T(8,128)(2,1)}), bf16[8192,256]{1,0:T(8,128)(2,1)}) %all-gather.7.cloned.1.call-update) | async-done | bytes 4194320 | tf_op jit(solution)/shard_map/all_gather | solution.py:687
  98.7 8.7 %attend_far.2 = (bf16[512,256]{1,0:T(8,128)(2,1)S(1)}, bf16[1024,256]{1,0:T(8,128)(2,1)S(1)}, bf16[1024,256]{1,0:T(8,128)(2,1)}, bf16[512,256]{1,0:T(8,128)(2,1)...) custom-call(bf16[256,1024]{1,0:T(8,128)(2,1)} %copy-done.16, ...), custom_call_target="tpu_custom_call" | custom-call | tf_op jit(solution)/shard_map/attend_far/pallas_call | solution.py:110
  114.0 6.4 %attend_near.2 = (bf16[512,256]{1,0:T(8,128)(2,1)S(1)}, f32[512,128]{1,0:T(8,128)S(1)}, bf16[256,1024]{1,0:T(8,128)(2,1)S(1)}, bf16[256,1024]{1,0:T(8,128)(2,1)S(1)}) custom-call(bf16[8,1024,256]{2,1,0:T(8,128)(2,1)} %bitcast.214, s32[1024,1]{1,0:T(8,128)} %copy.42.refs_4_.refs_6_.refs_1_.refs_13_, s32[1,1024]{1,0:T(1,128)S(1)} %bitcast.199, ...), custom_call_target="tpu_custom_call" | custom-call | flops 805306368 | tf_op jit(solution)/shard_map/attend_near/pallas_call | solution.py:110
  132.3 9.7 %all-gather.9.cloned.1.call-done = bf16[4096,256]{1,0:T(8,128)(2,1)} async-done(((bf16[1024,256]{1,0:T(8,128)(2,1)}), bf16[4096,256]{1,0:T(8,128)(2,1)}) %all-gather.9.cloned.1.call-update) | async-done | bytes 2097168 | tf_op jit(solution)/shard_map/all_gather | solution.py:86
  159.7 12.5 %collective-permute-done.27.refs_2_ = bf16[256,1024]{1,0:T(8,128)(2,1)S(1)} collective-permute-done((bf16[256,1024]{1,0:T(8,128)(2,1)S(1)}, bf16[256,1024]{1,0:T(8,128)(2,1)S(1)}, u32[]{:S(2)}, u32[]{:S(2)}) %collective-permute-start.27) | collective-permute-done | bytes 524320 | tf_op jit(solution)/shard_map/ppermute | solution.py:21
  184.8 8.2 %collective-permute-done.28.refs_0_.refs_2_ = bf16[256,1024]{1,0:T(8,128)(2,1)S(1)} collective-permute-done((bf16[256,1024]{1,0:T(8,128)(2,1)}, bf16[256,1024]{1,0:T(8,128)(2,1)S(1)}, u32[]{:S(2)}, u32[]{:S(2)}) %collective-permute-start.28) | collective-permute-done | bytes 524320 | tf_op jit(solution)/shard_map/ppermute | solution.py:21
  195.7 9.2 %attend_far.3 = (bf16[512,256]{1,0:T(8,128)(2,1)S(1)}, bf16[1024,256]{1,0:T(8,128)(2,1)S(1)}, bf16[1024,256]{1,0:T(8,128)(2,1)}, bf16[512,256]{1,0:T(8,128)(2,1)...) custom-call(bf16[256,1024]{1,0:T(8,128)(2,1)} %copy-done.77, ...), custom_call_target="tpu_custom_call" | custom-call | tf_op jit(solution)/shard_map/attend_far/pallas_call | solution.py:110
  210.6 6.4 %attend_near.3 = (bf16[512,256]{1,0:T(8,128)(2,1)S(1)}, f32[512,128]{1,0:T(8,128)S(1)}, bf16[256,1024]{1,0:T(8,128)(2,1)S(1)}, bf16[256,1024]{1,0:T(8,128)(2,1)S(1)}) custom-call(bf16[8,1024,256]{2,1,0:T(8,128)(2,1)} %bitcast.217, s32[1024,1]{1,0:T(8,128)} %copy.42.refs_4_.refs_6_.refs_1_.refs_13_, s32[1,1024]{1,0:T(1,128)S(1)} %bitcast.201, ...), custom_call_target="tpu_custom_call" | custom-call | flops 805306368 | tf_op jit(solution)/shard_map/attend_near/pallas_call | solution.py:110
  232.4 6.5 %feed.5 = (f32[512,1024]{1,0:T(8,128)}, bf16[512,1024]{1,0:T(8,128)(2,1)}, bf16[256,1024]{1,0:T(8,128)(2,1)S(1)}, bf16[256,1024]{1,0:T(8,128)(2,1)S(1)}) custom-call(bf16[256,1024]{1,0:T(8,128)(2,1)S(1)} %get-tuple-element.196.refs_0_, bf16[256,1024]{1,0:T(8,128)(2,1)} %copy-done.12, bf16[4,2048,256]{2,1,0:T(8,128)(2,1)} %bitcast.223, ...), custom_call_target="tpu_custom_call" | custom-call | flops 1073741824 | tf_op jit(solution)/shard_map/feed/pallas_call | solution.py:110
  248.6 6.6 %feed_back.3 = (bf16[512,1024]{1,0:T(8,128)(2,1)}, bf16[256,1024]{1,0:T(8,128)(2,1)S(1)}, bf16[256,1024]{1,0:T(8,128)(2,1)S(1)}) custom-call(bf16[256,1024]{1,0:T(8,128)(2,1)S(1)} %get-tuple-element.201.refs_0_.refs_2_, bf16[256,1024]{1,0:T(8,128)(2,1)} %copy-done.96, bf16[4,2048,256]{2,1,0:T(8,128)(2,1)} %bitcast.224, f32[512,1024]{1,0:T(8,128)} %get-tuple-element.202.refs_3_), custom_call_target="tpu_custom_call" | custom-call | flops 9200000000 | tf_op jit(solution)/shard_map/feed_back/pallas_call | solution.py:110
  255.2 6.3 %feed_grads.2 = (bf16[4,2048,256]{2,1,0:T(8,128)(2,1)}, f32[8,1024]{1,0:T(8,128)S(1)}) custom-call(bf16[256,1024]{1,0:T(8,128)(2,1)S(1)} %get-tuple-element.196.refs_0_, bf16[256,1024]{1,0:T(8,128)(2,1)S(1)} %copy-done.13, bf16[256,1024]{1,0:T(8,128)(2,1)S(1)} %get-tuple-element.201.refs_0_.refs_2_, bf16[256,1024]{1,0:T(8,128)(2,1)} %copy-done.96, ...), custom_call_target="tpu_custom_call" | custom-call | flops 6899999744 | tf_op jit(solution)/shard_map/feed_grads/pallas_call | solution.py:110
  271.3 12.8 %collective-permute-done.42.refs_2_.refs_6_ = bf16[256,1024]{1,0:T(8,128)(2,1)S(1)} collective-permute-done((bf16[256,1024]{1,0:T(8,128)(2,1)S(1)}, bf16[256,1024]{1,0:T(8,128)(2,1)S(1)}, u32[]{:S(2)}, u32[]{:S(2)}) %collective-permute-start.42) | collective-permute-done | bytes 524320 | tf_op jit(solution)/shard_map/ppermute | solution.py:21
  286.8 22.5 %attend_back.2 = (bf16[1024,256]{1,0:T(8,128)(2,1)S(1)}, bf16[1024,256]{1,0:T(8,128)(2,1)}, bf16[1024,256]{1,0:T(8,128)(2,1)}, bf16[256,1024]{1,0:T(8,128)(2,1)}, bf16[256,1024]{1,0:T(8,128)(2,1)}) custom-call(bf16[256,1024]{1,0:T(8,128)(2,1)} %copy-done.28, bf16[256,1024]{1,0:T(8,128)(2,1)} %copy-done.90, bf16[256,1024]{1,0:T(8,128)(2,1)} %copy-done.89, ...), custom_call_target="tpu_custom_call" | custom-call | flops 25300000768 | tf_op jit(solution)/shard_map/attend_back/pallas_call | solution.py:110
  313.9 8.0 %attention_grads.2 = (bf16[256,1024]{1,0:T(8,128)(2,1)S(1)}, bf16[256,1024]{1,0:T(8,128)(2,1)S(1)}, bf16[4,1024,256]{2,1,0:T(8,128)(2,1)}, f32[3,8,256]{2,1,0:T(8,128)S(1)}) custom-call(bf16[256,1024]{1,0:T(8,128)(2,1)} %get-tuple-element.181.refs_0_, bf16[256,1024]{1,0:T(8,128)(2,1)} %copy-done.10, bf16[256,1024]{1,0:T(8,128)(2,1)} %copy-done.77, ...), custom_call_target="tpu_custom_call" | custom-call | flops 9200000000 | tf_op jit(solution)/shard_map/attention_grads/pallas_call | solution.py:110
  340.7 6.0 %collective-permute-done.49.refs_0_.refs_6_ = bf16[256,1024]{1,0:T(8,128)(2,1)} collective-permute-done((bf16[256,1024]{1,0:T(8,128)(2,1)S(1)}, bf16[256,1024]{1,0:T(8,128)(2,1)}, u32[]{:S(2)}, u32[]{:S(2)}) %collective-permute-start.49) | collective-permute-done | bytes 524320 | tf_op jit(solution)/shard_map/ppermute | solution.py:21
  357.1 6.3 %feed_grads.3 = (bf16[4,1024,256]{2,1,0:T(8,128)(2,1)}, f32[8,512]{1,0:T(8,128)S(1)}) custom-call(bf16[256,1024]{1,0:T(8,128)(2,1)S(1)} %copy-done.19, bf16[256,1024]{1,0:T(8,128)(2,1)S(1)} %copy-done.21, bf16[256,1024]{1,0:T(8,128)(2,1)} %collective-permute-done.24.refs_0_.refs_2_, bf16[256,1024]{1,0:T(8,128)(2,1)} %copy-done.87, ...), custom_call_target="tpu_custom_call" | custom-call | flops 6899999744 | tf_op jit(solution)/shard_map/feed_grads/pallas_call | solution.py:110
  363.4 6.5 %collective-permute-done.52.refs_2_ = bf16[256,1024]{1,0:T(8,128)(2,1)S(1)} collective-permute-done((bf16[256,1024]{1,0:T(8,128)(2,1)S(1)}, bf16[256,1024]{1,0:T(8,128)(2,1)S(1)}, u32[]{:S(2)}, u32[]{:S(2)}) %collective-permute-start.52) | collective-permute-done | bytes 524320 | tf_op jit(solution)/shard_map/ppermute | solution.py:21
  380.8 7.7 %collective-permute-done.54.refs_2_.refs_6_ = bf16[256,1024]{1,0:T(8,128)(2,1)} collective-permute-done((bf16[256,1024]{1,0:T(8,128)(2,1)S(1)}, bf16[256,1024]{1,0:T(8,128)(2,1)}, u32[]{:S(2)}, u32[]{:S(2)}) %collective-permute-start.54) | collective-permute-done | bytes 524320 | tf_op jit(solution)/shard_map/ppermute | solution.py:21
  395.3 22.8 %attend_back.3 = (bf16[1024,256]{1,0:T(8,128)(2,1)S(1)}, bf16[1024,256]{1,0:T(8,128)(2,1)}, bf16[1024,256]{1,0:T(8,128)(2,1)}, bf16[256,1024]{1,0:T(8,128)(2,1)}, bf16[256,1024]{1,0:T(8,128)(2,1)}) custom-call(bf16[256,1024]{1,0:T(8,128)(2,1)} %copy-done.23, bf16[256,1024]{1,0:T(8,128)(2,1)} %collective-permute-done.53.refs_1_.refs_5_, ...), custom_call_target="tpu_custom_call" | custom-call | flops 25300000768 | tf_op jit(solution)/shard_map/attend_back/pallas_call | solution.py:110
  423.1 7.9 %attention_grads.3 = (bf16[256,1024]{1,0:T(8,128)(2,1)S(1)}, bf16[256,1024]{1,0:T(8,128)(2,1)S(1)}, bf16[4,1024,256]{2,1,0:T(8,128)(2,1)}, f32[3,8,256]{2,1,0:T(8,128)S(1)}) custom-call(bf16[256,1024]{1,0:T(8,128)(2,1)} %copy-done.4, bf16[256,1024]{1,0:T(8,128)(2,1)} %copy-done.5, bf16[256,1024]{1,0:T(8,128)(2,1)} %copy-done.16, ...), custom_call_target="tpu_custom_call" | custom-call | flops 9200000000 | tf_op jit(solution)/shard_map/attention_grads/pallas_call | solution.py:110
  471.3 11.0 %collective-permute-done.60 = bf16[256,1024]{1,0:T(8,128)(2,1)} collective-permute-done((bf16[256,1024]{1,0:T(8,128)(2,1)}, bf16[256,1024]{1,0:T(8,128)(2,1)}, u32[]{:S(2)}, u32[]{:S(2)}) %collective-permute-start.60) | collective-permute-done | bytes 524320 | tf_op jit(solution)/shard_map/ppermute | solution.py:21
  493.1 7.5 %collective-permute-done.61 = bf16[1024,256]{1,0:T(8,128)(2,1)S(1)} collective-permute-done((bf16[1024,256]{1,0:T(8,128)(2,1)}, bf16[1024,256]{1,0:T(8,128)(2,1)S(1)}, u32[]{:S(2)}, u32[]{:S(2)}) %collective-permute-start.61) | collective-permute-done | bytes 524320 | tf_op jit(solution)/shard_map/ppermute | solution.py:1129
  (516 shorter events, 259.9 us)
Async XLA Ops:
  7.3 88.5 %all-gather.7.cloned.1.call-start = ((), (), s32[]{:S(2)}) async-start(), calls=%async_computation.8 | async-start | bytes 4718592 | tf_op jit(solution)/shard_map/all_gather | solution.py:687
  15.7 126.3 %all-gather.9.cloned.1.call-start = ((), (), s32[]{:S(2)}) async-start(), calls=%async_computation.9 | async-start | bytes 2621440 | tf_op jit(solution)/shard_map/all_gather | solution.py:86
  17.8 30.6 %collective-permute-start = (bf16[256,1024]{1,0:T(8,128)(2,1)}, bf16[256,1024]{1,0:T(8,128)(2,1)}, u32[]{:S(2)}, u32[]{:S(2)}) collective-permute-start(bf16[256,1024]{1,0:T(8,128)(2,1)} %select_bitcast_fusion.2), channel_id=1, source_target_pairs={{0,16},{16,0},{1,17},{17,1},{2,18},{18,2},{3,19},{19,3},{4,20},{20... | collective-permute-start | bytes 1572872 | tf_op jit(solution)/shard_map/ppermute | solution.py:21
  43.0 30.1 %collective-permute-start.17 = (bf16[256,512]{1,0:T(8,128)(2,1)S(1)}, bf16[256,512]{1,0:T(8,128)(2,1)S(1)}, u32[]{:S(2)}, u32[]{:S(2)}) collective-permute-start(bf16[256,512]{1,0:T(8,128)(2,1)S(1)} %bitcast.232), channel_id=1, source_target_pairs={{0,16},{16,0},{1,17},{17,1},{2,18},{18,2},{3,19},{19,3},{4,20},{20... | collective-permute-start | bytes 786440 | tf_op jit(solution)/shard_map/ppermute | solution.py:21
  46.1 27.0 %collective-permute-start.18 = (bf16[512,256]{1,0:T(8,128)(2,1)S(1)}, bf16[512,256]{1,0:T(8,128)(2,1)S(1)}, u32[]{:S(2)}, u32[]{:S(2)}) collective-permute-start(bf16[512,256]{1,0:T(8,128)(2,1)S(1)} %bitcast.233), channel_id=1, source_target_pairs={{0,16},{16,0},{1,17},{17,1},{2,18},{18,2},{3,19},{19,3},{4,20},{20... | collective-permute-start | bytes 786440 | tf_op jit(solution)/shard_map/ppermute | solution.py:21
  74.3 157.3 %all-gather.11.cloned.1.call-start = ((), (), s32[]{:S(2)}) async-start(), calls=%async_computation.10 | async-start | bytes 5242880 | tf_op jit(solution)/shard_map/all_gather | solution.py:86
  79.7 29.2 %collective-permute-start.35 = (bf16[1024,256]{1,0:T(8,128)(2,1)}, bf16[1024,256]{1,0:T(8,128)(2,1)}, u32[]{:S(2)}, u32[]{:S(2)}) collective-permute-start(bf16[1024,256]{1,0:T(8,128)(2,1)} %pad_maximum_fusion.3), channel_id=1, source_target_pairs={{0,8},{4,12},{8,0},{12,4},{1,9},{5,13},{9,1},{13,5},{2,10},{6,14},... | collective-permute-start | bytes 1572872 | tf_op jit(solution)/shard_map/ppermute | solution.py:21
  111.1 267.8 %reduce-scatter.5.cloned.1.call-start = ((), (), s32[]{:S(2)}) async-start(), calls=%async_computation.4 | async-start | bytes 5242880 | tf_op jit(solution)/shard_map/reduce_scatter | solution.py:1004
  112.4 14.4 %collective-permute-start.21 = (bf16[256,1024]{1,0:T(8,128)(2,1)}, bf16[256,1024]{1,0:T(8,128)(2,1)S(1)}, u32[]{:S(2)}, u32[]{:S(2)}) collective-permute-start(bf16[256,1024]{1,0:T(8,128)(2,1)} %add_convert_fusion.5), channel_id=1, source_target_pairs={{0,8},{4,12},{8,0},{12,4},{1,9},{5,13},{9,1},{13,5},{2,10},{6,14},... | collective-permute-start | bytes 1572872 | tf_op jit(solution)/shard_map/ppermute | solution.py:21
  130.6 18.1 %collective-permute-start.24 = (bf16[256,1024]{1,0:T(8,128)(2,1)S(1)}, bf16[256,1024]{1,0:T(8,128)(2,1)}, u32[]{:S(2)}, u32[]{:S(2)}) collective-permute-start(bf16[256,1024]{1,0:T(8,128)(2,1)S(1)} %get-tuple-element.170.refs_0_), channel_id=1, source_target_pairs={{0,8},{4,12},{8,0},{12,4},{1,9},{5,13},{9,1},{13,5},{2,10},{6,14},... | collective-permute-start | bytes 1572872 | tf_op jit(solution)/shard_map/ppermute | solution.py:21
  178.5 14.5 %collective-permute-start.28 = (bf16[256,1024]{1,0:T(8,128)(2,1)}, bf16[256,1024]{1,0:T(8,128)(2,1)S(1)}, u32[]{:S(2)}, u32[]{:S(2)}) collective-permute-start(bf16[256,1024]{1,0:T(8,128)(2,1)} %get-tuple-element.181.refs_0_), channel_id=1, source_target_pairs={{0,8},{4,12},{8,0},{12,4},{1,9},{5,13},{9,1},{13,5},{2,10},{6,14},... | collective-permute-start | bytes 1572872 | tf_op jit(solution)/shard_map/ppermute | solution.py:21
  261.6 175.0 %reduce-scatter.7.cloned.1.call-start = ((), (), s32[]{:S(2)}) async-start(), calls=%async_computation.5 | async-start | bytes 2621440 | tf_op jit(solution)/shard_map/reduce_scatter | solution.py:1071
  332.3 14.4 %collective-permute-start.49 = (bf16[256,1024]{1,0:T(8,128)(2,1)S(1)}, bf16[256,1024]{1,0:T(8,128)(2,1)}, u32[]{:S(2)}, u32[]{:S(2)}) collective-permute-start(bf16[256,1024]{1,0:T(8,128)(2,1)S(1)} %get-tuple-element.229.refs_0_.refs_4_), channel_id=1, source_target_pairs={{0,8},{4,12},{8,0},{12,4},{1,9},{5,13},{9,1},{13,5},{2,10},{6,14},... | collective-permute-start | bytes 1572872 | tf_op jit(solution)/shard_map/ppermute | solution.py:21
  333.4 103.1 %reduce-scatter.9.cloned.1.call-start = ((), (), s32[]{:S(2)}) async-start(), calls=%async_computation.6 | async-start | bytes 2621440 | tf_op jit(solution)/shard_map/reduce_scatter | solution.py:1004
  354.3 15.7 %collective-permute-start.48 = (bf16[256,1024]{1,0:T(8,128)(2,1)S(1)}, bf16[256,1024]{1,0:T(8,128)(2,1)S(1)}, u32[]{:S(2)}, u32[]{:S(2)}) collective-permute-start(bf16[256,1024]{1,0:T(8,128)(2,1)S(1)} %copy-done.27), channel_id=1, source_target_pairs={{0,4},{4,0},{8,12},{12,8},{1,5},{5,1},{9,13},{13,9},{2,6},{6,2},{1... | collective-permute-start | bytes 1572872 | tf_op jit(solution)/shard_map/ppermute | solution.py:21
  378.8 16.5 %collective-permute-start.53 = (bf16[256,1024]{1,0:T(8,128)(2,1)S(1)}, bf16[256,1024]{1,0:T(8,128)(2,1)}, u32[]{:S(2)}, u32[]{:S(2)}) collective-permute-start(bf16[256,1024]{1,0:T(8,128)(2,1)S(1)} %get-tuple-element.246.refs_0_.refs_4_), channel_id=1, source_target_pairs={{0,4},{4,0},{8,12},{12,8},{1,5},{5,1},{9,13},{13,9},{2,6},{6,2},{1... | collective-permute-start | bytes 1572872 | tf_op jit(solution)/shard_map/ppermute | solution.py:21
  394.1 91.5 %reduce-scatter.11.cloned.1.call-start = ((), (), s32[]{:S(2)}) async-start(), calls=%async_computation.7 | async-start | bytes 2621440 | tf_op jit(solution)/shard_map/reduce_scatter | solution.py:1071
  394.3 23.9 %collective-permute-start.56 = (bf16[1024,256]{1,0:T(8,128)(2,1)}, bf16[1024,256]{1,0:T(8,128)(2,1)S(1)}, u32[]{:S(2)}, u32[]{:S(2)}) collective-permute-start(bf16[1024,256]{1,0:T(8,128)(2,1)} %slice_bitcast_fusion.2), channel_id=1, source_target_pairs={{0,8},{4,12},{8,0},{12,4},{1,9},{5,13},{9,1},{13,5},{2,10},{6,14},... | collective-permute-start | bytes 1572872 | tf_op jit(solution)/shard_map/ppermute | solution.py:21
  422.3 14.3 %collective-permute-start.59 = (bf16[256,1024]{1,0:T(8,128)(2,1)}, bf16[256,1024]{1,0:T(8,128)(2,1)}, u32[]{:S(2)}, u32[]{:S(2)}) collective-permute-start(bf16[256,1024]{1,0:T(8,128)(2,1)} %add_convert_fusion), channel_id=1, source_target_pairs={{0,8},{4,12},{8,0},{12,4},{1,9},{5,13},{9,1},{13,5},{2,10},{6,14},... | collective-permute-start | bytes 1572872 | tf_op jit(solution)/shard_map/ppermute | solution.py:21
  447.9 20.9 %collective-permute-start.77 = (bf16[1024,256]{1,0:T(8,128)(2,1)S(1)}, bf16[1024,256]{1,0:T(8,128)(2,1)}, u32[]{:S(2)}, u32[]{:S(2)}) collective-permute-start(bf16[1024,256]{1,0:T(8,128)(2,1)S(1)} %broadcast_select_fusion), channel_id=1, source_target_pairs={{0,16},{16,0},{1,17},{17,1},{2,18},{18,2},{3,19},{19,3},{4,20},{20... | collective-permute-start | bytes 1572872 | tf_op jit(solution)/shard_map/ppermute | solution.py:21
  448.7 44.4 %collective-permute-start.62 = (bf16[1024,256]{1,0:T(8,128)(2,1)}, bf16[1024,256]{1,0:T(8,128)(2,1)}, u32[]{:S(2)}, u32[]{:S(2)}) collective-permute-start(bf16[1024,256]{1,0:T(8,128)(2,1)} %bitcast.58), channel_id=1, source_target_pairs={{0,16},{1,17},{2,18},{3,19},{4,20},{5,21},{6,22},{7,23},{8,24},{9,... | collective-permute-start | bytes 1572872 | tf_op jit(solution)/shard_map/ppermute | solution.py:1128
  460.3 22.1 %collective-permute-start.60 = (bf16[256,1024]{1,0:T(8,128)(2,1)}, bf16[256,1024]{1,0:T(8,128)(2,1)}, u32[]{:S(2)}, u32[]{:S(2)}) collective-permute-start(bf16[256,1024]{1,0:T(8,128)(2,1)} %get-tuple-element.298), channel_id=1, source_target_pairs={{0,16},{16,0},{1,17},{17,1},{2,18},{18,2},{3,19},{19,3},{4,20},{20... | collective-permute-start | bytes 1572872 | tf_op jit(solution)/shard_map/ppermute | solution.py:21
  468.7 16.8 %collective-permute-start.75 = (bf16[64,1536]{1,0:T(8,128)(2,1)S(1)}, bf16[64,1536]{1,0:T(8,128)(2,1)S(1)}, u32[]{:S(2)}, u32[]{:S(2)}) collective-permute-start(bf16[64,1536]{1,0:T(8,128)(2,1)S(1)} %collective-permute-done.74.refs_2_), channel_id=1, source_target_pairs={{0,4},{4,0},{8,12},{12,8},{1,5},{5,1},{9,13},{13,9},{2,6},{6,2},{1... | collective-permute-start | bytes 589832 | tf_op jit(solution)/shard_map/ppermute | solution.py:21
  485.6 15.1 %collective-permute-start.61 = (bf16[1024,256]{1,0:T(8,128)(2,1)}, bf16[1024,256]{1,0:T(8,128)(2,1)S(1)}, u32[]{:S(2)}, u32[]{:S(2)}) collective-permute-start(bf16[1024,256]{1,0:T(8,128)(2,1)} %bitcast.230), channel_id=1, source_target_pairs={{16,0},{17,1},{18,2},{19,3},{20,4},{21,5},{22,6},{23,7},{24,8},{25... | collective-permute-start | bytes 1572872 | tf_op jit(solution)/shard_map/ppermute | solution.py:1129
  (159 other events, 1123.9 us)
Sparse Core Ops, SparseCore 0:
  15.8 79.8 all-gather.6
  97.3 44.6 all-gather.8
  144.2 79.4 all-gather.10
  261.7 75.4 reduce-scatter.4
  339.5 44.3 reduce-scatter.6
  394.2 41.5 reduce-scatter.8
  438.8 46.2 reduce-scatter.10

commit v5 on v4

--- a/solution.py
+++ b/solution.py
@@ -14,7 +14,7 @@
 big_negative = -1e30
 f32 = jnp.float32
 bf16 = jnp.bfloat16
-vmem_limit = 52 * 1024 * 1024
+vmem_limit = 32 * 1024 * 1024
 
 
 def swap(block, axis, bit):

time: 515 us -> 506 us (0.983)
  Pallas kernels: 178 us -> 119 us
  local copies, waits for them, and re-layouts: 39.8 us -> 94.5 us
  waiting for transfers between devices: 181 us -> 167 us
    pallas_call x27, Pallas kernels: 173 us -> 114 us  [call(): pl.pallas_call(body, in_specs=[spec_of(arg) for arg in args], out_specs=(...]
    unnamed x201 -> x401, local copies, waits for them, and re-layouts: 30.1 us -> 74.6 us
    all_gather x1, waiting for transfers between devices: 15.3 us -> 4.69 us  [per_device(): lax.all_gather(pack, ('section', 'dp'), axis=0, tiled=False)]
    all_gather x2, waiting for transfers between devices: 9.74 us -> 2.2 us  [gather_groups(): return lax.all_gather(block, 'dp', axis=0, tiled=False)]
    reshape x6, local copies, waits for them, and re-layouts: 0.49 us -> 7.94 us  [biases(): pieces.append(full[:, start:start + size].reshape(1, groups * size))]
  transfers between devices with their start and end apart: 85 -> 85, of which waited for: 45 -> 45; matrix products, arithmetic and copies ran while one was open for 7% -> 11% of each run, Pallas kernels for 31% -> 21%
where the time goes in v5:
time: 506 us; the launch traced here: 498 us
  waiting for transfers between devices  167 us (33%)
  Pallas kernels  119 us (24%)
  local copies, waits for them, and re-layouts  94.5 us (19%)
  starting transfers between devices  64.3 us (13%)
  other arithmetic  36.8 us (7%)
  between operations  16.6 us (3%)
    ppermute x69, waiting for transfers between devices, swap(): lax.ppermute(block, axis, [(i, i ^ bit) for i in range(lax.axis_size(axis...  145 us
    pallas_call x27, Pallas kernels, call(): pl.pallas_call(body, in_specs=[spec_of(arg) for arg in args], out_specs=(...  114 us
    unnamed x401, local copies, waits for them, and re-layouts  74.6 us
    ppermute x69, starting transfers between devices, swap(): lax.ppermute(block, axis, [(i, i ^ bit) for i in range(lax.axis_size(axis...  46.6 us
    ppermute x7, starting transfers between devices, per_device(): lax.ppermute(term, ('section', 'dp'), route)  10.6 us
  transfers between devices with their start and end apart: 85, of which 45 were waited for; matrix products, arithmetic and copies ran while one was open for 11% of the time, Pallas kernels for 21%

profile of v5, /device:TPU:0, one launch (start us, length us, event | category | flops | bytes accessed | tf_op | source)
XLA Modules:
  0.0 498.4 jit_solution(17147986283682726011)
XLA Ops:
  33.9 6.4 %collective-permute-done.13 = f32[8,1536]{1,0:T(8,128)S(1)} collective-permute-done((f32[8,1536]{1,0:T(8,128)S(1)}, f32[8,1536]{1,0:T(8,128)S(1)}, u32[]{:S(2)}, u32[]{:S(2)}) %collective-permute-start.13) | collective-permute-done | bytes 49184 | tf_op jit(solution)/shard_map/ppermute | solution.py:729
  51.1 13.3 %collective-permute-done.2.refs_2_ = bf16[256,1024]{1,0:T(8,128)(2,1)S(1)} collective-permute-done((bf16[256,1024]{1,0:T(8,128)(2,1)S(1)}, bf16[256,1024]{1,0:T(8,128)(2,1)S(1)}, u32[]{:S(2)}, u32[]{:S(2)}) %collective-permute-start.2) | collective-permute-done | bytes 524320 | tf_op jit(solution)/shard_map/ppermute | solution.py:21
  91.0 4.7 all-gather.7.cloned.1.call-done
  101.4 5.3 %attend_far.2 = (bf16[512,256]{1,0:T(8,128)(2,1)S(1)}, bf16[1024,256]{1,0:T(8,128)(2,1)S(1)}, bf16[1024,256]{1,0:T(8,128)(2,1)S(1)}, bf16[512,256]{1,0:T(8,128)(...) custom-call(bf16[256,1024]{1,0:T(8,128)(2,1)S(1)} %copy-done.64, ...), custom_call_target="tpu_custom_call" | custom-call | tf_op jit(solution)/shard_map/attend_far/pallas_call | solution.py:110
  120.7 4.4 attend_near.2
  163.4 12.5 %collective-permute-done.27.refs_2_ = bf16[256,1024]{1,0:T(8,128)(2,1)S(1)} collective-permute-done((bf16[256,1024]{1,0:T(8,128)(2,1)S(1)}, bf16[256,1024]{1,0:T(8,128)(2,1)S(1)}, u32[]{:S(2)}, u32[]{:S(2)}) %collective-permute-start.27) | collective-permute-done | bytes 524320 | tf_op jit(solution)/shard_map/ppermute | solution.py:21
  180.4 11.3 %collective-permute-done.28.refs_0_.refs_2_ = bf16[256,1024]{1,0:T(8,128)(2,1)S(1)} collective-permute-done((bf16[256,1024]{1,0:T(8,128)(2,1)S(1)}, bf16[256,1024]{1,0:T(8,128)(2,1)S(1)}, u32[]{:S(2)}, u32[]{:S(2)}) %collective-permute-start.28) | collective-permute-done | bytes 524320 | tf_op jit(solution)/shard_map/ppermute | solution.py:21
  193.6 5.8 %attend_far.3 = (bf16[512,256]{1,0:T(8,128)(2,1)S(1)}, bf16[1024,256]{1,0:T(8,128)(2,1)S(1)}, bf16[1024,256]{1,0:T(8,128)(2,1)S(1)}, bf16[512,256]{1,0:T(8,128)(...) custom-call(bf16[256,1024]{1,0:T(8,128)(2,1)S(1)} %collective-permute-done.28.refs_0_, ...), custom_call_target="tpu_custom_call" | custom-call | tf_op jit(solution)/shard_map/attend_far/pallas_call | solution.py:110
  203.8 4.6 attend_near.3
  208.8 7.6 %collective-permute-done.33.refs_2_ = bf16[256,1024]{1,0:T(8,128)(2,1)S(1)} collective-permute-done((bf16[256,1024]{1,0:T(8,128)(2,1)S(1)}, bf16[256,1024]{1,0:T(8,128)(2,1)S(1)}, u32[]{:S(2)}, u32[]{:S(2)}) %collective-permute-start.33) | collective-permute-done | bytes 524320 | tf_op jit(solution)/shard_map/ppermute | solution.py:21
  227.9 4.6 feed.5
  260.4 12.5 %collective-permute-done.42.refs_2_.refs_6_ = bf16[256,1024]{1,0:T(8,128)(2,1)S(1)} collective-permute-done((bf16[256,1024]{1,0:T(8,128)(2,1)S(1)}, bf16[256,1024]{1,0:T(8,128)(2,1)S(1)}, u32[]{:S(2)}, u32[]{:S(2)}) %collective-permute-start.42) | collective-permute-done | bytes 524320 | tf_op jit(solution)/shard_map/ppermute | solution.py:21
  274.9 18.5 %attend_back.2 = (bf16[1024,256]{1,0:T(8,128)(2,1)S(1)}, bf16[1024,256]{1,0:T(8,128)(2,1)S(1)}, bf16[1024,256]{1,0:T(8,128)(2,1)S(1)}, bf16[256,1024]{1,0:T(8,128)(2,1)S(1)}, bf16[256,1024]{1,0:T(8,128)(2,1)S(1)}) custom-call(bf16[256,1024]{1,0:T(8,128)(2,1)S(1)} %get-tuple-element.211.refs_0_.refs_4_, ...), custom_call_target="tpu_custom_call" | custom-call | flops 25300000768 | tf_op jit(solution)/shard_map/attend_back/pallas_call | solution.py:110
  302.0 7.7 %collective-permute-done.46.refs_2_ = bf16[256,1024]{1,0:T(8,128)(2,1)S(1)} collective-permute-done((bf16[256,1024]{1,0:T(8,128)(2,1)S(1)}, bf16[256,1024]{1,0:T(8,128)(2,1)S(1)}, u32[]{:S(2)}, u32[]{:S(2)}) %collective-permute-start.46) | collective-permute-done | bytes 524320 | tf_op jit(solution)/shard_map/ppermute | solution.py:21
  343.0 4.2 feed_grads.3
  348.6 6.9 %collective-permute-done.52.refs_2_ = bf16[256,1024]{1,0:T(8,128)(2,1)S(1)} collective-permute-done((bf16[256,1024]{1,0:T(8,128)(2,1)S(1)}, bf16[256,1024]{1,0:T(8,128)(2,1)S(1)}, u32[]{:S(2)}, u32[]{:S(2)}) %collective-permute-start.52) | collective-permute-done | bytes 524320 | tf_op jit(solution)/shard_map/ppermute | solution.py:21
  364.3 7.1 %collective-permute-done.54.refs_2_.refs_6_ = bf16[256,1024]{1,0:T(8,128)(2,1)} collective-permute-done((bf16[256,1024]{1,0:T(8,128)(2,1)}, bf16[256,1024]{1,0:T(8,128)(2,1)}, u32[]{:S(2)}, u32[]{:S(2)}) %collective-permute-start.54) | collective-permute-done | bytes 524320 | tf_op jit(solution)/shard_map/ppermute | solution.py:21
  385.5 19.8 %attend_back.3 = (bf16[1024,256]{1,0:T(8,128)(2,1)S(1)}, bf16[1024,256]{1,0:T(8,128)(2,1)S(1)}, bf16[1024,256]{1,0:T(8,128)(2,1)S(1)}, bf16[256,1024]{1,0:T(8,128)(2,1)S(1)}, bf16[256,1024]{1,0:T(8,128)(2,1)S(1)}) custom-call(bf16[256,1024]{1,0:T(8,128)(2,1)} %get-tuple-element.246.refs_0_.refs_4_, ...), custom_call_target="tpu_custom_call" | custom-call | flops 25300000768 | tf_op jit(solution)/shard_map/attend_back/pallas_call | solution.py:110
  409.5 4.9 attention_grads.3
  415.9 6.6 %collective-permute-done.59.refs_2_ = bf16[256,1024]{1,0:T(8,128)(2,1)S(1)} collective-permute-done((bf16[256,1024]{1,0:T(8,128)(2,1)}, bf16[256,1024]{1,0:T(8,128)(2,1)S(1)}, u32[]{:S(2)}, u32[]{:S(2)}) %collective-permute-start.59) | collective-permute-done | bytes 524320 | tf_op jit(solution)/shard_map/ppermute | solution.py:21
  455.0 4.4 collective-permute-done.74.refs_2_
  462.1 9.5 %collective-permute-done.60 = bf16[256,1024]{1,0:T(8,128)(2,1)} collective-permute-done((bf16[256,1024]{1,0:T(8,128)(2,1)}, bf16[256,1024]{1,0:T(8,128)(2,1)}, u32[]{:S(2)}, u32[]{:S(2)}) %collective-permute-start.60) | collective-permute-done | bytes 524320 | tf_op jit(solution)/shard_map/ppermute | solution.py:21
  477.0 4.2 mod_grads.1
  482.4 7.0 %collective-permute-done.61 = bf16[1024,256]{1,0:T(8,128)(2,1)S(1)} collective-permute-done((bf16[1024,256]{1,0:T(8,128)(2,1)}, bf16[1024,256]{1,0:T(8,128)(2,1)S(1)}, u32[]{:S(2)}, u32[]{:S(2)}) %collective-permute-start.61) | collective-permute-done | bytes 524320 | tf_op jit(solution)/shard_map/ppermute | solution.py:1129
  (716 shorter events, 287.9 us)
Async XLA Ops:
  7.3 88.5 %all-gather.7.cloned.1.call-start = ((), (), s32[]{:S(2)}) async-start(), calls=%async_computation.8 | async-start | bytes 4718592 | tf_op jit(solution)/shard_map/all_gather | solution.py:687
  15.7 126.3 %all-gather.9.cloned.1.call-start = ((), (), s32[]{:S(2)}) async-start(), calls=%async_computation.9 | async-start | bytes 2621440 | tf_op jit(solution)/shard_map/all_gather | solution.py:86
  17.8 30.7 %collective-permute-start = (bf16[256,1024]{1,0:T(8,128)(2,1)}, bf16[256,1024]{1,0:T(8,128)(2,1)}, u32[]{:S(2)}, u32[]{:S(2)}) collective-permute-start(bf16[256,1024]{1,0:T(8,128)(2,1)} %select_bitcast_fusion.2), channel_id=1, source_target_pairs={{0,16},{16,0},{1,17},{17,1},{2,18},{18,2},{3,19},{19,3},{4,20},{20... | collective-permute-start | bytes 1572872 | tf_op jit(solution)/shard_map/ppermute | solution.py:21
  26.6 14.3 %collective-permute-start.10 = (f32[8,1536]{1,0:T(8,128)S(1)}, f32[8,1536]{1,0:T(8,128)S(1)}, u32[]{:S(2)}, u32[]{:S(2)}) collective-permute-start(f32[8,1536]{1,0:T(8,128)S(1)} %get-tuple-element.317), channel_id=1, source_target_pairs={{0,16},{1,17},{2,18},{3,19},{16,0},{17,1},{18,2},{19,3},{4,20},{5,... | collective-permute-start | bytes 147464 | tf_op jit(solution)/shard_map/ppermute | solution.py:729
  43.0 26.8 %collective-permute-start.17 = (bf16[256,512]{1,0:T(8,128)(2,1)}, bf16[256,512]{1,0:T(8,128)(2,1)S(1)}, u32[]{:S(2)}, u32[]{:S(2)}) collective-permute-start(bf16[256,512]{1,0:T(8,128)(2,1)} %bitcast.43), channel_id=1, source_target_pairs={{0,16},{16,0},{1,17},{17,1},{2,18},{18,2},{3,19},{19,3},{4,20},{20... | collective-permute-start | bytes 786440 | tf_op jit(solution)/shard_map/ppermute | solution.py:21
  46.2 23.7 %collective-permute-start.18 = (bf16[512,256]{1,0:T(8,128)(2,1)}, bf16[512,256]{1,0:T(8,128)(2,1)S(1)}, u32[]{:S(2)}, u32[]{:S(2)}) collective-permute-start(bf16[512,256]{1,0:T(8,128)(2,1)} %bitcast.44), channel_id=1, source_target_pairs={{0,16},{16,0},{1,17},{17,1},{2,18},{18,2},{3,19},{19,3},{4,20},{20... | collective-permute-start | bytes 786440 | tf_op jit(solution)/shard_map/ppermute | solution.py:21
  73.1 150.7 %all-gather.11.cloned.1.call-start = ((), (), s32[]{:S(2)}) async-start(), calls=%async_computation.10 | async-start | bytes 5242880 | tf_op jit(solution)/shard_map/all_gather | solution.py:86
  89.6 21.7 %collective-permute-start.35 = (bf16[1024,256]{1,0:T(8,128)(2,1)}, bf16[1024,256]{1,0:T(8,128)(2,1)}, u32[]{:S(2)}, u32[]{:S(2)}) collective-permute-start(bf16[1024,256]{1,0:T(8,128)(2,1)} %pad_maximum_fusion.3), channel_id=1, source_target_pairs={{0,8},{4,12},{8,0},{12,4},{1,9},{5,13},{9,1},{13,5},{2,10},{6,14},... | collective-permute-start | bytes 1572872 | tf_op jit(solution)/shard_map/ppermute | solution.py:21
  113.5 248.9 %reduce-scatter.5.cloned.1.call-start = ((), (), s32[]{:S(2)}) async-start(), calls=%async_computation.4 | async-start | bytes 5242880 | tf_op jit(solution)/shard_map/reduce_scatter | solution.py:1004
  115.9 14.6 %collective-permute-start.21 = (bf16[256,1024]{1,0:T(8,128)(2,1)}, bf16[256,1024]{1,0:T(8,128)(2,1)}, u32[]{:S(2)}, u32[]{:S(2)}) collective-permute-start(bf16[256,1024]{1,0:T(8,128)(2,1)} %add_convert_fusion.5), channel_id=1, source_target_pairs={{0,8},{4,12},{8,0},{12,4},{1,9},{5,13},{9,1},{13,5},{2,10},{6,14},... | collective-permute-start | bytes 1572872 | tf_op jit(solution)/shard_map/ppermute | solution.py:21
  138.2 14.7 %collective-permute-start.24 = (bf16[256,1024]{1,0:T(8,128)(2,1)}, bf16[256,1024]{1,0:T(8,128)(2,1)}, u32[]{:S(2)}, u32[]{:S(2)}) collective-permute-start(bf16[256,1024]{1,0:T(8,128)(2,1)} %get-tuple-element.170.refs_0_), channel_id=1, source_target_pairs={{0,8},{4,12},{8,0},{12,4},{1,9},{5,13},{9,1},{13,5},{2,10},{6,14},... | collective-permute-start | bytes 1572872 | tf_op jit(solution)/shard_map/ppermute | solution.py:21
  177.3 14.3 %collective-permute-start.28 = (bf16[256,1024]{1,0:T(8,128)(2,1)S(1)}, bf16[256,1024]{1,0:T(8,128)(2,1)S(1)}, u32[]{:S(2)}, u32[]{:S(2)}) collective-permute-start(bf16[256,1024]{1,0:T(8,128)(2,1)S(1)} %get-tuple-element.181.refs_0_), channel_id=1, source_target_pairs={{0,8},{4,12},{8,0},{12,4},{1,9},{5,13},{9,1},{13,5},{2,10},{6,14},... | collective-permute-start | bytes 1572872 | tf_op jit(solution)/shard_map/ppermute | solution.py:21
  250.8 172.5 %reduce-scatter.7.cloned.1.call-start = ((), (), s32[]{:S(2)}) async-start(), calls=%async_computation.5 | async-start | bytes 2621440 | tf_op jit(solution)/shard_map/reduce_scatter | solution.py:1071
  314.7 14.7 %collective-permute-start.49 = (bf16[256,1024]{1,0:T(8,128)(2,1)}, bf16[256,1024]{1,0:T(8,128)(2,1)}, u32[]{:S(2)}, u32[]{:S(2)}) collective-permute-start(bf16[256,1024]{1,0:T(8,128)(2,1)} %get-tuple-element.229.refs_0_.refs_4_), channel_id=1, source_target_pairs={{0,8},{4,12},{8,0},{12,4},{1,9},{5,13},{9,1},{13,5},{2,10},{6,14},... | collective-permute-start | bytes 1572872 | tf_op jit(solution)/shard_map/ppermute | solution.py:21
  316.2 107.2 %reduce-scatter.9.cloned.1.call-start = ((), (), s32[]{:S(2)}) async-start(), calls=%async_computation.6 | async-start | bytes 2621440 | tf_op jit(solution)/shard_map/reduce_scatter | solution.py:1004
  340.4 15.1 %collective-permute-start.48 = (bf16[256,1024]{1,0:T(8,128)(2,1)S(1)}, bf16[256,1024]{1,0:T(8,128)(2,1)S(1)}, u32[]{:S(2)}, u32[]{:S(2)}) collective-permute-start(bf16[256,1024]{1,0:T(8,128)(2,1)S(1)} %copy-done.105), channel_id=1, source_target_pairs={{0,4},{4,0},{8,12},{12,8},{1,5},{5,1},{9,13},{13,9},{2,6},{6,2},{1... | collective-permute-start | bytes 1572872 | tf_op jit(solution)/shard_map/ppermute | solution.py:21
  362.4 16.8 %collective-permute-start.53 = (bf16[256,1024]{1,0:T(8,128)(2,1)}, bf16[256,1024]{1,0:T(8,128)(2,1)}, u32[]{:S(2)}, u32[]{:S(2)}) collective-permute-start(bf16[256,1024]{1,0:T(8,128)(2,1)} %get-tuple-element.246.refs_0_.refs_4_), channel_id=1, source_target_pairs={{0,4},{4,0},{8,12},{12,8},{1,5},{5,1},{9,13},{13,9},{2,6},{6,2},{1... | collective-permute-start | bytes 1572872 | tf_op jit(solution)/shard_map/ppermute | solution.py:21
  377.9 97.0 %reduce-scatter.11.cloned.1.call-start = ((), (), s32[]{:S(2)}) async-start(), calls=%async_computation.7 | async-start | bytes 2621440 | tf_op jit(solution)/shard_map/reduce_scatter | solution.py:1071
  378.4 28.5 %collective-permute-start.56 = (bf16[1024,256]{1,0:T(8,128)(2,1)}, bf16[1024,256]{1,0:T(8,128)(2,1)S(1)}, u32[]{:S(2)}, u32[]{:S(2)}) collective-permute-start(bf16[1024,256]{1,0:T(8,128)(2,1)} %slice_bitcast_fusion.2), channel_id=1, source_target_pairs={{0,8},{4,12},{8,0},{12,4},{1,9},{5,13},{9,1},{13,5},{2,10},{6,14},... | collective-permute-start | bytes 1572872 | tf_op jit(solution)/shard_map/ppermute | solution.py:21
  437.4 22.1 %collective-permute-start.77 = (bf16[1024,256]{1,0:T(8,128)(2,1)}, bf16[1024,256]{1,0:T(8,128)(2,1)}, u32[]{:S(2)}, u32[]{:S(2)}) collective-permute-start(bf16[1024,256]{1,0:T(8,128)(2,1)} %broadcast_select_fusion), channel_id=1, source_target_pairs={{0,16},{16,0},{1,17},{17,1},{2,18},{18,2},{3,19},{19,3},{4,20},{20... | collective-permute-start | bytes 1572872 | tf_op jit(solution)/shard_map/ppermute | solution.py:21
  438.1 44.3 %collective-permute-start.62 = (bf16[1024,256]{1,0:T(8,128)(2,1)}, bf16[1024,256]{1,0:T(8,128)(2,1)}, u32[]{:S(2)}, u32[]{:S(2)}) collective-permute-start(bf16[1024,256]{1,0:T(8,128)(2,1)} %bitcast.58), channel_id=1, source_target_pairs={{0,16},{1,17},{2,18},{3,19},{4,20},{5,21},{6,22},{7,23},{8,24},{9,... | collective-permute-start | bytes 1572872 | tf_op jit(solution)/shard_map/ppermute | solution.py:1128
  449.8 21.9 %collective-permute-start.60 = (bf16[256,1024]{1,0:T(8,128)(2,1)}, bf16[256,1024]{1,0:T(8,128)(2,1)}, u32[]{:S(2)}, u32[]{:S(2)}) collective-permute-start(bf16[256,1024]{1,0:T(8,128)(2,1)} %get-tuple-element.298), channel_id=1, source_target_pairs={{0,16},{16,0},{1,17},{17,1},{2,18},{18,2},{3,19},{19,3},{4,20},{20... | collective-permute-start | bytes 1572872 | tf_op jit(solution)/shard_map/ppermute | solution.py:21
  459.3 15.5 %collective-permute-start.75 = (bf16[64,1536]{1,0:T(8,128)(2,1)S(1)}, bf16[64,1536]{1,0:T(8,128)(2,1)S(1)}, u32[]{:S(2)}, u32[]{:S(2)}) collective-permute-start(bf16[64,1536]{1,0:T(8,128)(2,1)S(1)} %collective-permute-done.74.refs_2_), channel_id=1, source_target_pairs={{0,4},{4,0},{8,12},{12,8},{1,5},{5,1},{9,13},{13,9},{2,6},{6,2},{1... | collective-permute-start | bytes 589832 | tf_op jit(solution)/shard_map/ppermute | solution.py:21
  474.9 14.5 %collective-permute-start.61 = (bf16[1024,256]{1,0:T(8,128)(2,1)}, bf16[1024,256]{1,0:T(8,128)(2,1)S(1)}, u32[]{:S(2)}, u32[]{:S(2)}) collective-permute-start(bf16[1024,256]{1,0:T(8,128)(2,1)} %bitcast.234), channel_id=1, source_target_pairs={{16,0},{17,1},{18,2},{19,3},{20,4},{21,5},{22,6},{23,7},{24,8},{25... | collective-permute-start | bytes 1572872 | tf_op jit(solution)/shard_map/ppermute | solution.py:1129
  (259 other events, 1891.3 us)
Sparse Core Ops, SparseCore 0:
  15.8 79.8 all-gather.6
  97.3 44.5 all-gather.8
  144.1 79.4 all-gather.10
  250.3 75.4 reduce-scatter.4
  328.1 44.3 reduce-scatter.6
  378.0 41.7 reduce-scatter.8
  422.8 46.2 reduce-scatter.10
